TPU v7x, 32 devices: a whole 2x2x4 slice. The times are simulated.
32 devices in a mesh: section: 2 (over x), dp: 16 (over z, y, core).
Axes of the slice: x: 2, y: 2, z: 4, core: 2. Of those that a mesh axis runs over, the one named last changes fastest.
Arguments:
- pixels: bfloat16 [64, 196, 768], P('dp')
- visible: int32 [64, 49], P('dp'), may hold values from 0 to 195, as said below
- restore: int32 [64, 196], P('dp'), may hold values from 0 to 195, as said below
- mat_master: float32 [2, 7667712], P('section', 'dp')
- mat_first: float32 [2, 7667712], P('section', 'dp')
- mat_second: float32 [2, 7667712], P('section', 'dp')
- vec_master: float32 [2, 162816], P('section', 'dp')
- vec_first: float32 [2, 162816], P('section', 'dp')
- vec_second: float32 [2, 162816], P('section', 'dp')
Outputs:
- loss_sum: float32 [], replicated
- grad_norm: float32 [], replicated
- mat_new: float32 [2, 7667712], P('section', 'dp')
- mat_first_new: float32 [2, 7667712], P('section', 'dp')
- mat_second_new: float32 [2, 7667712], P('section', 'dp')
- mat_copy: bfloat16 [2, 7667712], P('section', 'dp')
- vec_new: float32 [2, 162816], P('section', 'dp')
- vec_first_new: float32 [2, 162816], P('section', 'dp')
- vec_second_new: float32 [2, 162816], P('section', 'dp')
- vec_copy: bfloat16 [2, 162816], P('section', 'dp')
Inputs may be any that keep to these rules, and one draw needn't show every extreme that they name: restore[i] is the inverse of a permutation of the 196 patches whose first 49 entries are visible[i], in order. `visible`: each row holds 49 different patches.
All inputs are finite; a program needn't handle non-finite values.
Results may differ from a plain program's by a relative error of at most 0.011.
Values may be sent and summed in bfloat16 or wider, within the bound.
A program may use at most 576 MiB of HBM per device.

v0:
```python
import math

import jax
import jax.numpy as jnp
from jax import lax
from jax.sharding import PartitionSpec as P

PIX = 768
DE = 768
HE = 12
FE = 3072
DD = 512
HD = 16
FD = 2048
PATCHES = 196
VIS = 49
MICRO = 2
STEP = 10


def shifted(value, axis, steps):
    count = lax.axis_size(axis)
    initial, last = (max(0, -steps), min(count, count - steps))
    return lax.ppermute(value, axis, [(source, source + steps) for source in range(initial, last)])


def carve(flat, shapes):
    pieces = []
    offset = 0
    for shape in shapes:
        count = math.prod(shape)
        pieces.append(flat[offset : offset + count].reshape(shape))
        offset = offset + count
    return pieces


def encoder_shapes():
    mats = [(PIX, DE), (DE, 3 * DE), (DE, DE), (DE, FE), (FE, DE)]
    vecs = [
        (DE,),
        (PATCHES, DE),
        (DE,),
        (DE,),
        (2 * DE,),
        (DE,),
        (DE,),
        (DE,),
        (FE,),
        (DE,),
        (DE,),
        (DE,),
    ]
    return (mats, vecs)


def decoder_shapes():
    mats = [(DE, DD), (DD, 3 * DD), (DD, DD), (DD, FD), (FD, DD), (DD, PIX)]
    vecs = [
        (DD,),
        (DD,),
        (PATCHES, DD),
        (DD,),
        (DD,),
        (2 * DD,),
        (DD,),
        (DD,),
        (DD,),
        (FD,),
        (DD,),
        (DD,),
        (DD,),
        (PIX,),
    ]
    return (mats, vecs)


def layer_norm(values, gain, shift):
    centred = values - jnp.mean(values, -1, keepdims=True)
    spread = jnp.mean(centred * centred, -1, keepdims=True)
    return centred * lax.rsqrt(spread + 1e-06) * gain + shift


def adam_update(master, first, second, grad, rate, decay):
    first = 0.9 * first + 0.1 * grad
    second = 0.95 * second + 0.05 * grad * grad
    step_first = first / (1.0 - 0.9**STEP)
    step_second = second / (1.0 - 0.95**STEP)
    master = master - rate * (step_first / (jnp.sqrt(step_second) + 1e-08) + decay * master)
    return (master, first, second)


def make_model():

    def value_plain(value):
        return lax.optimization_barrier(value.astype(jnp.bfloat16)).astype(jnp.float32)

    round_value = jax.custom_vjp(value_plain)

    def value_keep(value):
        return (value_plain(value), None)

    def value_pass(kept, grad):
        return (grad,)

    round_value.defvjp(value_keep, value_pass)

    def grad_plain(value):
        return value

    round_grad = jax.custom_vjp(grad_plain)

    def grad_keep(value):
        return (value, None)

    def grad_pass(kept, grad):
        return (value_plain(grad),)

    round_grad.defvjp(grad_keep, grad_pass)

    def product_plain(left, right):
        return jnp.matmul(
            left.astype(jnp.bfloat16),
            right.astype(jnp.bfloat16),
            preferred_element_type=jnp.float32,
        )

    product = jax.custom_vjp(product_plain)

    def product_keep(left, right):
        return (product_plain(left, right), (left.astype(jnp.bfloat16), right.astype(jnp.bfloat16)))

    def product_back(kept, grad):
        left, right = kept
        grad = grad.astype(jnp.bfloat16)
        left_grad = jnp.matmul(
            grad, jnp.swapaxes(right, -1, -2), preferred_element_type=jnp.float32
        )
        right_grad = jnp.matmul(
            jnp.swapaxes(left, -1, -2), grad, preferred_element_type=jnp.float32
        )
        return (left_grad, right_grad)

    product.defvjp(product_keep, product_back)

    def linear(values, weight):
        shape = values.shape
        result = round_grad(product(values.reshape(-1, shape[-1]), weight))
        return result.reshape(shape[:-1] + (weight.shape[1],))

    def block(state, mats, vecs, heads):
        w_qkv, w_proj, w_up, w_down = mats
        gain_one, shift_one, qv_bias, proj_bias, gain_two, shift_two, up_bias, down_bias = vecs
        batch, count, width = state.shape
        size = width // heads
        normed = round_value(layer_norm(state, gain_one, shift_one))
        bias = jnp.concatenate(
            [qv_bias[:width], jnp.zeros((width,), qv_bias.dtype), qv_bias[width:]]
        )
        mixed = (
            (linear(normed, w_qkv) + bias)
            .reshape(batch, count, 3, heads, size)
            .transpose(2, 0, 3, 1, 4)
        )
        query = round_value(mixed[0] * size ** (-0.5))
        keys = round_value(mixed[1])
        values = round_value(mixed[2])
        scores = round_grad(product(query, jnp.swapaxes(keys, -1, -2)))
        weights = round_value(jax.nn.softmax(scores, axis=-1))
        attended = round_grad(product(weights, values))
        attended = round_value(attended.transpose(0, 2, 1, 3).reshape(batch, count, width))
        state = state + linear(attended, w_proj) + proj_bias
        normed = round_value(layer_norm(state, gain_two, shift_two))
        hidden = round_value(jax.nn.gelu(linear(normed, w_up) + up_bias))
        return state + linear(hidden, w_down) + down_bias

    def encoder(mats, vecs, pixels, visible):
        shapes_mat, shapes_vec = encoder_shapes()
        w_embed, w_qkv, w_proj, w_up, w_down = carve(mats, shapes_mat)
        pieces = carve(vecs, shapes_vec)
        chosen = jnp.take_along_axis(pixels, visible[:, :, None], axis=1)
        state = linear(chosen, w_embed) + pieces[0] + pieces[1][visible]
        state = block(state, (w_qkv, w_proj, w_up, w_down), pieces[2:10], HE)
        return round_value(layer_norm(state, pieces[10], pieces[11]))

    def decoder(mats, vecs, latent, pixels, restore):
        latent = round_grad(latent)
        shapes_mat, shapes_vec = decoder_shapes()
        w_embed, w_qkv, w_proj, w_up, w_down, w_head = carve(mats, shapes_mat)
        pieces = carve(vecs, shapes_vec)
        batch = latent.shape[0]
        embedded = linear(latent, w_embed) + pieces[0]
        filler = jnp.broadcast_to(pieces[1], (batch, PATCHES - VIS, DD))
        joined = jnp.concatenate([embedded, filler], 1)
        state = jnp.take_along_axis(joined, restore[:, :, None], axis=1) + pieces[2]
        state = block(state, (w_qkv, w_proj, w_up, w_down), pieces[3:11], HD)
        guess = linear(round_value(layer_norm(state, pieces[11], pieces[12])), w_head) + pieces[13]
        masked = (restore >= VIS).astype(guess.dtype)
        error = guess - pixels
        return jnp.sum(jnp.mean(error * error, -1) * masked)

    return (encoder, decoder)


def body(
    pixels, visible, restore, mat_master, mat_first, mat_second, vec_master, vec_first, vec_second
):
    encoder, decoder = make_model()
    whole_mats, whole_vecs = (
        lax.all_gather(mat_master.astype(jnp.bfloat16), "dp", axis=1, tiled=True),
        lax.all_gather(vec_master.astype(jnp.bfloat16), "dp", axis=1, tiled=True),
    )
    mats = whole_mats[0].astype(jnp.float32)
    vecs = whole_vecs[0].astype(jnp.float32)
    encoding = lax.axis_index("section") == 0
    masked_total = (PATCHES - VIS) * pixels.shape[0] * lax.axis_size("dp")
    share = pixels.shape[0] // MICRO
    grad_mats = jnp.zeros_like(mats)
    grad_vecs = jnp.zeros_like(vecs)
    loss_local = jnp.zeros((), jnp.float32)
    for micro in range(MICRO):
        images = pixels[micro * share : (micro + 1) * share].astype(jnp.float32)
        seen = visible[micro * share : (micro + 1) * share]
        places = restore[micro * share : (micro + 1) * share]

        def encode(mat_all, vec_all):
            return lax.cond(
                encoding,
                lambda m, v: encoder(m, v, images, seen),
                lambda m, v: jnp.zeros((share, VIS, DE), jnp.float32),
                mat_all,
                vec_all,
            )

        latent, pull_encoder = jax.vjp(encode, mats, vecs)
        arrived = shifted(latent.astype(jnp.bfloat16), "section", 1).astype(jnp.float32)

        def decode(mat_all, vec_all, incoming):
            return lax.cond(
                encoding,
                lambda m, v, l: jnp.zeros((), jnp.float32),
                lambda m, v, l: decoder(m, v, l, images, places),
                mat_all,
                vec_all,
                incoming,
            )

        value, pull_decoder = jax.vjp(decode, mats, vecs, arrived)
        dmat_dec, dvec_dec, returned = pull_decoder(jnp.ones((), jnp.float32) / masked_total)
        sent_back = shifted(returned.astype(jnp.bfloat16), "section", -1).astype(jnp.float32)
        dmat_enc, dvec_enc = pull_encoder(sent_back)
        loss_local = loss_local + value
        grad_mats = grad_mats + dmat_dec + dmat_enc
        grad_vecs = grad_vecs + dvec_dec + dvec_enc
    summed_mats, summed_vecs = (
        lax.psum_scatter(grad_mats[None], "dp", scatter_dimension=1, tiled=True),
        lax.psum_scatter(grad_vecs[None], "dp", scatter_dimension=1, tiled=True),
    )
    square = jnp.sum(summed_mats * summed_mats) + jnp.sum(summed_vecs * summed_vecs)
    square_all, loss_sum = lax.psum((square, loss_local), ("section", "dp"))
    grad_norm = jnp.sqrt(square_all)
    factor = jnp.minimum(1.0, 0.001 / (grad_norm + 1e-06))
    mat_new, mat_first_new, mat_second_new = adam_update(
        mat_master, mat_first, mat_second, factor * summed_mats, 0.05, 0.05
    )
    vec_new, vec_first_new, vec_second_new = adam_update(
        vec_master, vec_first, vec_second, factor * summed_vecs, 0.3, 0.0
    )
    return (
        loss_sum,
        grad_norm,
        mat_new,
        mat_first_new,
        mat_second_new,
        mat_new.astype(jnp.bfloat16),
        vec_new,
        vec_first_new,
        vec_second_new,
        vec_new.astype(jnp.bfloat16),
    )


def solution(mesh):
    return jax.shard_map(
        body,
        mesh=mesh,
        in_specs=(
            P("dp", None, None),
            P("dp", None),
            P("dp", None),
            P("section", "dp"),
            P("section", "dp"),
            P("section", "dp"),
            P("section", "dp"),
            P("section", "dp"),
            P("section", "dp"),
        ),
        out_specs=(
            P(),
            P(),
            P("section", "dp"),
            P("section", "dp"),
            P("section", "dp"),
            P("section", "dp"),
            P("section", "dp"),
            P("section", "dp"),
            P("section", "dp"),
            P("section", "dp"),
        ),
        check_vma=False,
    )
```

profile of v0, /device:TPU:0, one launch (start us, length us, event | category | flops | bytes accessed | tf_op | source)
XLA Modules:
  0.0 2760.9 jit_solution(11259906612500781263)
XLA Ops:
  11.4 4.4 convert_element_type.810
  18.0 85.2 %all-reduce.100.cloned.1.call-done = bf16[162816]{0:T(1024)(128)(2,1)} async-done(((bf16[162816]{0:T(1024)(128)(2,1)}), bf16[162816]{0:T(1024)(128)(2,1)}) %all-reduce.100.cloned.1.call-update) | async-done | bytes 325648
  104.2 156.8 %all-gather.2.cloned.1.call-done = bf16[1,7667712]{1,0:T(2,128)(2,1)} async-done(((bf16[1,479232]{1,0:T(2,128)(2,1)}), bf16[1,7667712]{1,0:T(2,128)(2,1)}) %all-gather.2.cloned.1.call-update) | async-done | bytes 15335440 | tf_op jit(solution)/shard_map/all_gather | solution.py:209
  260.9 35.4 %convert_element_type.827 = f32[1,7667712]{1,0:T(1,128)} convert(bf16[1,7667712]{1,0:T(2,128)(2,1)} %all-gather.2.cloned.1.call-done) | non-fusion elementwise | flops 7667712 | bytes 46006272 | tf_op jit(solution)/shard_map/convert_element_type | solution.py:212
  296.4 123.2 %conditional.10 = (f32[2,49,768]{2,1,0:T(8,128)S(1)}, f32[2,49,768]{2,1,0:T(8,128)S(1)}, bf16[98,768]{1,0:T(8,128)(2,1)}, s32[2,49,1]{1,0,2:T(2,128)}, f32[2,49,...) conditional(s32[]{:T(128)} %convert_element_type.808, () %tuple.80, ...), branch_computations={%region_22.25_spmd, %region_23.34_spmd} | conditional | flops 1532532224 | bytes 207092928 | solution.py:226
  296.6 16.0 convert.44
  334.4 8.3 fusion.213
  342.8 5.2 reshape.1519
  352.1 5.1 convert_element_type.674
  373.1 9.5 reshape.1522
  382.6 9.2 convert_element_type.687
  391.8 8.2 reshape.1521
  400.0 8.3 convert_element_type.685
  408.3 6.3 multiply_convert_fusion.2
  422.3 122.1 %conditional.8 = (f32[2,49,768]{2,1,0:T(8,128)S(1)}, f32[2,49,768]{2,1,0:T(8,128)S(1)}, bf16[98,768]{1,0:T(8,128)(2,1)}, s32[2,49,1]{1,0,2:T(2,128)S(1)}, f32[2,...) conditional(s32[]{:T(128)} %convert_element_type.808, () %tuple.76, ...), branch_computations={%region_0.0_spmd, %region_1.11_spmd} | conditional | flops 1532532224 | bytes 214482848 | solution.py:226
  422.3 16.1 convert.40
  460.3 8.3 fusion.196
  468.7 5.2 reshape.1508
  477.9 5.2 convert_element_type.622
  498.9 9.4 reshape.1511
  508.3 9.2 convert_element_type.635
  517.6 8.2 reshape.1510
  525.8 8.3 convert_element_type.633
  534.0 6.2 multiply_convert_fusion
  547.4 41.0 %conditional.11 = (f32[]{:T(128)}, bf16[98,768]{1,0:T(8,128)(2,1)}, bf16[768,512]{1,0:T(8,128)(2,1)}, s32[2,196,1]{1,0,2:T(2,128)S(1)}, f32[2,196,512]{2,1,0:T(8...) conditional(s32[]{:T(128)} %convert_element_type.808, ...), branch_computations={%region_32.45_spmd, %region_43.46_spmd} | conditional | flops 3042089472 | bytes 240721040 | solution.py:238
  588.4 20.7 conditional.14
  598.9 10.3 broadcast.1321
  610.4 37.9 %conditional.9 = (f32[]{:T(128)}, bf16[98,768]{1,0:T(8,128)(2,1)}, bf16[768,512]{1,0:T(8,128)(2,1)}, s32[2,196,1]{1,0,2:T(2,128)S(1)}, f32[2,196,512]{2,1,0:T(8,...) conditional(s32[]{:T(128)} %convert_element_type.808, ...), branch_computations={%region_10.23_spmd, %region_21.24_spmd} | conditional | flops 3042089472 | bytes 240721040 | solution.py:238
  648.3 20.3 conditional.12
  658.4 10.1 broadcast.1211
  669.8 132.4 %collective-permute-done.3 = bf16[2,49,768]{2,1,0:T(8,128)(2,1)} collective-permute-done((bf16[2,49,768]{2,1,0:T(8,128)(2,1)}, bf16[2,49,768]{2,1,0:T(8,128)(2,1)}, u32[]{:S(2)}, u32[]{:S(2)}) %collective-permute-start.3) | collective-permute-done | bytes 150560 | tf_op jit(solution)/shard_map/ppermute | solution.py:24
  803.2 199.8 %conditional.15 = (f32[7667712]{0:T(1024)}, f32[162816]{0:T(1024)}) conditional(s32[]{:T(128)} %convert_element_type.808, () %tuple.90, (f32[1,1,768]{2,1,0:T(1,128)}, f32[2,49,768]{2,1,0:T(8,128)S(1)}, f32[2,49,1]{1,0,2:T(2,128)}, f32[2,49,768]{2,1,0:T(8,128)}, f32[2,49,1]{1,0,2:T(2,128)}, /*index=5*/bf16[98,3072]{1,0:T(8,128)(2,1)}, ...), branch_computations={%region_114.0_spmd, %region_115.137_spmd} | conditional | flops 2961753600 | bytes 289310784 | solution.py:226
  819.1 4.8 fusion.239
  849.2 12.7 scatter_custom_fusion.3
  876.1 5.0 convolution_bitcast_fusion.21
  881.1 8.1 copy.267
  889.1 8.0 reshape.1402
  897.1 6.0 convolution_bitcast_fusion.22
  903.1 9.6 copy.258
  912.8 9.4 copy.338
  922.2 6.2 convolution_bitcast_fusion.23
  928.4 9.6 copy.257
  938.0 10.9 reshape.1396
  948.9 53.7 %pad_add_fusion.12 = f32[7667712]{0:T(1024)} fusion(f32[589824]{0:T(1024)S(1)} %copy-done.30, f32[1769472]{0:T(1024)} %reshape.1402, f32[589824]{0:T(1024)} %reshape.1401, f32[2359296]{0:T(1024)} %bitcast.604, f32[2359296]{0:T(1024)} %reshape.1396), kind=kLoop, calls=%fused_computation.481 | loop fusion | flops 30670848 | bytes 61341696 | tf_op jit(solution)/shard_map/transpose(jvp())/cond/branch_1_fun/add_any | solution.py:32
  1003.0 168.3 %collective-permute-done.2 = bf16[2,49,768]{2,1,0:T(8,128)(2,1)} collective-permute-done((bf16[2,49,768]{2,1,0:T(8,128)(2,1)}, bf16[2,49,768]{2,1,0:T(8,128)(2,1)}, u32[]{:S(2)}, u32[]{:S(2)}) %collective-permute-start.2) | collective-permute-done | bytes 150560 | tf_op jit(solution)/shard_map/ppermute | solution.py:24
  1172.2 186.8 %conditional.13 = (f32[7667712]{0:T(1024)}, f32[162816]{0:T(1024)}) conditional(s32[]{:T(128)} %convert_element_type.808, () %tuple.86, (f32[1,1,768]{2,1,0:T(1,128)}, f32[2,49,768]{2,1,0:T(8,128)S(1)}, f32[2,49,1]{1,0,2:T(2,128)}, f32[2,49,768]{2,1,0:T(8,128)}, f32[2,49,1]{1,0,2:T(2,128)}, /*index=5*/bf16[98,3072]{1,0:T(8,128)(2,1)}, ...), branch_computations={%region_69.72_spmd, %region_70.92_spmd} | conditional | flops 2961753600 | bytes 284475584 | solution.py:226
  1188.2 4.8 fusion.237
  1232.2 5.0 convolution_bitcast_fusion.8
  1237.1 8.0 copy.242
  1245.2 8.0 reshape.1374
  1253.2 6.0 convolution_bitcast_fusion.9
  1259.2 9.6 copy.233
  1268.7 9.5 copy.333
  1278.2 6.1 convolution_bitcast_fusion.10
  1284.4 9.6 copy.232
  1293.9 10.9 reshape.1368
  1304.8 54.0 %pad_add_fusion.4 = f32[7667712]{0:T(1024)} fusion(f32[589824]{0:T(1024)S(1)} %copy-done.31, f32[1769472]{0:T(1024)} %reshape.1374, f32[589824]{0:T(1024)} %reshape.1373, f32[2359296]{0:T(1024)} %bitcast.605, f32[2359296]{0:T(1024)} %reshape.1368), kind=kLoop, calls=%fused_computation.360 | loop fusion | flops 30670848 | bytes 61341696 | tf_op jit(solution)/shard_map/transpose(jvp())/cond/branch_1_fun/add_any | solution.py:32
  1360.8 36.7 %copy.325 = f32[1,162816]{0,1:T(8,128)} copy(f32[1,162816]{1,0:T(1,128)S(1)} %bitcast.651) | data formatting | bytes 1302528
  1397.6 70.9 %add_add_fusion.20 = f32[7667712]{0:T(1024)} fusion(f32[7667712]{0:T(1024)} %get-tuple-element.872, f32[7667712]{0:T(1024)} %get-tuple-element.834, f32[7667712]{0:T(1024)} %get-tuple-element.754, f32[7667712]{0:T(1024)} %get-tuple-element.792), kind=kLoop, calls=%fused_computation.538 | loop fusion | flops 23003136 | bytes 153354240 | tf_op jit(solution)/shard_map/add | solution.py:252
  1470.5 694.8 %reduce-scatter.5.cloned.1.call-done = f32[10176,1]{1,0:T(8,128)} async-done(((f32[162816,1]{1,0:T(8,128)}), f32[10176,1]{1,0:T(8,128)}) %reduce-scatter.5.cloned.1.call-update) | async-done | bytes 40720
  2169.3 519.6 %all-reduce.102.cloned.1.call-done = f32[1,7667712]{1,0:T(1,128)} async-done(((f32[1,7667712]{1,0:T(1,128)}), f32[1,7667712]{1,0:T(1,128)}) %all-reduce.102.cloned.1.call-update) | async-done | bytes 30670864
  2688.9 5.6 multiply_reduce_fusion.42
  2695.8 40.2 %all-reduce.96 = (f32[]{:T(128)}, f32[]{:T(128)}) all-reduce(f32[]{:T(128)S(6)} %add.852, f32[]{:T(128)S(6)} %add.859), channel_id=1, replica_groups=mesh['section'=2,'dp'=16] {'section','dp'}, use_global_device_ids=true, to_apply=%region_44.47 | all-reduce | flops 2 | bytes 16 | tf_op jit(solution)/shard_map/psum | solution.py:259
  2737.8 15.2 fusion.194
  (570 shorter events, 295.7 us)
Async XLA Ops:
  7.2 96.0 %all-reduce.100.cloned.1.call-start = ((), (), s32[]{:S(2)}) async-start(), calls=%async_computation.2 | async-start | bytes 651264
  11.4 4.5 copy-start.136
  11.4 249.5 %all-gather.2.cloned.1.call-start = ((), (), s32[]{:S(2)}) async-start(), calls=%async_computation.1 | async-start | bytes 32587776 | tf_op jit(solution)/shard_map/all_gather | solution.py:209
  15.9 2149.4 %reduce-scatter.5.cloned.1.call-start = ((), (), s32[]{:S(2)}) async-start(), calls=%async_computation.3 | async-start | bytes 88571904
  18.0 278.4 %copy-start.24 = (f32[2,196,768]{2,1,0:T(8,128)}, f32[2,196,768]{2,1,0:T(8,128)S(1)}, u32[]{:S(2)}) copy-start(f32[2,196,768]{2,1,0:T(8,128)S(1)} %get-tuple-element.1785) | copy-start | bytes 3612676
  104.2 192.2 %copy-start.16 = (f32[162816]{0:T(1024)}, f32[162816]{0:T(1024)S(1)}, u32[]{:S(2)}) copy-start(f32[162816]{0:T(1024)S(1)} %convert_element_type.829) | copy-start | bytes 1953796
  104.2 192.2 %copy-start.201 = (s32[4,49]{1,0:T(4,128)S(1)}, s32[4,49]{1,0:T(4,128)}, u32[]{:S(2)}) copy-start(s32[4,49]{1,0:T(4,128)} %param.30) | copy-start | bytes 2356
  326.3 4.1 copy-start.191
  361.5 6.4 copy-start.77
  361.5 6.4 copy-start.104
  361.5 6.4 copy-start.183
  364.0 4.3 copy-start.143
  400.0 8.3 copy-start.152
  400.0 14.6 slice-start.4
  408.3 6.3 slice-start.5
  408.3 6.3 copy-start.187
  414.6 3.4 copy-start.156
  414.6 3.4 copy-start.179
  415.6 3.6 copy-start.33
  420.4 126.9 %collective-permute-start.1 = (bf16[2,49,768]{2,1,0:T(8,128)(2,1)}, bf16[2,49,768]{2,1,0:T(8,128)(2,1)}, u32[]{:S(2)}, u32[]{:S(2)}) collective-permute-start(bf16[2,49,768]{2,1,0:T(8,128)(2,1)} %convert_element_type.819), channel_id=1, source_target_pairs={{0,16},{1,17},{2,18},{3,19},{4,20},{5,21},{6,22},{7,23},{8,24},{9,... | collective-permute-start | bytes 451592 | tf_op jit(solution)/shard_map/ppermute | solution.py:24
  422.3 16.1 copy-start.202
  422.3 16.9 copy-start.17
  452.2 4.2 copy-start.193
  487.3 7.0 copy-start.78
  487.3 7.0 copy-start.106
  487.3 7.0 copy-start.184
  489.8 4.9 copy-start.145
  525.8 14.5 slice-start.6
  534.0 6.2 slice-start.7
  534.0 6.2 copy-start.188
  545.3 65.1 %collective-permute-start = (bf16[2,49,768]{2,1,0:T(8,128)(2,1)}, bf16[2,49,768]{2,1,0:T(8,128)(2,1)}, u32[]{:S(2)}, u32[]{:S(2)}) collective-permute-start(bf16[2,49,768]{2,1,0:T(8,128)(2,1)} %convert_element_type.816), channel_id=1, source_target_pairs={{0,16},{1,17},{2,18},{3,19},{4,20},{5,21},{6,22},{7,23},{8,24},{9,... | collective-permute-start | bytes 451592 | tf_op jit(solution)/shard_map/ppermute | solution.py:24
  609.1 193.1 %collective-permute-start.3 = (bf16[2,49,768]{2,1,0:T(8,128)(2,1)}, bf16[2,49,768]{2,1,0:T(8,128)(2,1)}, u32[]{:S(2)}, u32[]{:S(2)}) collective-permute-start(bf16[2,49,768]{2,1,0:T(8,128)(2,1)} %get-tuple-element.836), channel_id=1, source_target_pairs={{16,0},{17,1},{18,2},{19,3},{20,4},{21,5},{22,6},{23,7},{24,8},{25... | collective-permute-start | bytes 451592 | tf_op jit(solution)/shard_map/ppermute | solution.py:24
  668.5 502.7 %collective-permute-start.2 = (bf16[2,49,768]{2,1,0:T(8,128)(2,1)}, bf16[2,49,768]{2,1,0:T(8,128)(2,1)}, u32[]{:S(2)}, u32[]{:S(2)}) collective-permute-start(bf16[2,49,768]{2,1,0:T(8,128)(2,1)} %get-tuple-element.756), channel_id=1, source_target_pairs={{16,0},{17,1},{18,2},{19,3},{20,4},{21,5},{22,6},{23,7},{24,8},{25... | collective-permute-start | bytes 451592 | tf_op jit(solution)/shard_map/ppermute | solution.py:24
  803.1 369.1 %copy-start.39 = (f32[2,49,768]{2,1,0:T(8,128)S(1)}, f32[2,49,768]{2,1,0:T(8,128)}, u32[]{:S(2)}) copy-start(f32[2,49,768]{2,1,0:T(8,128)} %copy-done.38) | copy-start | bytes 903172
  819.1 4.8 copy-start.41
  825.6 5.9 copy-start.149
  829.3 3.9 copy-start.107
  829.4 5.1 copy-start.131
  831.5 3.4 copy-start.144
  842.9 3.4 copy-start.35
  842.9 5.4 copy-start.108
  848.2 13.7 copy-start.151
  848.3 13.7 copy-start.171
  848.3 13.7 copy-start.173
  848.3 13.7 copy-start.175
  848.3 13.7 copy-start.177
  889.1 8.0 copy-start.42
  912.8 9.4 copy-start.116
  938.0 10.9 copy-start.30
  1188.1 4.8 copy-start.43
  1188.2 5.9 copy-start.220
  1188.2 5.9 copy-start.212
  1194.1 5.8 copy-start.150
  1199.9 3.4 copy-start.146
  1211.2 3.4 copy-start.222
  1211.2 3.4 copy-start.210
  1245.2 8.0 copy-start.44
  1268.7 9.5 copy-start.118
  1293.9 10.9 copy-start.31
  1397.6 1291.3 %all-reduce.102.cloned.1.call-start = ((), (), s32[]{:S(2)}) async-start(), calls=%async_computation.4 | async-start | bytes 61341696
  2165.3 571.5 %copy-start.147 = (f32[1,10176]{1,0:T(1,128)S(1)}, f32[1,10176]{1,0:T(1,128)}, u32[]{:S(2)}) copy-start(f32[1,10176]{1,0:T(1,128)} %param.35) | copy-start | bytes 122116
  2165.3 571.5 %copy-start.153 = (f32[1,10176]{1,0:T(1,128)S(1)}, f32[1,10176]{1,0:T(1,128)}, u32[]{:S(2)}) copy-start(f32[1,10176]{1,0:T(1,128)} %param.36) | copy-start | bytes 122116
  2165.3 571.5 %copy-start.154 = (f32[1,10176]{1,0:T(1,128)S(1)}, f32[1,10176]{1,0:T(1,128)}, u32[]{:S(2)}) copy-start(f32[1,10176]{1,0:T(1,128)} %param.37) | copy-start | bytes 122116
  2168.6 569.2 %copy-start.40 = (f32[1,479232]{1,0:T(1,128)S(1)}, f32[1,479232]{1,0:T(1,128)}, u32[]{:S(2)}) copy-start(f32[1,479232]{1,0:T(1,128)} %param.32) | copy-start | bytes 5750788
  (49 other events, 113.3 us)
Sparse Core Ops, SparseCore 0:
  12.0 91.1 all-reduce.99
  105.4 155.4 all-gather.1
  1397.7 767.5 reduce-scatter.4
  2169.3 519.6 all-reduce.101
where the time goes:
time: 2770 us; the launch traced here: 2760 us
  waiting for transfers between devices  1760 us (64%)
  local copies, waits for them, and re-layouts  437 us (16%)
  other arithmetic  359 us (13%)
  matrix products  110 us (4%)
  blocking collectives  40.2 us (1%)
  loops' own time  31.6 us (1%)
    unnamed x7, waiting for transfers between devices  1300 us
    ppermute x4, waiting for transfers between devices, shifted(): lax.ppermute(value, axis, [(source, source + steps) for source in range(i...  301 us
    all_gather x1, waiting for transfers between devices, body(): lax.all_gather(mat_master.astype(jnp.bfloat16), 'dp', axis=1, tiled=True)  157 us
    convert_element_type x40, local copies, waits for them, and re-layouts, linear(): result = round_grad(product(values.reshape(-1, shape[-1]), weight))  110 us
    add_any x4, other arithmetic, carve(): pieces.append(flat[offset:offset + count].reshape(shape))  109 us
    another operation x94, local copies, waits for them, and re-layouts  95.2 us
    dot_general x28, matrix products, linear(): result = round_grad(product(values.reshape(-1, shape[-1]), weight))  90.7 us
    add x1, other arithmetic, body(): grad_mats = grad_mats + dmat_dec + dmat_enc  70.9 us
  transfers between devices with their start and end apart: 8, of which 6 were waited for; matrix products, arithmetic and copies ran while one was open for 18% of the time, Pallas kernels for 0%

commit v1 on v0

v1 whole, which is shorter than its diff:
```python
import functools
import math

import jax
import jax.numpy as jnp
from jax import lax
from jax.experimental import pallas as pl
from jax.experimental.pallas import tpu as pltpu
from jax.sharding import PartitionSpec as P

PIX = 768
DE = 768
HE = 12
FE = 3072
DD = 512
HD = 16
FD = 2048
PATCHES = 196
VIS = 49
STEP = 10
ROWS_E = 64
ROWS_D = 208
EPS = 1e-6
BF = jnp.bfloat16
F32 = jnp.float32
VMEM_LIMIT = 63 * 1024 * 1024

ENC_MATS = [(PIX, DE), (DE, 3 * DE), (DE, DE), (DE, FE), (FE, DE)]
DEC_MATS = [(DE, DD), (DD, 3 * DD), (DD, DD), (DD, FD), (FD, DD), (DD, PIX)]
ENC_VECS = [DE, PATCHES * DE, DE, DE, 2 * DE, DE, DE, DE, FE, DE, DE, DE]
DEC_VECS = [DD, DD, PATCHES * DD, DD, DD, 2 * DD, DD, DD, DD, FD, DD, DD, DD, PIX]


def starts(sizes):
    total, found = 0, []
    for size in sizes:
        found.append(total)
        total += size
    return found, total


ENC_TILES = [k * n // 2048 for k, n in ENC_MATS]
DEC_TILES = [k * n // 2048 for k, n in DEC_MATS]
ENC_BASE, ENC_TOTAL = starts(ENC_TILES)
DEC_BASE, DEC_TOTAL = starts(DEC_TILES)
EV, _ = starts([size // 128 for size in ENC_VECS])
DV, _ = starts([size // 128 for size in DEC_VECS])


class Mat:
    def __init__(self, ref, base, shape):
        self.rows, self.columns = shape
        self.blocks = self.columns // 128
        count = self.rows * self.columns // 2048
        self.ref = ref.at[pl.ds(base, count)].reshape(self.rows // 16, self.blocks, 16, 128)

    def cols(self, block):
        parts = [self.ref[:, 2 * block + half].reshape(self.rows, 128) for half in range(2)]
        return jnp.concatenate(parts, 1)

    def band(self, block):
        part = self.ref.at[pl.ds(block * 16, 16)]
        return jnp.concatenate([part[:, j].reshape(256, 128) for j in range(self.blocks)], 1)

    def put_cols(self, block, value):
        for half in range(2):
            piece = value[:, half * 128 : (half + 1) * 128].astype(BF)
            self.ref[:, 2 * block + half] = piece.reshape(self.rows // 16, 16, 128)

    def put_band(self, block, value):
        part = self.ref.at[pl.ds(block * 16, 16)]
        for j in range(self.blocks):
            part[:, j] = value[:, j * 128 : (j + 1) * 128].astype(BF).reshape(16, 16, 128)


def dot(a, b):
    return jnp.dot(a, b, preferred_element_type=F32)


def dot_t(a, b):
    return lax.dot_general(a, b, (((1,), (1,)), ((), ())), preferred_element_type=F32)


def t_dot(a, b):
    return lax.dot_general(a, b, (((0,), (0,)), ((), ())), preferred_element_type=F32)


def loop(count, body, init=0):
    return lax.fori_loop(0, count, body, init)


def lanes(block, width=256):
    return pl.ds(pl.multiple_of(block * width, width), width)


def row_of(vec, start, width):
    return jnp.concatenate([vec[start + j : start + j + 1, :] for j in range(width // 128)], 1)


def row_at(vec, start, block):
    return jnp.concatenate([vec[pl.ds(start + 2 * block + h, 1), :] for h in range(2)], 1)


def put_row(dvec, start, value):
    for j in range(value.shape[1] // 128):
        dvec[start + j : start + j + 1, :] = value[:, j * 128 : (j + 1) * 128]


def put_row_at(dvec, start, block, value):
    for h in range(2):
        dvec[pl.ds(start + 2 * block + h, 1), :] = value[:, h * 128 : (h + 1) * 128]


def fold(value):
    return value.reshape(value.shape[0] // 8, 8, value.shape[1]).sum(0)


def total_row(value):
    return jnp.sum(value, 0, keepdims=True)


def norm_parts(x):
    mean = jnp.mean(x, -1, keepdims=True)
    centred = x - mean
    scale = lax.rsqrt(jnp.mean(centred * centred, -1, keepdims=True) + EPS)
    return centred * scale, scale


CHUNK = 32


def chunk_rows(i):
    return pl.ds(pl.multiple_of(i * CHUNK, CHUNK), CHUNK)


def norm_rows(x_ref, out_ref, vec, gain_at, shift_at, width, add_ref=None, bias_at=None):
    gain, shift = row_of(vec, gain_at, width), row_of(vec, shift_at, width)
    bias = None if bias_at is None else row_of(vec, bias_at, width)

    def step(i, carry):
        rows = chunk_rows(i)
        x = x_ref[rows, :]
        if add_ref is not None:
            x = x + add_ref[rows, :] + bias
            add_ref[rows, :] = x
        unit, _ = norm_parts(x)
        out_ref[rows, :] = (unit * gain + shift).astype(BF)
        return carry

    loop(x_ref.shape[0] // CHUNK, step)


def norm_back_rows(x_ref, dy_ref, dx_ref, dxb_ref, vec, dvec, gain_at, shift_at, width, bias_at, add):
    gain = row_of(vec, gain_at, width)
    zero = jnp.zeros((8, width), F32)

    def step(i, carry):
        dgain, dshift, dbias = carry
        rows = chunk_rows(i)
        unit, scale = norm_parts(x_ref[rows, :])
        dy = dy_ref[rows, :].astype(F32)
        dunit = dy * gain
        dx = scale * (
            dunit
            - jnp.mean(dunit, -1, keepdims=True)
            - unit * jnp.mean(dunit * unit, -1, keepdims=True)
        )
        if add:
            dx = dx + dx_ref[rows, :]
        dx_ref[rows, :] = dx
        dxb_ref[rows, :] = dx.astype(BF)
        return dgain + fold(dy * unit), dshift + fold(dy), dbias + fold(dx)

    dgain, dshift, dbias = loop(x_ref.shape[0] // CHUNK, step, (zero, zero, zero))
    put_row(dvec, gain_at, total_row(dgain))
    put_row(dvec, shift_at, total_row(dshift))
    if bias_at is not None:
        put_row(dvec, bias_at, total_row(dbias))
    return dbias


GELU_C = math.sqrt(2.0 / math.pi)


def gelu_parts(x):
    square = x * x
    t = jnp.tanh(x * (GELU_C + (GELU_C * 0.044715) * square))
    half = 0.5 * (1.0 + t)
    return x * half, half + (0.5 * x) * (1.0 - t * t) * (
        GELU_C + (3.0 * 0.044715 * GELU_C) * square
    )


def head_mask(size):
    lane = lax.broadcasted_iota(jnp.int32, (1, 128), 1)
    return [(lane >= h * size) & (lane < (h + 1) * size) for h in range(128 // size)]


def attention(qkv, probs, att, bias, group, groups, width, size):
    blocks = width // 128
    masks = head_mask(size)

    def step(i, carry):
        g, b = i // blocks, i % blocks
        rows = pl.ds(pl.multiple_of(g * group, 16), group)
        q = qkv[rows, lanes(b, 128)]
        k = qkv[rows, lanes(blocks + b, 128)]
        v = qkv[rows, lanes(2 * blocks + b, 128)]
        out = jnp.zeros((group, 128), F32)
        for h, mask in enumerate(masks):
            s = dot_t(jnp.where(mask, q, jnp.zeros_like(q)), k) + bias
            e = jnp.exp(s - jnp.max(s, -1, keepdims=True))
            p = (e * (1.0 / jnp.sum(e, -1, keepdims=True))).astype(BF)
            probs[i * len(masks) + h] = p
            out = jnp.where(mask, dot(p, v), out)
        att[rows, lanes(b, 128)] = out.astype(BF)
        return carry

    loop(groups * blocks, step)


def attention_back(qkv, probs, datt, dqkv, dvec, qv_at, group, groups, width, size):
    blocks = width // 128
    masks = head_mask(size)
    scale = size ** (-0.5)
    for j in range(2 * blocks):
        dvec[qv_at + j : qv_at + j + 1, :] = jnp.zeros((1, 128), F32)

    def step(i, carry):
        g, b = i // blocks, i % blocks
        rows = pl.ds(pl.multiple_of(g * group, 16), group)
        q = qkv[rows, lanes(b, 128)]
        k = qkv[rows, lanes(blocks + b, 128)]
        v = qkv[rows, lanes(2 * blocks + b, 128)]
        da = datt[rows, lanes(b, 128)]
        zero = jnp.zeros((group, 128), F32)
        dq, dk, dv = zero, zero, zero
        for h, mask in enumerate(masks):
            p = probs[i * len(masks) + h]
            dp = dot_t(jnp.where(mask, da, jnp.zeros_like(da)), v)
            wide = p.astype(F32)
            prod = wide * dp
            ds = (prod - wide * jnp.sum(prod, -1, keepdims=True)).astype(BF)
            dq = jnp.where(mask, dot(ds, k), dq)
            dk = jnp.where(mask, t_dot(ds, q), dk)
            dv = jnp.where(mask, t_dot(p, da), dv)
        dq = dq * scale
        dqkv[rows, lanes(b, 128)] = dq.astype(BF)
        dqkv[rows, lanes(blocks + b, 128)] = dk.astype(BF)
        dqkv[rows, lanes(2 * blocks + b, 128)] = dv.astype(BF)
        dvec[pl.ds(qv_at + b, 1), :] += total_row(dq)
        dvec[pl.ds(qv_at + blocks + b, 1), :] += total_row(dv)
        return carry

    loop(groups * blocks, step)


def block_forward(s, mats, vec, at, width, hidden, size, bias, group, groups):
    w_qkv, w_proj, w_up, w_down = mats
    pairs = width // 256
    scale = size ** (-0.5)
    norm_rows(s.x0, s.n1, vec, at["g1"], at["s1"], width)

    def qkv_step(j, carry):
        part = j // pairs
        row = row_at(vec, at["qv"], jnp.where(part == 0, j, jnp.maximum(j - pairs, 0)))
        value = dot(s.n1[...], w_qkv.cols(j)) + jnp.where(part == 1, 0.0, row)
        s.qkv[:, lanes(j)] = (value * jnp.where(part == 0, scale, 1.0)).astype(BF)
        return carry

    loop(3 * pairs, qkv_step)
    attention(s.qkv, s.probs, s.att, bias, group, groups, width, size)

    def proj_step(j, carry):
        s.x1[:, lanes(j)] = dot(s.att[...], w_proj.cols(j))
        return carry

    loop(pairs, proj_step)
    norm_rows(s.x0, s.n2, vec, at["g2"], at["s2"], width, s.x1, at["bo"])

    def mlp_step(j, carry):
        h = dot(s.n2[...], w_up.cols(j)) + row_at(vec, at["bu"], j)
        s.h[:, lanes(j)] = h
        u = gelu_parts(h)[0].astype(BF)
        update = dot(u, w_down.band(j))

        @pl.when(j == 0)
        def _():
            s.x2[...] = update

        @pl.when(j > 0)
        def _():
            s.x2[...] += update

        return carry

    loop(hidden // 256, mlp_step)


def block_backward(s, mats, grads, vec, dvec, at, width, hidden, size, group, groups):
    w_qkv, w_proj, w_up, w_down = mats
    d_qkv, d_proj, d_up, d_down = grads
    pairs = width // 256
    s.flip[...] = s.n2[...].T

    def mlp_step(j, carry):
        dxb = s.dxb[...]
        u, slope = gelu_parts(s.h[:, lanes(j)])
        dh = dot_t(dxb, w_down.band(j)) * slope
        put_row_at(dvec, at["bu"], j, total_row(fold(dh)))
        dh = dh.astype(BF)
        d_down.put_band(j, t_dot(u.astype(BF), dxb))
        d_up.put_cols(j, dot(s.flip[...], dh))
        update = dot_t(dh, w_up.cols(j))

        @pl.when(j == 0)
        def _():
            s.dn[...] = update

        @pl.when(j > 0)
        def _():
            s.dn[...] += update

        return carry

    loop(hidden // 256, mlp_step)
    norm_back_rows(s.x1, s.dn, s.dx, s.dxb, vec, dvec, at["g2"], at["s2"], width, at["bo"], True)

    def proj_step(j, carry):
        dxb = s.dxb[...]
        s.datt[:, lanes(j)] = dot_t(dxb, w_proj.band(j)).astype(BF)
        d_proj.put_band(j, t_dot(s.att[:, lanes(j)], dxb))
        return carry

    loop(pairs, proj_step)
    attention_back(s.qkv, s.probs, s.datt, s.dqkv, dvec, at["qv"], group, groups, width, size)
    s.flip[...] = s.n1[...].T

    def weight_step(j, carry):
        d_qkv.put_cols(j, dot(s.flip[...], s.dqkv[:, lanes(j)]))
        return carry

    loop(3 * pairs, weight_step)

    def input_step(j, carry):
        s.dn[:, lanes(j)] = dot_t(s.dqkv[...], w_qkv.band(j))
        return carry

    loop(pairs, input_step)
    norm_back_rows(s.x0, s.dn, s.dx, s.dxb, vec, dvec, at["g1"], at["s1"], width, None, True)


ENC_AT = dict(g1=EV[2], s1=EV[3], qv=EV[4], bo=EV[5], g2=EV[6], s2=EV[7], bu=EV[8])
DEC_AT = dict(g1=DV[3], s1=DV[4], qv=DV[5], bo=DV[6], g2=DV[7], s2=DV[8], bu=DV[9])


class Bag:
    def __init__(self, names, refs):
        for name, ref in zip(names, refs):
            setattr(self, name, ref)


def load_mats(source, kept, sem, copies):
    started = []
    for index, (pick, start, count) in enumerate(copies):
        copy = pltpu.make_async_copy(pick(source), kept.at[pl.ds(start, count)], sem.at[index])
        copy.start()
        started.append(copy)
    return started


def plain_copies(base, tiles):
    return [
        ((lambda ref, a=a, c=c: ref.at[pl.ds(a, c)]), a, c) for a, c in zip(base, tiles)
    ]


def visible_rows(column, count):
    lane = lax.broadcasted_iota(jnp.int32, (1, count), 1)
    return jnp.where(column == lane, 1.0, 0.0).astype(BF)


def encoder_bias(rows):
    r = lax.broadcasted_iota(jnp.int32, (rows, rows), 0)
    c = lax.broadcasted_iota(jnp.int32, (rows, rows), 1)
    same = (r // ROWS_E == c // ROWS_E) & (c % ROWS_E < VIS)
    return jnp.where(same, 0.0, -1e30)


ENC_KEEP = ["pick", "x0", "n1", "qkv", "probs", "att", "x1", "n2", "h", "x2"]


def enc_shapes(images):
    rows = images * ROWS_E
    return dict(
        pick=((rows, PIX), BF),
        x0=((rows, DE), F32),
        n1=((rows, DE), BF),
        qkv=((rows, 3 * DE), BF),
        probs=((HE, rows, rows), BF),
        att=((rows, DE), BF),
        x1=((rows, DE), F32),
        n2=((rows, DE), BF),
        h=((rows, FE), F32),
        x2=((rows, DE), F32),
    )


def position_column(vec, start, blocks, j):
    return vec[pl.ds(start + j, PATCHES, stride=blocks), :]


def encoder_forward_kernel(images, copies, vis, pix, vec, weights, *refs):
    latent = refs[0]
    s = Bag(ENC_KEEP, refs[1 : 1 + len(ENC_KEEP)])
    kept, posit, sem = refs[1 + len(ENC_KEEP) :]
    started = load_mats(weights, kept, sem, copies)
    rows = images * ROWS_E
    mats = [Mat(kept, b, shape) for b, shape in zip(ENC_BASE, ENC_MATS)]
    posit[...] = jnp.zeros_like(posit)
    for j in range(DE // 128):
        posit[0:PATCHES, j * 128 : (j + 1) * 128] = position_column(vec, EV[1], DE // 128, j)
    for i in range(images):
        where = pl.ds(i * ROWS_E, ROWS_E)
        hot = visible_rows(vis[where, :], ROWS_D)
        s.pick[where, :] = dot(hot, pix[i]).astype(BF)
        s.x0[where, :] = dot(hot, posit[...].astype(BF)) + row_of(vec, EV[0], DE)
    for copy in started:
        copy.wait()

    def embed_step(j, carry):
        s.x0[:, lanes(j)] += dot(s.pick[...], mats[0].cols(j))
        return carry

    loop(DE // 256, embed_step)
    block_forward(
        s, mats[1:5], vec, ENC_AT, DE, FE, DE // HE, encoder_bias(rows), rows, 1
    )
    norm_rows(s.x1, latent, vec, EV[10], EV[11], DE, s.x2, EV[9])


def encoder_forward(images, copies, vis, pix, vec, weights):
    shapes = enc_shapes(images)
    rows = images * ROWS_E
    vm = pl.BlockSpec(memory_space=pltpu.VMEM)
    return pl.pallas_call(
        functools.partial(encoder_forward_kernel, images, copies),
        out_shape=[jax.ShapeDtypeStruct((rows, DE), BF)]
        + [jax.ShapeDtypeStruct(*shapes[name]) for name in ENC_KEEP],
        in_specs=[vm, vm, vm, pl.BlockSpec(memory_space=pl.ANY)],
        out_specs=[vm] * (1 + len(ENC_KEEP)),
        scratch_shapes=[
            pltpu.VMEM((ENC_TOTAL, 16, 128), BF),
            pltpu.VMEM((ROWS_D, DE), F32),
            pltpu.SemaphoreType.DMA((len(copies),)),
        ],
        name="encoder_forward",
        compiler_params=pltpu.CompilerParams(vmem_limit_bytes=VMEM_LIMIT),
    )(vis, pix, vec, weights)


def store_mats(kept, out, sem, index, base, count):
    copy = pltpu.make_async_copy(
        kept.at[pl.ds(base, count)], out.at[pl.ds(base, count)], sem.at[index]
    )
    copy.start()
    return copy


def encoder_backward_kernel(images, copies, vis, vec, dlatent, *refs):
    s = Bag(ENC_KEEP, refs[: len(ENC_KEEP)])
    weights, dmats, dvec = refs[len(ENC_KEEP) : len(ENC_KEEP) + 3]
    kept, dkept, s.dx, s.dxb, s.dn, s.datt, s.dqkv, s.flip, sem, out_sem = refs[
        len(ENC_KEEP) + 3 :
    ]
    started = load_mats(weights, kept, sem, copies)
    rows = images * ROWS_E
    mats = [Mat(kept, b, shape) for b, shape in zip(ENC_BASE, ENC_MATS)]
    grads = [Mat(dkept, b, shape) for b, shape in zip(ENC_BASE, ENC_MATS)]
    dvec[EV[11] + DE // 128 :, :] = jnp.zeros_like(dvec[EV[11] + DE // 128 :, :])
    norm_back_rows(
        s.x2, dlatent, s.dx, s.dxb, vec, dvec, EV[10], EV[11], DE, EV[9], False
    )
    for copy in started:
        copy.wait()
    block_backward(
        s, mats[1:5], grads[1:5], vec, dvec, ENC_AT, DE, FE, DE // HE, rows, 1
    )
    put_row(dvec, EV[0], jnp.sum(s.dx[...], 0, keepdims=True))

    def embed_step(j, carry):
        grads[0].put_band(j, t_dot(s.pick[:, lanes(j)], s.dxb[...]))
        return carry

    loop(DE // 256, embed_step)
    out = store_mats(dkept, dmats, out_sem, 0, 0, ENC_TOTAL)
    hot = visible_rows(vis[...], ROWS_D)
    for j in range(DE // 128):
        value = t_dot(hot, s.dxb[:, j * 128 : (j + 1) * 128])
        dvec[pl.ds(EV[1] + j, PATCHES, stride=DE // 128), :] = value[0:PATCHES]
    out.wait()


def encoder_backward(images, copies, vis, vec, dlatent, saved, weights):
    rows = images * ROWS_E
    vm = pl.BlockSpec(memory_space=pltpu.VMEM)
    hbm = pl.BlockSpec(memory_space=pl.ANY)
    return pl.pallas_call(
        functools.partial(encoder_backward_kernel, images, copies),
        out_shape=[
            jax.ShapeDtypeStruct((ENC_TOTAL, 16, 128), BF),
            jax.ShapeDtypeStruct(vec.shape, F32),
        ],
        in_specs=[vm] * (3 + len(ENC_KEEP)) + [hbm],
        out_specs=[hbm, vm],
        scratch_shapes=[
            pltpu.VMEM((ENC_TOTAL, 16, 128), BF),
            pltpu.VMEM((ENC_TOTAL, 16, 128), BF),
            pltpu.VMEM((rows, DE), F32),
            pltpu.VMEM((rows, DE), BF),
            pltpu.VMEM((rows, DE), F32),
            pltpu.VMEM((rows, DE), BF),
            pltpu.VMEM((rows, 3 * DE), BF),
            pltpu.VMEM((DE, rows), BF),
            pltpu.SemaphoreType.DMA((len(copies),)),
            pltpu.SemaphoreType.DMA((1,)),
        ],
        name="encoder_backward",
        compiler_params=pltpu.CompilerParams(vmem_limit_bytes=VMEM_LIMIT),
    )(vis, vec, dlatent, *saved, weights)


def decoder_kernel(images, copies, masked_total, latent, places, pix, vec, weights, *refs):
    dlatent, loss, dmats, dvec = refs[:4]
    s = Bag(
        ["x0", "x1", "x2", "n1", "n2", "qkv", "probs", "att", "h", "dx", "dxb", "dn", "dqkv", "flip"],
        refs[4:18],
    )
    kept, dkept, posit, dguess, sem, out_sem = refs[18:]
    s.datt = s.n2
    rows = images * ROWS_D
    mats = [Mat(kept, b, shape) for b, shape in zip(DEC_BASE, DEC_MATS)]
    grads = [Mat(dkept, b, shape) for b, shape in zip(DEC_BASE, DEC_MATS)]
    started = load_mats(weights, kept, sem, copies)
    posit[...] = jnp.zeros_like(posit)
    for j in range(DD // 128):
        posit[0:PATCHES, j * 128 : (j + 1) * 128] = position_column(vec, DV[2], DD // 128, j)
    dvec[DV[13] + PIX // 128 :, :] = jnp.zeros_like(dvec[DV[13] + PIX // 128 :, :])
    for copy in started:
        copy.wait()
    for i in range(images):
        part = pl.ds(i * ROWS_E, ROWS_E)
        where = pl.ds(i * ROWS_D, ROWS_D)
        for j in range(DD // 256):
            cut = slice(j * 256, (j + 1) * 256)
            z = dot(latent[part, :], mats[0].cols(j)) + row_of(vec, DV[0] + 2 * j, 256)
            place = places[where, :]
            hot = visible_rows(jnp.where(place < VIS, place, -1), ROWS_E)
            high = z.astype(BF)
            low = (z - high.astype(F32)).astype(BF)
            token = jnp.where(place >= VIS, 1.0, 0.0) * row_of(vec, DV[1] + 2 * j, 256)
            s.x0[where, cut] = dot(hot, high) + dot(hot, low) + token + posit[:, cut]
    lane = lax.broadcasted_iota(jnp.int32, (1, ROWS_D), 1)
    bias = jnp.where(lane < PATCHES, 0.0, -1e30)
    block_forward(
        s, mats[1:5], vec, DEC_AT, DD, FD, DD // HD, bias, ROWS_D, images
    )
    norm_rows(s.x1, s.dxb, vec, DV[11], DV[12], DD, s.x2, DV[10])
    factor = 2.0 / (PIX * masked_total)

    def head_step(j, total):
        value = dot(s.dxb[...], mats[5].cols(j)) + row_at(vec, DV[13], j)
        count = jnp.zeros((8, 256), F32)
        column = jnp.zeros((8, 256), F32)
        for i in range(images):
            where = slice(i * ROWS_D, (i + 1) * ROWS_D)
            error = value[where] - pix[i, :, lanes(j)].astype(F32)
            error = jnp.where(places[where, :] >= VIS, error, 0.0)
            count = count + fold(error * error)
            error = error * factor
            column = column + fold(error)
            dguess[where, lanes(j)] = error.astype(BF)
        put_row_at(dvec, DV[13], j, total_row(column))
        return total + count

    total = loop(PIX // 256, head_step, jnp.zeros((8, 256), F32))
    loss[...] = jnp.broadcast_to(jnp.sum(total) * (1.0 / PIX), (8, 128))
    s.flip[...] = s.dxb[...].T

    def head_weight_step(j, carry):
        grads[5].put_cols(j, dot(s.flip[...], dguess[:, lanes(j)]))
        return carry

    loop(PIX // 256, head_weight_step)

    def head_input_step(j, carry):
        s.dn[:, lanes(j)] = dot_t(dguess[...], mats[5].band(j))
        return carry

    loop(DD // 256, head_input_step)
    norm_back_rows(s.x2, s.dn, s.dx, s.dxb, vec, dvec, DV[11], DV[12], DD, DV[10], False)
    block_backward(
        s, mats[1:5], grads[1:5], vec, dvec, DEC_AT, DD, FD, DD // HD, ROWS_D, images
    )
    token = jnp.zeros((8, DD), F32)
    spot = jnp.zeros((ROWS_D, DD), F32)
    back = []
    for i in range(images):
        where = pl.ds(i * ROWS_D, ROWS_D)
        place = places[where, :]
        dx = s.dx[where, :]
        spot = spot + dx
        token = token + fold(jnp.where(place >= VIS, dx, 0.0))
        hot = visible_rows(jnp.where(place < VIS, place, -1), ROWS_E)
        back.append(t_dot(hot, s.dxb[where, :]))
    posit[...] = spot
    for j in range(DD // 128):
        dvec[pl.ds(DV[2] + j, PATCHES, stride=DD // 128), :] = posit[
            0:PATCHES, j * 128 : (j + 1) * 128
        ]
    put_row(dvec, DV[1], total_row(token))
    back = jnp.concatenate(back, 0)
    put_row(dvec, DV[0], jnp.sum(back, 0, keepdims=True))
    back = back.astype(BF)
    for j in range(DE // 256):
        grads[0].put_band(j, t_dot(latent[:, j * 256 : (j + 1) * 256], back))
        dlatent[:, j * 256 : (j + 1) * 256] = dot_t(back, mats[0].band(j)).astype(BF)
    out = store_mats(dkept, dmats, out_sem, 0, 0, DEC_TOTAL)
    out.wait()


def decoder_step(images, copies, masked_total, latent, places, pix, vec, weights):
    rows = images * ROWS_D
    vm = pl.BlockSpec(memory_space=pltpu.VMEM)
    hbm = pl.BlockSpec(memory_space=pl.ANY)
    probs = images * HD
    return pl.pallas_call(
        functools.partial(decoder_kernel, images, copies, masked_total),
        out_shape=[
            jax.ShapeDtypeStruct((images * ROWS_E, DE), BF),
            jax.ShapeDtypeStruct((8, 128), F32),
            jax.ShapeDtypeStruct((DEC_TOTAL, 16, 128), BF),
            jax.ShapeDtypeStruct(vec.shape, F32),
        ],
        in_specs=[vm, vm, vm, vm, hbm],
        out_specs=[vm, vm, hbm, vm],
        scratch_shapes=[
            pltpu.VMEM((rows, DD), F32),
            pltpu.VMEM((rows, DD), F32),
            pltpu.VMEM((rows, DD), F32),
            pltpu.VMEM((rows, DD), BF),
            pltpu.VMEM((rows, DD), BF),
            pltpu.VMEM((rows, 3 * DD), BF),
            pltpu.VMEM((probs, ROWS_D, ROWS_D), BF),
            pltpu.VMEM((rows, DD), BF),
            pltpu.VMEM((rows, FD), F32),
            pltpu.VMEM((rows, DD), F32),
            pltpu.VMEM((rows, DD), BF),
            pltpu.VMEM((rows, DD), F32),
            pltpu.VMEM((rows, 3 * DD), BF),
            pltpu.VMEM((DD, rows), BF),
            pltpu.VMEM((DEC_TOTAL, 16, 128), BF),
            pltpu.VMEM((DEC_TOTAL, 16, 128), BF),
            pltpu.VMEM((ROWS_D, DD), F32),
            pltpu.VMEM((rows, PIX), BF),
            pltpu.SemaphoreType.DMA((len(copies),)),
            pltpu.SemaphoreType.DMA((1,)),
        ],
        name="decoder_step",
        compiler_params=pltpu.CompilerParams(vmem_limit_bytes=VMEM_LIMIT),
    )(latent, places, pix, vec, weights)


def natural(flat, shapes):
    pieces, offset = [], 0
    for rows, columns in shapes:
        piece = flat[offset : offset + rows * columns].reshape(rows // 16, 16, columns // 128, 128)
        pieces.append(piece.transpose(0, 2, 1, 3).reshape(-1, 16, 128))
        offset += rows * columns
    return jnp.concatenate(pieces, 0)


def flat_from_natural(tiles, shapes, total):
    pieces, offset = [], 0
    for rows, columns in shapes:
        count = rows * columns // 2048
        piece = tiles[offset : offset + count].reshape(rows // 16, columns // 128, 16, 128)
        pieces.append(piece.transpose(0, 2, 1, 3).reshape(-1))
        offset += count
    flat = jnp.concatenate(pieces)
    return jnp.pad(flat, (0, total - flat.shape[0]))


def shifted(value, axis, steps):
    count = lax.axis_size(axis)
    initial, last = (max(0, -steps), min(count, count - steps))
    return lax.ppermute(value, axis, [(source, source + steps) for source in range(initial, last)])


def adam_update(master, first, second, grad, rate, decay):
    first = 0.9 * first + 0.1 * grad
    second = 0.95 * second + 0.05 * grad * grad
    step_first = first / (1.0 - 0.9**STEP)
    step_second = second / (1.0 - 0.95**STEP)
    master = master - rate * (step_first / (jnp.sqrt(step_second) + 1e-08) + decay * master)
    return (master, first, second)


def body(
    pixels, visible, restore, mat_master, mat_first, mat_second, vec_master, vec_first, vec_second
):
    images = pixels.shape[0]
    total = mat_master.shape[1] * lax.axis_size("dp")
    masked_total = (PATCHES - VIS) * images * lax.axis_size("dp")
    encoding = lax.axis_index("section") == 0
    enc_copies = plain_copies(ENC_BASE, ENC_TILES)
    dec_copies = plain_copies(DEC_BASE, DEC_TILES)
    mats = lax.all_gather(mat_master.astype(BF), "dp", axis=1, tiled=True)[0]
    vecs = lax.all_gather(vec_master.astype(BF), "dp", axis=1, tiled=True)[0]
    vecs = vecs.astype(F32).reshape(-1, 128)
    pix = jnp.pad(pixels, ((0, 0), (0, ROWS_D - PATCHES), (0, 0)))
    vis = jnp.pad(visible, ((0, 0), (0, ROWS_E - VIS)), constant_values=-1).reshape(-1, 1)
    places = jnp.pad(restore, ((0, 0), (0, ROWS_D - PATCHES)), constant_values=-1).reshape(-1, 1)
    weights = lax.cond(
        encoding,
        lambda m: natural(m, ENC_MATS),
        lambda m: jnp.pad(natural(m, DEC_MATS), ((0, ENC_TOTAL - DEC_TOTAL), (0, 0), (0, 0))),
        mats,
    )
    blank_saved = [jnp.zeros(*item) for item in enc_shapes(images).values()]
    blank_latent = jnp.zeros((images * ROWS_E, DE), BF)
    latent, saved = lax.cond(
        encoding,
        lambda: (lambda out: (out[0], list(out[1:])))(
            encoder_forward(images, enc_copies, vis, pix, vecs, weights)
        ),
        lambda: (blank_latent, blank_saved),
    )
    arrived = shifted(latent, "section", 1)
    dlatent, loss, dmat_dec, dvec_dec = lax.cond(
        encoding,
        lambda: [
            blank_latent,
            jnp.zeros((8, 128), F32),
            jnp.zeros((DEC_TOTAL, 16, 128), BF),
            jnp.zeros(vecs.shape, F32),
        ],
        lambda: list(
            decoder_step(images, dec_copies, masked_total, arrived, places, pix, vecs, weights)
        ),
    )
    returned = shifted(dlatent, "section", -1)

    def encoder_side():
        dmats, dvec = encoder_backward(images, enc_copies, vis, vecs, returned, saved, weights)
        return flat_from_natural(dmats.astype(F32), ENC_MATS, total), dvec

    grad_mats, grad_vecs = lax.cond(
        encoding,
        encoder_side,
        lambda: (flat_from_natural(dmat_dec.astype(F32), DEC_MATS, total), dvec_dec),
    )
    summed_mats = lax.psum_scatter(grad_mats[None], "dp", scatter_dimension=1, tiled=True)
    summed_vecs = lax.psum_scatter(
        grad_vecs.reshape(1, -1), "dp", scatter_dimension=1, tiled=True
    )
    square = jnp.sum(summed_mats * summed_mats) + jnp.sum(summed_vecs * summed_vecs)
    square_all, loss_sum = lax.psum((square, loss[0, 0]), ("section", "dp"))
    grad_norm = jnp.sqrt(square_all)
    factor = jnp.minimum(1.0, 0.001 / (grad_norm + 1e-06))
    mat_new, mat_first_new, mat_second_new = adam_update(
        mat_master, mat_first, mat_second, factor * summed_mats, 0.05, 0.05
    )
    vec_new, vec_first_new, vec_second_new = adam_update(
        vec_master, vec_first, vec_second, factor * summed_vecs, 0.3, 0.0
    )
    return (
        loss_sum,
        grad_norm,
        mat_new,
        mat_first_new,
        mat_second_new,
        mat_new.astype(BF),
        vec_new,
        vec_first_new,
        vec_second_new,
        vec_new.astype(BF),
    )


def solution(mesh):
    split = P("section", "dp")
    return jax.shard_map(
        body,
        mesh=mesh,
        in_specs=(P("dp", None, None), P("dp", None), P("dp", None)) + (split,) * 6,
        out_specs=(P(), P()) + (split,) * 8,
        check_vma=False,
    )
```

time: 2770 us -> 2360 us (0.85)
  local copies, waits for them, and re-layouts: 437 us -> 181 us
  matrix products: 110 us -> 0 us
  waiting for transfers between devices: 1760 us -> 1670 us
  Pallas kernels: 0 us -> 75.3 us
    all_gather x0 -> x1, other arithmetic: none -> 325 us  [body(): mats = lax.all_gather(mat_master.astype(BF), 'dp', axis=1, tiled=True)[0]]
    ppermute x4 -> x2, waiting for transfers between devices: 301 us -> 140 us  [shifted(): lax.ppermute(value, axis, [(source, source + steps) for source in range(i...]
    convert_element_type x48 -> x0, local copies, waits for them, and re-layouts: 114 us -> none  [the longest x40 110 us: linear(): result = round_grad(product(values.reshape(-1, shape[-1]), weight))]
    add_any x6 -> x0, other arithmetic: 109 us -> none  [the longest x4 109 us: carve(): pieces.append(flat[offset:offset + count].reshape(shape))]
    dot_general x38 -> x0, matrix products: 105 us -> none  [the longest x28 90.7 us: linear(): result = round_grad(product(values.reshape(-1, shape[-1]), weight))]
    another operation x94 -> x6, local copies, waits for them, and re-layouts: 95.2 us -> 6.92 us
    pallas_call x0 -> x2, Pallas kernels: none -> 75.3 us  [the longest x1 42.1 us: encoder_backward(): pl.pallas_call(functools.partial(encoder_backward_kernel, images, copies)...]
    add x2 -> x0, other arithmetic: 72.7 us -> none  [the longest x1 70.9 us: body(): grad_mats = grad_mats + dmat_dec + dmat_enc]
  transfers between devices with their start and end apart: 8 -> 6, of which waited for: 6 -> 6; matrix products, arithmetic and copies ran while one was open for 18% -> 1% of each run, Pallas kernels for 0% -> 0%
where the time goes in v1:
time: 2360 us; the launch traced here: 2350 us
  waiting for transfers between devices  1670 us (71%)
  other arithmetic  354 us (15%)
  local copies, waits for them, and re-layouts  181 us (8%)
  Pallas kernels  75.3 us (3%)
  blocking collectives  40.5 us (2%)
    unnamed x7, waiting for transfers between devices  1370 us
    all_gather x1, other arithmetic, body(): mats = lax.all_gather(mat_master.astype(BF), 'dp', axis=1, tiled=True)[0]  325 us
    all_gather x1, waiting for transfers between devices, body(): mats = lax.all_gather(mat_master.astype(BF), 'dp', axis=1, tiled=True)[0]  156 us
    ppermute x2, waiting for transfers between devices, shifted(): lax.ppermute(value, axis, [(source, source + steps) for source in range(i...  140 us
  transfers between devices with their start and end apart: 6, of which 6 were waited for; matrix products, arithmetic and copies ran while one was open for 1% of the time, Pallas kernels for 0%

profile of v1, /device:TPU:0, one launch (start us, length us, event | category | flops | bytes accessed | tf_op | source)
XLA Modules:
  0.0 2351.0 jit_solution(1323611388548964331)
XLA Ops:
  7.3 1.0 convert_reduce_fusion
  8.2 1.3 fusion.14
  10.8 0.7 copy-done.4
  11.5 4.3 convert_element_type.41
  16.2 1.1 pad.22
  17.3 85.9 %all-reduce.11.cloned.1.call-done = bf16[162816]{0:T(1024)(128)(2,1)} async-done(((bf16[162816]{0:T(1024)(128)(2,1)}), bf16[162816]{0:T(1024)(128)(2,1)}) %all-reduce.11.cloned.1.call-update) | async-done | bytes 325648
  103.1 1.9 bitcast_convert_fusion
  105.0 155.9 %all-gather.2.cloned.1.call-done = bf16[1,7667712]{1,0:T(2,128)(2,1)} async-done(((bf16[1,479232]{1,0:T(2,128)(2,1)}), bf16[1,7667712]{1,0:T(2,128)(2,1)}) %all-gather.2.cloned.1.call-update) | async-done | bytes 15335440 | tf_op jit(solution)/shard_map/all_gather | solution.py:718
  260.9 324.7 %reduce.1 = bf16[7667712]{0:T(1024)(128)(2,1)} reduce(bf16[1,7667712]{1,0:T(2,128)(2,1)} %all-gather.2.cloned.1.call-done, bf16[]{:T(256)} %constant.98), dimensions={0}, to_apply=%all_gather.7.reduce_sub_computation | reduce | bytes 30670850 | tf_op jit(solution)/shard_map/all_gather | solution.py:718
  585.7 42.8 %conditional.4 = (bf16[3744,16,128]{2,1,0:T(8,128)(2,1)}) conditional(s32[]{:T(128)} %convert_element_type.37, bf16[7667712]{0:T(1024)(128)(2,1)} %reduce.1, bf16[7667712]{0:T(1024)(128)(2,1)} %reduce.1), branch_computations={%region_0.1_spmd, %region_1.2_spmd} | conditional | bytes 121503800 | solution.py:724
  585.8 2.8 fusion.9
  589.2 1.3 constant_dynamic-update-slice_fusion.10
  590.5 1.2 slice-done.2
  591.7 3.5 slice.160
  595.1 2.9 copy.68
  598.1 2.4 constant_dynamic-update-slice_fusion.9
  601.1 1.3 constant_dynamic-update-slice_fusion.8
  602.3 6.6 fusion.8
  608.9 1.3 copy.70
  610.2 2.6 constant_dynamic-update-slice_fusion.7
  612.8 8.9 slice.166
  621.7 4.2 copy.71
  625.9 2.6 constant_dynamic-update-slice_fusion.6
  628.4 34.2 %conditional.5 = ((bf16[256,768]{1,0:T(8,128)(2,1)}, bf16[256,768]{1,0:T(8,128)(2,1)}, f32[256,768]{1,0:T(8,128)S(1)}, bf16[256,768]{1,0:T(8,128)(2,1)}, bf16[25...) conditional(s32[]{:T(128)} %convert_element_type.37, () %tuple.36, ...), branch_computations={%region_2.3_spmd, %region_3.4_spmd} | conditional | bytes 10223742 | solution.py:732
  628.6 0.8 copy.85.vis
  629.4 33.2 %encoder_forward.1 = (bf16[256,768]{1,0:T(8,128)(2,1)}, bf16[256,768]{1,0:T(8,128)(2,1)}, f32[256,768]{1,0:T(8,128)S(1)}, bf16[256,768]{1,0:T(8,128)(2,1)}, bf16...) custom-call(s32[256,1]{1,0:T(8,128)} %copy.85.vis, ...), custom_call_target="tpu_custom_call" | custom-call | tf_op jit(solution)/shard_map/cond/branch_1_fun/encoder_forward/pallas_call | solution.py:446
  662.6 2.1 collective-permute-start
  664.7 8.6 collective-permute-done
  673.3 5.3 conditional.6
  673.3 0.8 broadcast.24
  674.1 3.7 broadcast.26
  677.8 0.9 broadcast.27
  678.7 1.3 collective-permute-start.1
  679.9 131.8 %collective-permute-done.1 = bf16[256,768]{1,0:T(8,128)(2,1)} collective-permute-done((bf16[256,768]{1,0:T(8,128)(2,1)}, bf16[256,768]{1,0:T(8,128)(2,1)}, u32[]{:S(2)}, u32[]{:S(2)}) %collective-permute-start.1) | collective-permute-done | bytes 393248 | tf_op jit(solution)/shard_map/ppermute | solution.py:697
  811.8 138.2 %conditional.7 = (f32[7667712]{0:T(1024)}, f32[1272,128]{1,0:T(8,128)}) conditional(s32[]{:T(128)} %convert_element_type.37, (bf16[1920,16,128]{2,1,0:T(8,128)(2,1)}, f32[1272,128]{1,0:T(8,128)}) %tuple.40, (s32[256,1]{0,1:T(1,128)S(1)}, f32[1272,128]{1,0:T(8,128)}, bf16[256,768]{1,0:T(8,128)(2,1)}, bf16[256,768]{1,0:T(8,128)(2,1)}, ...), branch_computations={%region_7.8_spmd, %region_8.9_spmd} | conditional | bytes 264243344 | solution.py:758
  820.5 0.8 copy.86.vis
  821.3 42.1 %encoder_backward.1 = (bf16[3744,16,128]{2,1,0:T(8,128)(2,1)}, f32[1272,128]{1,0:T(8,128)}) custom-call(s32[256,1]{1,0:T(8,128)} %copy.86.vis, f32[1272,128]{1,0:T(8,128)} %get-tuple-element.70.vec, bf16[256,768]{1,0:T(8,128)(2,1)} %get-tuple-element.71.dlatent, bf16[256,768]{1,0:T(8,128)(2,1)} %get-tuple-element.72.refs_0_, ...), custom_call_target="tpu_custom_call" | custom-call | tf_op jit(solution)/shard_map/cond/branch_1_fun/encoder_backward/pallas_call | solution.py:508
  863.4 3.3 fusion.13
  866.8 1.0 copy.102
  867.8 1.7 reshape.221
  869.4 3.2 constant_dynamic-update-slice_fusion.21
  872.6 2.6 slice.187
  875.2 6.8 copy.100
  882.0 8.9 reshape.223
  890.8 5.2 constant_dynamic-update-slice_fusion.20
  896.1 1.0 copy.101
  897.1 1.6 reshape.225
  898.7 3.3 constant_dynamic-update-slice_fusion.19
  902.0 6.9 fusion.12
  908.9 4.2 copy.82
  913.1 4.9 constant_dynamic-update-slice_fusion.18
  918.1 1.8 slice-done.4
  920.1 9.2 copy.99
  929.3 12.1 reshape.229
  941.4 8.4 constant_dynamic-update-slice_fusion.17
  950.0 37.3 %copy.89 = f32[1,162816]{0,1:T(8,128)} copy(f32[1,162816]{1,0:T(1,128)} %bitcast.135) | data formatting | bytes 1302528
  988.7 1.2 slice.179
  989.9 765.0 %reduce-scatter.5.cloned.1.call-done = f32[10176,1]{1,0:T(8,128)} async-done(((f32[162816,1]{1,0:T(8,128)}), f32[10176,1]{1,0:T(8,128)}) %reduce-scatter.5.cloned.1.call-update) | async-done | bytes 40720
  1754.9 3.3 copy.90
  1758.9 519.7 %all-reduce.13.cloned.1.call-done = f32[1,7667712]{1,0:T(1,128)} async-done(((f32[1,7667712]{1,0:T(1,128)}), f32[1,7667712]{1,0:T(1,128)}) %all-reduce.13.cloned.1.call-update) | async-done | bytes 30670864
  2278.6 5.6 multiply_reduce_fusion
  2285.5 40.5 %all-reduce.7 = (f32[]{:T(128)}, f32[]{:T(128)}) all-reduce(f32[]{:T(128)} %bitcast.70, f32[]{:T(128)S(6)} %add.54), channel_id=1, replica_groups=mesh['section'=2,'dp'=16] {'section','dp'}, use_global_device_ids=true, to_apply=%region_6.7 | all-reduce | flops 2 | bytes 16 | tf_op jit(solution)/shard_map/psum | solution.py:768
  2326.7 1.0 fusion.2
  2327.7 15.2 fusion.4
  (47 shorter events, 3.6 us)
Async XLA Ops:
  7.2 8.7 copy-start.10
  7.2 8.8 copy-start.5
  7.2 96.0 %all-reduce.11.cloned.1.call-start = ((), (), s32[]{:S(2)}) async-start(), calls=%async_computation.2 | async-start | bytes 651264
  10.7 0.7 copy-start.4
  11.5 249.4 %all-gather.2.cloned.1.call-start = ((), (), s32[]{:S(2)}) async-start(), calls=%async_computation.1 | async-start | bytes 32587776 | tf_op jit(solution)/shard_map/all_gather | solution.py:718
  15.9 1739.1 %reduce-scatter.5.cloned.1.call-start = ((), (), s32[]{:S(2)}) async-start(), calls=%async_computation.3 | async-start | bytes 88571904
  589.2 2.4 slice-start.2
  598.1 2.4 copy-start.3
  628.4 44.9 %copy-start.9 = (s32[4,196]{1,0:T(4,128)S(1)}, s32[4,196]{1,0:T(4,128)}, u32[]{:S(2)}) copy-start(s32[4,196]{1,0:T(4,128)} %param.19) | copy-start | bytes 9412
  662.6 10.7 collective-permute-start
  678.6 133.1 %copy-start.11 = (f32[8,128]{1,0:T(8,128)}, f32[8,128]{1,0:T(8,128)S(1)}, u32[]{:S(2)}) copy-start(f32[8,128]{1,0:T(8,128)S(1)} %get-tuple-element.113) | copy-start | bytes 12292
  678.7 133.1 %collective-permute-start.1 = (bf16[256,768]{1,0:T(8,128)(2,1)}, bf16[256,768]{1,0:T(8,128)(2,1)}, u32[]{:S(2)}, u32[]{:S(2)}) collective-permute-start(bf16[256,768]{1,0:T(8,128)(2,1)} %get-tuple-element.116), channel_id=1, source_target_pairs={{16,0},{17,1},{18,2},{19,3},{20,4},{21,5},{22,6},{23,7},{24,8},{25... | collective-permute-start | bytes 1179656 | tf_op jit(solution)/shard_map/ppermute | solution.py:697
  890.8 5.2 copy-start
  913.1 5.0 slice-start.3
  913.1 6.8 slice-start.4
  913.1 7.0 slice-start.5
  987.3 1291.3 %all-reduce.13.cloned.1.call-start = ((), (), s32[]{:S(2)}) async-start(), calls=%async_computation.4 | async-start | bytes 61341696
  987.9 1338.8 %copy-start.6 = (f32[1,10176]{1,0:T(1,128)S(1)}, f32[1,10176]{1,0:T(1,128)}, u32[]{:S(2)}) copy-start(f32[1,10176]{1,0:T(1,128)} %param.23) | copy-start | bytes 122116
  987.9 1338.8 %copy-start.7 = (f32[1,10176]{1,0:T(1,128)S(1)}, f32[1,10176]{1,0:T(1,128)}, u32[]{:S(2)}) copy-start(f32[1,10176]{1,0:T(1,128)} %param.24) | copy-start | bytes 122116
  987.9 1338.8 %copy-start.8 = (f32[1,10176]{1,0:T(1,128)S(1)}, f32[1,10176]{1,0:T(1,128)}, u32[]{:S(2)}) copy-start(f32[1,10176]{1,0:T(1,128)} %param.25) | copy-start | bytes 122116
  987.9 1339.8 %copy-start.1 = (f32[1,479232]{1,0:T(1,128)S(1)}, f32[1,479232]{1,0:T(1,128)}, u32[]{:S(2)}) copy-start(f32[1,479232]{1,0:T(1,128)} %param.20) | copy-start | bytes 5750788
Sparse Core Ops, SparseCore 0:
  12.0 91.1 all-reduce.10
  105.4 155.4 all-gather.1
  987.4 767.4 reduce-scatter.4
  1758.9 519.6 all-reduce.12

commit v2 on v1

--- a/solution.py
+++ b/solution.py
@@ -360,18 +360,75 @@
             setattr(self, name, ref)
 
 
-def load_mats(source, kept, sem, copies):
+class Layout:
+    def __init__(self, shape, moves, shared):
+        self.shape, self.moves, self.shared = shape, moves, shared
+
+
+def plain_layout(total):
+    return Layout((total, 16, 128), [(lambda ref: ref, 0, total)], [])
+
+
+def slot_layout(plan, shape):
+    moves, shared, done = [], [], 0
+    for device, (first, count, _) in enumerate(plan):
+        skip = max(0, done - first)
+        if skip and count:
+            shared.append((lambda ref, d=device, n=skip: ref.at[d, pl.ds(0, n)], first, skip))
+        if count:
+            moves.append(
+                (
+                    lambda ref, d=device, a=skip, n=count - skip: ref.at[d, pl.ds(a, n)],
+                    first + skip,
+                    count - skip,
+                )
+            )
+        done = first + count
+    return Layout(shape, moves, shared)
+
+
+def whole_slots(plan, shape):
+    moves = [
+        (lambda ref, d=device, n=count: ref.at[d, pl.ds(0, n)], first, count)
+        for device, (first, count, _) in enumerate(plan)
+        if count
+    ]
+    return Layout(shape, moves, [])
+
+
+SHARED = 24
+
+
+def load_mats(source, kept, side, sem, layout):
     started = []
-    for index, (pick, start, count) in enumerate(copies):
+    for index, (pick, start, count) in enumerate(layout.moves):
         copy = pltpu.make_async_copy(pick(source), kept.at[pl.ds(start, count)], sem.at[index])
         copy.start()
         started.append(copy)
+    for index, (pick, start, count) in enumerate(layout.shared):
+        copy = pltpu.make_async_copy(
+            pick(source),
+            side.at[index, pl.ds(0, count)],
+            sem.at[len(layout.moves) + index],
+        )
+        copy.start()
+        started.append(copy)
     return started
 
 
-def plain_copies(base, tiles):
+def finish_mats(started, kept, side, layout):
+    for copy in started:
+        copy.wait()
+    for index, (_, start, count) in enumerate(layout.shared):
+        there = pl.ds(start, count)
+        both = kept[there].astype(F32) + side[index, 0:count].astype(F32)
+        kept[there] = both.astype(BF)
+
+
+def load_scratch(layout):
     return [
-        ((lambda ref, a=a, c=c: ref.at[pl.ds(a, c)]), a, c) for a, c in zip(base, tiles)
+        pltpu.VMEM((max(1, len(layout.shared)), SHARED, 16, 128), BF),
+        pltpu.SemaphoreType.DMA((len(layout.moves) + len(layout.shared),)),
     ]
 
 
@@ -410,11 +467,11 @@
     return vec[pl.ds(start + j, PATCHES, stride=blocks), :]
 
 
-def encoder_forward_kernel(images, copies, vis, pix, vec, weights, *refs):
+def encoder_forward_kernel(images, layout, vis, pix, vec, weights, *refs):
     latent = refs[0]
     s = Bag(ENC_KEEP, refs[1 : 1 + len(ENC_KEEP)])
-    kept, posit, sem = refs[1 + len(ENC_KEEP) :]
-    started = load_mats(weights, kept, sem, copies)
+    kept, posit, side, sem = refs[1 + len(ENC_KEEP) :]
+    started = load_mats(weights, kept, side, sem, layout)
     rows = images * ROWS_E
     mats = [Mat(kept, b, shape) for b, shape in zip(ENC_BASE, ENC_MATS)]
     posit[...] = jnp.zeros_like(posit)
@@ -425,8 +482,7 @@
         hot = visible_rows(vis[where, :], ROWS_D)
         s.pick[where, :] = dot(hot, pix[i]).astype(BF)
         s.x0[where, :] = dot(hot, posit[...].astype(BF)) + row_of(vec, EV[0], DE)
-    for copy in started:
-        copy.wait()
+    finish_mats(started, kept, side, layout)
 
     def embed_step(j, carry):
         s.x0[:, lanes(j)] += dot(s.pick[...], mats[0].cols(j))
@@ -439,12 +495,12 @@
     norm_rows(s.x1, latent, vec, EV[10], EV[11], DE, s.x2, EV[9])
 
 
-def encoder_forward(images, copies, vis, pix, vec, weights):
+def encoder_forward(images, layout, vis, pix, vec, weights):
     shapes = enc_shapes(images)
     rows = images * ROWS_E
     vm = pl.BlockSpec(memory_space=pltpu.VMEM)
     return pl.pallas_call(
-        functools.partial(encoder_forward_kernel, images, copies),
+        functools.partial(encoder_forward_kernel, images, layout),
         out_shape=[jax.ShapeDtypeStruct((rows, DE), BF)]
         + [jax.ShapeDtypeStruct(*shapes[name]) for name in ENC_KEEP],
         in_specs=[vm, vm, vm, pl.BlockSpec(memory_space=pl.ANY)],
@@ -452,28 +508,29 @@
         scratch_shapes=[
             pltpu.VMEM((ENC_TOTAL, 16, 128), BF),
             pltpu.VMEM((ROWS_D, DE), F32),
-            pltpu.SemaphoreType.DMA((len(copies),)),
-        ],
+        ]
+        + load_scratch(layout),
         name="encoder_forward",
         compiler_params=pltpu.CompilerParams(vmem_limit_bytes=VMEM_LIMIT),
     )(vis, pix, vec, weights)
 
 
-def store_mats(kept, out, sem, index, base, count):
-    copy = pltpu.make_async_copy(
-        kept.at[pl.ds(base, count)], out.at[pl.ds(base, count)], sem.at[index]
-    )
-    copy.start()
-    return copy
-
-
-def encoder_backward_kernel(images, copies, vis, vec, dlatent, *refs):
+def store_mats(kept, out, sem, layout):
+    started = []
+    for index, (pick, start, count) in enumerate(layout.moves):
+        copy = pltpu.make_async_copy(kept.at[pl.ds(start, count)], pick(out), sem.at[index])
+        copy.start()
+        started.append(copy)
+    return started
+
+
+def encoder_backward_kernel(images, layout, out_layout, vis, vec, dlatent, *refs):
     s = Bag(ENC_KEEP, refs[: len(ENC_KEEP)])
     weights, dmats, dvec = refs[len(ENC_KEEP) : len(ENC_KEEP) + 3]
-    kept, dkept, s.dx, s.dxb, s.dn, s.datt, s.dqkv, s.flip, sem, out_sem = refs[
+    kept, dkept, s.dx, s.dxb, s.dn, s.datt, s.dqkv, s.flip, out_sem, side, sem = refs[
         len(ENC_KEEP) + 3 :
     ]
-    started = load_mats(weights, kept, sem, copies)
+    started = load_mats(weights, kept, side, sem, layout)
     rows = images * ROWS_E
     mats = [Mat(kept, b, shape) for b, shape in zip(ENC_BASE, ENC_MATS)]
     grads = [Mat(dkept, b, shape) for b, shape in zip(ENC_BASE, ENC_MATS)]
@@ -481,8 +538,7 @@
     norm_back_rows(
         s.x2, dlatent, s.dx, s.dxb, vec, dvec, EV[10], EV[11], DE, EV[9], False
     )
-    for copy in started:
-        copy.wait()
+    finish_mats(started, kept, side, layout)
     block_backward(
         s, mats[1:5], grads[1:5], vec, dvec, ENC_AT, DE, FE, DE // HE, rows, 1
     )
@@ -493,22 +549,23 @@
         return carry
 
     loop(DE // 256, embed_step)
-    out = store_mats(dkept, dmats, out_sem, 0, 0, ENC_TOTAL)
+    stores = store_mats(dkept, dmats, out_sem, out_layout)
     hot = visible_rows(vis[...], ROWS_D)
     for j in range(DE // 128):
         value = t_dot(hot, s.dxb[:, j * 128 : (j + 1) * 128])
         dvec[pl.ds(EV[1] + j, PATCHES, stride=DE // 128), :] = value[0:PATCHES]
-    out.wait()
-
-
-def encoder_backward(images, copies, vis, vec, dlatent, saved, weights):
+    for copy in stores:
+        copy.wait()
+
+
+def encoder_backward(images, layout, out_layout, vis, vec, dlatent, saved, weights):
     rows = images * ROWS_E
     vm = pl.BlockSpec(memory_space=pltpu.VMEM)
     hbm = pl.BlockSpec(memory_space=pl.ANY)
     return pl.pallas_call(
-        functools.partial(encoder_backward_kernel, images, copies),
+        functools.partial(encoder_backward_kernel, images, layout, out_layout),
         out_shape=[
-            jax.ShapeDtypeStruct((ENC_TOTAL, 16, 128), BF),
+            jax.ShapeDtypeStruct(out_layout.shape, BF),
             jax.ShapeDtypeStruct(vec.shape, F32),
         ],
         in_specs=[vm] * (3 + len(ENC_KEEP)) + [hbm],
@@ -522,32 +579,31 @@
             pltpu.VMEM((rows, DE), BF),
             pltpu.VMEM((rows, 3 * DE), BF),
             pltpu.VMEM((DE, rows), BF),
-            pltpu.SemaphoreType.DMA((len(copies),)),
-            pltpu.SemaphoreType.DMA((1,)),
-        ],
+            pltpu.SemaphoreType.DMA((len(out_layout.moves),)),
+        ]
+        + load_scratch(layout),
         name="encoder_backward",
         compiler_params=pltpu.CompilerParams(vmem_limit_bytes=VMEM_LIMIT),
     )(vis, vec, dlatent, *saved, weights)
 
 
-def decoder_kernel(images, copies, masked_total, latent, places, pix, vec, weights, *refs):
+def decoder_kernel(images, layout, out_layout, masked_total, latent, places, pix, vec, weights, *refs):
     dlatent, loss, dmats, dvec = refs[:4]
     s = Bag(
         ["x0", "x1", "x2", "n1", "n2", "qkv", "probs", "att", "h", "dx", "dxb", "dn", "dqkv", "flip"],
         refs[4:18],
     )
-    kept, dkept, posit, dguess, sem, out_sem = refs[18:]
+    kept, dkept, posit, dguess, out_sem, side, sem = refs[18:]
     s.datt = s.n2
     rows = images * ROWS_D
     mats = [Mat(kept, b, shape) for b, shape in zip(DEC_BASE, DEC_MATS)]
     grads = [Mat(dkept, b, shape) for b, shape in zip(DEC_BASE, DEC_MATS)]
-    started = load_mats(weights, kept, sem, copies)
+    started = load_mats(weights, kept, side, sem, layout)
     posit[...] = jnp.zeros_like(posit)
     for j in range(DD // 128):
         posit[0:PATCHES, j * 128 : (j + 1) * 128] = position_column(vec, DV[2], DD // 128, j)
     dvec[DV[13] + PIX // 128 :, :] = jnp.zeros_like(dvec[DV[13] + PIX // 128 :, :])
-    for copy in started:
-        copy.wait()
+    finish_mats(started, kept, side, layout)
     for i in range(images):
         part = pl.ds(i * ROWS_E, ROWS_E)
         where = pl.ds(i * ROWS_D, ROWS_D)
@@ -625,21 +681,21 @@
     for j in range(DE // 256):
         grads[0].put_band(j, t_dot(latent[:, j * 256 : (j + 1) * 256], back))
         dlatent[:, j * 256 : (j + 1) * 256] = dot_t(back, mats[0].band(j)).astype(BF)
-    out = store_mats(dkept, dmats, out_sem, 0, 0, DEC_TOTAL)
-    out.wait()
-
-
-def decoder_step(images, copies, masked_total, latent, places, pix, vec, weights):
+    for copy in store_mats(dkept, dmats, out_sem, out_layout):
+        copy.wait()
+
+
+def decoder_step(images, layout, out_layout, masked_total, latent, places, pix, vec, weights):
     rows = images * ROWS_D
     vm = pl.BlockSpec(memory_space=pltpu.VMEM)
     hbm = pl.BlockSpec(memory_space=pl.ANY)
     probs = images * HD
     return pl.pallas_call(
-        functools.partial(decoder_kernel, images, copies, masked_total),
+        functools.partial(decoder_kernel, images, layout, out_layout, masked_total),
         out_shape=[
             jax.ShapeDtypeStruct((images * ROWS_E, DE), BF),
             jax.ShapeDtypeStruct((8, 128), F32),
-            jax.ShapeDtypeStruct((DEC_TOTAL, 16, 128), BF),
+            jax.ShapeDtypeStruct(out_layout.shape, BF),
             jax.ShapeDtypeStruct(vec.shape, F32),
         ],
         in_specs=[vm, vm, vm, vm, hbm],
@@ -663,9 +719,9 @@
             pltpu.VMEM((DEC_TOTAL, 16, 128), BF),
             pltpu.VMEM((ROWS_D, DD), F32),
             pltpu.VMEM((rows, PIX), BF),
-            pltpu.SemaphoreType.DMA((len(copies),)),
-            pltpu.SemaphoreType.DMA((1,)),
-        ],
+            pltpu.SemaphoreType.DMA((len(out_layout.moves),)),
+        ]
+        + load_scratch(layout),
         name="decoder_step",
         compiler_params=pltpu.CompilerParams(vmem_limit_bytes=VMEM_LIMIT),
     )(latent, places, pix, vec, weights)
@@ -691,10 +747,517 @@
     return jnp.pad(flat, (0, total - flat.shape[0]))
 
 
-def shifted(value, axis, steps):
-    count = lax.axis_size(axis)
-    initial, last = (max(0, -steps), min(count, count - steps))
-    return lax.ppermute(value, axis, [(source, source + steps) for source in range(initial, last)])
+MESH = pl.DeviceIdType.MESH
+DEPTH, WIDTH = 4, 2
+SLOT_M, SLOT_V = 264, 5
+SLOT = SLOT_M + SLOT_V
+PART = ((0, 224), (224, SLOT - 224))
+MARGIN = 384
+
+
+def shard_plan(shapes, total, devices):
+    lines = total // devices // 128
+    plans = []
+    for device in range(devices):
+        low, high = device * lines, (device + 1) * lines
+        first, count, pieces = 0, 0, []
+        line, tile = 0, 0
+        for rows, columns in shapes:
+            blocks = columns // 128
+            begin, end = max(low, line), min(high, line + rows * blocks)
+            if begin < end:
+                top, bottom = (begin - line) // blocks, (end - line) // blocks
+                assert top * blocks == begin - line and bottom * blocks == end - line
+                up, down = top // 16, -(-bottom // 16)
+                if not pieces:
+                    first = tile + up * blocks
+                pieces.append((blocks, line + up * 16 * blocks - low, down - up, count))
+                count += (down - up) * blocks
+            line += rows * blocks
+            tile += rows * blocks // 16
+        plans.append((first, count, pieces))
+    return plans
+
+
+def devices_around(z, y, c, s):
+    at = lambda zz, yy, cc: (s, zz * 4 + yy * 2 + cc)
+    around = {"side": at(z, 1 - y, c), "core": at(z, y, 1 - c)}
+    if z + 1 < DEPTH:
+        around["up"] = at(z + 1, y, c)
+    if z > 0:
+        around["down"] = at(z - 1, y, c)
+    return around
+
+
+def greet(around):
+    barrier = pltpu.get_barrier_semaphore()
+    for target in around.values():
+        pl.semaphore_signal(barrier, inc=1, device_id=target, device_id_type=MESH)
+    pl.semaphore_wait(barrier, len(around))
+
+
+def place():
+    d = lax.axis_index("dp")
+    return lax.axis_index("section"), d // 4, (d // 2) % 2, d % 2
+
+
+def for_each_depth(run):
+    s, z_now, y, c = place()
+    for z in range(DEPTH):
+        pl.when(z_now == z)(functools.partial(run, s, z, y, c))
+
+
+def gather_kernel(own, out, send, recv, local):
+    def run(s, z, y, c):
+        around = devices_around(z, y, c, s)
+        greet(around)
+        slot = lambda zz, yy, cc: zz * 4 + yy * 2 + cc
+        sent = []
+
+        def at(ref, index, part):
+            start, count = PART[part]
+            return ref.at[index, pl.ds(start, count)]
+
+        def push(index, part, targets, mine=False):
+            start, count = PART[part]
+            for name in targets:
+                if name not in around:
+                    continue
+                copy = pltpu.make_async_remote_copy(
+                    own.at[pl.ds(start, count)] if mine else at(out, index, part),
+                    at(out, index, part),
+                    send.at[len(sent)],
+                    recv.at[index, part],
+                    device_id=around[name],
+                    device_id_type=MESH,
+                )
+                copy.start()
+                sent.append(copy)
+
+        def arrive(index, part):
+            pltpu.make_async_remote_copy(
+                at(out, index, part),
+                at(out, index, part),
+                send.at[0],
+                recv.at[index, part],
+                device_id=around["core"],
+                device_id_type=MESH,
+            ).wait_recv()
+
+        me = slot(z, y, c)
+        push(me, 1, ["side"], True)
+        push(me, 0, ["up", "down", "side"], True)
+        push(me, 1, ["up", "down"], True)
+        push(me, 0, ["core"], True)
+        push(me, 1, ["core"], True)
+        keep = pltpu.make_async_copy(own, out.at[me], local)
+        keep.start()
+        arrive(slot(z, 1 - y, c), 1)
+        push(slot(z, 1 - y, c), 1, ["up", "down", "core"])
+        for k in range(1, DEPTH):
+            for zz in (z - k, z + k):
+                if 0 <= zz < DEPTH:
+                    onward = "up" if zz < z else "down"
+                    arrive(slot(zz, y, c), 0)
+                    push(slot(zz, y, c), 0, [onward, "side", "core"])
+                    for yy in (y, 1 - y):
+                        arrive(slot(zz, yy, c), 1)
+                        push(slot(zz, yy, c), 1, [onward, "core"])
+            for zz in sorted({z - k + 1, z + k - 1}):
+                if 0 <= zz < DEPTH:
+                    arrive(slot(zz, 1 - y, c), 0)
+                    push(slot(zz, 1 - y, c), 0, ["core"])
+        for zz in (z - DEPTH + 1, z + DEPTH - 1):
+            if 0 <= zz < DEPTH:
+                arrive(slot(zz, 1 - y, c), 0)
+                push(slot(zz, 1 - y, c), 0, ["core"])
+        for zz in range(DEPTH):
+            for yy in range(WIDTH):
+                for part in range(2):
+                    arrive(slot(zz, yy, 1 - c), part)
+        keep.wait()
+        for copy in sent:
+            copy.wait_send()
+
+    for_each_depth(run)
+
+
+def gather_slots(own):
+    hbm = pl.BlockSpec(memory_space=pl.ANY)
+    return pl.pallas_call(
+        gather_kernel,
+        out_shape=jax.ShapeDtypeStruct((16, SLOT, 16, 128), BF),
+        in_specs=[hbm],
+        out_specs=hbm,
+        scratch_shapes=[
+            pltpu.SemaphoreType.DMA((48,)),
+            pltpu.SemaphoreType.DMA((16, 2)),
+            pltpu.SemaphoreType.DMA,
+        ],
+        name="gather_slots",
+        compiler_params=pltpu.CompilerParams(collective_id=0, has_side_effects=True),
+    )(own)
+
+
+def send_order(z):
+    order = []
+    for k in range(DEPTH - 1, -1, -1):
+        for zz in (z + k, z - k):
+            if 0 <= zz < DEPTH and zz not in order:
+                order.append(zz)
+    return order
+
+
+def add_tiles(target, sources, start, count):
+    step = 8
+
+    def some(base, size):
+        value = sources[0][pl.ds(base, size)].astype(F32)
+        for source in sources[1:]:
+            value = value + source[pl.ds(base, size)].astype(F32)
+        target[pl.ds(base, size)] = value.astype(target.dtype)
+
+    def body(i, carry):
+        some(start + i * step, step)
+        return carry
+
+    lax.fori_loop(0, count // step, body, 0)
+    if count % step:
+        some(start + count // step * step, count % step)
+
+
+class Shifted:
+    def __init__(self, ref, start):
+        self.ref, self.start = ref, start
+
+    def __getitem__(self, index):
+        return self.ref[pl.ds(index.start - self.start, index.size)]
+
+
+def scatter_kernel(mats, vecs, out, held, core_in, side_a, side_b, z_a, z_b, load, send, r_core, r_side, r_z):
+    def run(s, z, y, c):
+        around = devices_around(z, y, c, s)
+        loads = {}
+        order = send_order(z)
+        slot = lambda zz, yy, cc: zz * 4 + yy * 2 + cc
+        n = 0
+        for cc in (1 - c, c):
+            for zz in order:
+                for yy in (1 - y, y):
+                    index = slot(zz, yy, cc)
+                    pair = (
+                        pltpu.make_async_copy(
+                            mats.at[index], held.at[index, pl.ds(0, SLOT_M)], load.at[n]
+                        ),
+                        pltpu.make_async_copy(
+                            vecs.at[index], held.at[index, pl.ds(SLOT_M, SLOT_V)], load.at[16 + n]
+                        ),
+                    )
+                    for copy in pair:
+                        copy.start()
+                    loads[n] = pair
+                    n += 1
+        greet(around)
+        sent = []
+
+        def remote(source, target, sem, name):
+            return pltpu.make_async_remote_copy(
+                source,
+                target,
+                send.at[len(sent)],
+                sem,
+                device_id=around[name],
+                device_id_type=MESH,
+            )
+
+        def push(source, target, sem, name):
+            copy = remote(source, target, sem, name)
+            copy.start()
+            sent.append(copy)
+
+        def cut(index, part):
+            start, count = PART[part]
+            return held.at[index, pl.ds(start, count)]
+
+        def arrive(target, sem):
+            pltpu.make_async_remote_copy(
+                target, target, send.at[0], sem, device_id=around["core"], device_id_type=MESH
+            ).wait_recv()
+
+        n = 0
+        for zz in order:
+            for yy in (1 - y, y):
+                for copy in loads[n]:
+                    copy.wait()
+                push(
+                    held.at[slot(zz, yy, 1 - c)],
+                    core_in.at[zz * 2 + yy],
+                    r_core.at[zz * 2 + yy],
+                    "core",
+                )
+                n += 1
+        ready = set()
+
+        def prepare(zz, flip):
+            if (zz, flip) in ready:
+                return
+            ready.add((zz, flip))
+            yy = 1 - y if flip else y
+            for copy in loads[8 + order.index(zz) * 2 + (0 if flip else 1)]:
+                copy.wait()
+            arrive(core_in.at[zz * 2 + yy], r_core.at[zz * 2 + yy])
+
+        def z_in(part, way, zz, yy):
+            if part == 0:
+                return z_a.at[way, zz], r_z.at[way, zz, 2]
+            return z_b.at[way, zz, yy], r_z.at[way, zz, yy]
+
+        def side_sources(zz, yy):
+            return [held.at[slot(zz, yy, c)], core_in.at[zz * 2 + yy]]
+
+        for zz in order:
+            prepare(zz, True)
+            index = slot(zz, 1 - y, c)
+            add_tiles(held.at[index], side_sources(zz, 1 - y), *PART[0])
+            push(cut(index, 0), side_a.at[zz], r_side.at[zz], "side")
+
+        def along(part, zz, flip):
+            yy = 1 - y if flip else y
+            prepare(zz, flip)
+            index = slot(zz, yy, c)
+            way, name, first = (0, "up", 0) if zz > z else (1, "down", DEPTH - 1)
+            sources = side_sources(zz, yy)
+            if part == 0:
+                arrive(side_a.at[zz], r_side.at[zz])
+                sources.append(side_a.at[zz])
+            if z != first:
+                ref, sem = z_in(part, way, zz, yy)
+                arrive(ref, sem)
+                sources.append(ref if part == 0 else Shifted(ref, PART[1][0]))
+            add_tiles(held.at[index], sources, *PART[part])
+            ref, sem = z_in(part, way, zz, yy)
+            push(cut(index, part), ref, sem, name)
+
+        def gathered(part, yy):
+            found = []
+            for way, here in ((0, z > 0), (1, z < DEPTH - 1)):
+                if here:
+                    ref, sem = z_in(part, way, z, yy)
+                    arrive(ref, sem)
+                    found.append(ref if part == 0 else Shifted(ref, PART[1][0]))
+            return found
+
+        for zz in order[:-1]:
+            along(1, zz, True)
+            along(1, zz, False)
+        prepare(z, False)
+        index = slot(z, 1 - y, c)
+        add_tiles(held.at[index], side_sources(z, 1 - y) + gathered(1, 1 - y), *PART[1])
+        push(cut(index, 1), side_b, r_side.at[DEPTH], "side")
+        for zz in order[:-1]:
+            along(0, zz, False)
+        arrive(side_b, r_side.at[DEPTH])
+        add_tiles(
+            out,
+            side_sources(z, y) + gathered(1, y) + [Shifted(side_b, PART[1][0])],
+            *PART[1],
+        )
+        arrive(side_a.at[z], r_side.at[z])
+        add_tiles(out, side_sources(z, y) + [side_a.at[z]] + gathered(0, y), *PART[0])
+        for copy in sent:
+            copy.wait_send()
+
+    for_each_depth(run)
+
+
+def scatter_slots(mats, vecs):
+    hbm = pl.BlockSpec(memory_space=pl.ANY)
+    tail = PART[1][1]
+    return pl.pallas_call(
+        scatter_kernel,
+        out_shape=jax.ShapeDtypeStruct((SLOT, 16, 128), F32),
+        in_specs=[hbm, hbm],
+        out_specs=pl.BlockSpec(memory_space=pltpu.VMEM),
+        scratch_shapes=[
+            pltpu.VMEM((16, SLOT, 16, 128), BF),
+            pltpu.VMEM((8, SLOT, 16, 128), BF),
+            pltpu.VMEM((DEPTH, PART[0][1], 16, 128), BF),
+            pltpu.VMEM((tail, 16, 128), BF),
+            pltpu.VMEM((2, DEPTH, PART[0][1], 16, 128), BF),
+            pltpu.VMEM((2, DEPTH, 2, tail, 16, 128), BF),
+            pltpu.SemaphoreType.DMA((32,)),
+            pltpu.SemaphoreType.DMA((24,)),
+            pltpu.SemaphoreType.DMA((8,)),
+            pltpu.SemaphoreType.DMA((DEPTH + 1,)),
+            pltpu.SemaphoreType.DMA((2, DEPTH, 3)),
+        ],
+        name="scatter_slots",
+        compiler_params=pltpu.CompilerParams(
+            collective_id=1, has_side_effects=True, vmem_limit_bytes=VMEM_LIMIT
+        ),
+    )(mats, vecs)
+
+
+def piece_table(lines):
+    plans = [shard_plan(m, lines * 128 * 16, 16) for m in (ENC_MATS, DEC_MATS)]
+    most = max(len(pieces) for plan in plans for _, _, pieces in plan)
+    table = [
+        [[list(p) for p in pieces] + [[0] * 4] * (most - len(pieces)) for _, _, pieces in plan]
+        for plan in plans
+    ]
+    widths = sorted({p[0] for plan in plans for _, _, pieces in plan for p in pieces})
+    return plans, table, widths
+
+
+def each_tile(table, widths, run):
+    for piece in range(table.shape[0]):
+        for width in widths:
+
+            @pl.when(table[piece, 0] == width)
+            def _(piece=piece, width=width):
+                def step(i, carry):
+                    for j in range(width):
+                        line = MARGIN + table[piece, 1] + i * (16 * width) + j
+                        run(line, width, table[piece, 3] + i * width + j)
+                    return carry
+
+                lax.fori_loop(0, table[piece, 2], step, 0)
+
+
+def pack_kernel(widths, table, mat, vec, out, lines, sem):
+    count = mat.shape[0]
+    copy = pltpu.make_async_copy(mat, lines.at[pl.ds(MARGIN, count)], sem)
+    copy.start()
+    lines[0:MARGIN, :] = jnp.zeros((MARGIN, 128), F32)
+    lines[MARGIN + count :, :] = jnp.zeros((MARGIN, 128), F32)
+    out[SLOT_M:] = vec[...].astype(BF).reshape(SLOT_V, 16, 128)
+    copy.wait()
+
+    def run(line, width, tile):
+        out[tile] = lines[pl.ds(line, 16, stride=width), :].astype(BF)
+
+    each_tile(table, widths, run)
+
+
+def pack(table, widths, mat, vec):
+    vm = pl.BlockSpec(memory_space=pltpu.VMEM)
+    return pl.pallas_call(
+        functools.partial(pack_kernel, widths),
+        out_shape=jax.ShapeDtypeStruct((SLOT, 16, 128), BF),
+        in_specs=[
+            pl.BlockSpec(memory_space=pltpu.SMEM),
+            pl.BlockSpec(memory_space=pl.ANY),
+            vm,
+        ],
+        out_specs=vm,
+        scratch_shapes=[
+            pltpu.VMEM((mat.shape[0] + 2 * MARGIN, 128), F32),
+            pltpu.SemaphoreType.DMA,
+        ],
+        name="pack",
+        compiler_params=pltpu.CompilerParams(vmem_limit_bytes=VMEM_LIMIT),
+    )(table, mat, vec)
+
+
+def unpack_kernel(widths, table, total, loss, grad, vec, part, lines):
+    count = grad.shape[0]
+    lines[...] = jnp.zeros_like(lines)
+
+    def run(line, width, tile):
+        lines[pl.ds(line, 16, stride=width), :] = total[tile]
+
+    each_tile(table, widths, run)
+    vec[...] = total[SLOT_M:].reshape(SLOT_V * 16, 128)
+
+    def square(i, carry):
+        rows = pl.ds(pl.multiple_of(i * 96, 96), 96)
+        value = lines[pl.ds(pl.multiple_of(MARGIN + i * 96, 96), 96), :]
+        grad[rows, :] = value
+        return carry + fold(value * value)
+
+    carry = fold(vec[...] * vec[...])
+    carry = lax.fori_loop(0, count // 96, square, carry)
+    row = lax.broadcasted_iota(jnp.int32, (8, 128), 0)
+    part[...] = jnp.where(row == 0, jnp.sum(carry), loss[...])
+
+
+def unpack(table, widths, count, total, loss):
+    vm = pl.BlockSpec(memory_space=pltpu.VMEM)
+    return pl.pallas_call(
+        functools.partial(unpack_kernel, widths),
+        out_shape=[
+            jax.ShapeDtypeStruct((count, 128), F32),
+            jax.ShapeDtypeStruct((SLOT_V * 16, 128), F32),
+            jax.ShapeDtypeStruct((8, 128), F32),
+        ],
+        in_specs=[pl.BlockSpec(memory_space=pltpu.SMEM), vm, vm],
+        out_specs=[vm, vm, vm],
+        scratch_shapes=[pltpu.VMEM((count + 2 * MARGIN, 128), F32)],
+        name="unpack",
+        compiler_params=pltpu.CompilerParams(vmem_limit_bytes=VMEM_LIMIT),
+    )(table, total, loss)
+
+
+def total_kernel(part, out, parts, send, recv):
+    s, d = lax.axis_index("section"), lax.axis_index("dp")
+    count = parts.shape[0]
+    me = s * 16 + d
+    barrier = pltpu.get_barrier_semaphore()
+
+    def target(k):
+        other = lax.rem(me + k, count)
+        return other, (other // 16, lax.rem(other, 16))
+
+    for k in range(1, count):
+        pl.semaphore_signal(barrier, inc=1, device_id=target(k)[1], device_id_type=MESH)
+    pl.semaphore_wait(barrier, count - 1)
+    sent = []
+    for k in range(1, count):
+        copy = pltpu.make_async_remote_copy(
+            part,
+            parts.at[me],
+            send.at[k],
+            recv.at[me],
+            device_id=target(k)[1],
+            device_id_type=MESH,
+        )
+        copy.start()
+        sent.append(copy)
+    parts[me] = part[...]
+    for k in range(1, count):
+        other = target(k)[0]
+        pltpu.make_async_remote_copy(
+            part,
+            parts.at[other],
+            send.at[k],
+            recv.at[other],
+            device_id=target(k)[1],
+            device_id_type=MESH,
+        ).wait_recv()
+    out[...] = jnp.sum(parts[...], 0)
+    for copy in sent:
+        copy.wait_send()
+
+
+def total_over_all(part):
+    vm = pl.BlockSpec(memory_space=pltpu.VMEM)
+    return pl.pallas_call(
+        total_kernel,
+        out_shape=jax.ShapeDtypeStruct((8, 128), F32),
+        in_specs=[vm],
+        out_specs=vm,
+        scratch_shapes=[
+            pltpu.VMEM((32, 8, 128), F32),
+            pltpu.SemaphoreType.DMA((32,)),
+            pltpu.SemaphoreType.DMA((32,)),
+        ],
+        name="total",
+        compiler_params=pltpu.CompilerParams(collective_id=2, has_side_effects=True),
+    )(part)
+
+
+def clip_factor(square):
+    return jnp.minimum(1.0, 0.001 / (jnp.sqrt(square) + 1e-06))
 
 
 def adam_update(master, first, second, grad, rate, decay):
@@ -706,6 +1269,131 @@
     return (master, first, second)
 
 
+def adam_kernel(total, grad, master, first, second, new, new_first, new_second, copy):
+    factor = clip_factor(total[0:1, :])
+    step = 104
+
+    def run(i, carry):
+        rows = pl.ds(pl.multiple_of(i * step, 8), step)
+        a, b, c = adam_update(
+            master[rows, :], first[rows, :], second[rows, :], factor * grad[rows, :], 0.05, 0.05
+        )
+        new[rows, :] = a
+        new_first[rows, :] = b
+        new_second[rows, :] = c
+        return carry
+
+    lax.fori_loop(0, grad.shape[0] // step, run, 0)
+    copy[...] = new[...].astype(BF)
+
+
+def adam(total, grad, master, first, second):
+    count = grad.shape[0]
+    size = 624
+    block = pl.BlockSpec((size, 128), lambda i: (i, 0))
+    shape = jax.ShapeDtypeStruct((count, 128), F32)
+    return pl.pallas_call(
+        adam_kernel,
+        grid=(count // size,),
+        out_shape=[shape] * 3 + [jax.ShapeDtypeStruct((count, 128), BF)],
+        in_specs=[pl.BlockSpec((8, 128), lambda i: (0, 0))] + [block] * 4,
+        out_specs=[block] * 4,
+        name="adam",
+        compiler_params=pltpu.CompilerParams(vmem_limit_bytes=VMEM_LIMIT),
+    )(total, grad, master, first, second)
+
+
+def shifted(value, axis, steps):
+    count = lax.axis_size(axis)
+    initial, last = (max(0, -steps), min(count, count - steps))
+    return lax.ppermute(value, axis, [(source, source + steps) for source in range(initial, last)])
+
+
+def train(images, masked_total, enc, dec, enc_out, dec_out, pixels, visible, restore, vecs, weights):
+    encoding = lax.axis_index("section") == 0
+    pix = jnp.pad(pixels, ((0, 0), (0, ROWS_D - PATCHES), (0, 0)))
+    vis = jnp.pad(visible, ((0, 0), (0, ROWS_E - VIS)), constant_values=-1).reshape(-1, 1)
+    places = jnp.pad(restore, ((0, 0), (0, ROWS_D - PATCHES)), constant_values=-1).reshape(-1, 1)
+    blank_saved = [jnp.zeros(*item) for item in enc_shapes(images).values()]
+    blank_latent = jnp.zeros((images * ROWS_E, DE), BF)
+    latent, *saved = lax.cond(
+        encoding,
+        lambda: list(encoder_forward(images, enc, vis, pix, vecs, weights)),
+        lambda: [blank_latent] + blank_saved,
+    )
+    arrived = shifted(latent, "section", 1)
+    dlatent, loss, dmats, dvec = lax.cond(
+        encoding,
+        lambda: [
+            blank_latent,
+            jnp.zeros((8, 128), F32),
+            jnp.zeros(dec_out.shape, BF),
+            jnp.zeros(vecs.shape, F32),
+        ],
+        lambda: list(
+            decoder_step(
+                images, dec, dec_out, masked_total, arrived, places, pix, vecs, weights
+            )
+        ),
+    )
+    returned = shifted(dlatent, "section", -1)
+    if dec_out.shape == enc_out.shape:
+        other = lambda: [dmats, dvec]
+    else:
+        more = enc_out.shape[0] - dec_out.shape[0]
+        other = lambda: [jnp.pad(dmats, ((0, more), (0, 0), (0, 0))), dvec]
+    dmats, dvec = lax.cond(
+        encoding,
+        lambda: list(
+            encoder_backward(images, enc, enc_out, vis, vecs, returned, saved, weights)
+        ),
+        other,
+    )
+    return dmats, dvec, loss
+
+
+def body_block(
+    pixels, visible, restore, mat_master, mat_first, mat_second, vec_master, vec_first, vec_second
+):
+    images = pixels.shape[0]
+    masked_total = (PATCHES - VIS) * images * 16
+    count, size = mat_master.shape[1] // 128, vec_master.shape[1]
+    plans, table, widths = piece_table(count)
+    table = jnp.asarray(table, jnp.int32)[lax.axis_index("section"), lax.axis_index("dp")]
+    lines = [value.reshape(count, 128) for value in (mat_master, mat_first, mat_second)]
+    room = SLOT_V * 2048
+    own = pack(
+        table, widths, lines[0], jnp.pad(vec_master[0], (0, room - size)).reshape(-1, 128)
+    )
+    slots = gather_slots(own)
+    vecs = slots[:, SLOT_M:].reshape(16, room)[:, :size].reshape(-1, 128).astype(F32)
+    inward = [slot_layout(plan, slots.shape) for plan in plans]
+    outward = [whole_slots(plan, (16, SLOT_M, 16, 128)) for plan in plans]
+    dmats, dvec, loss = train(
+        images, masked_total, *inward, *outward, pixels, visible, restore, vecs, slots
+    )
+    dvec = jnp.pad(dvec.reshape(16, size), ((0, 0), (0, room - size))).astype(BF)
+    total = scatter_slots(dmats, dvec.reshape(16, SLOT_V, 16, 128))
+    grad, grad_vec, part = unpack(table, widths, count, total, loss)
+    total = total_over_all(part)
+    square, loss_sum = total[0, 0], total[1, 0]
+    news = adam(total, grad, *lines)
+    vec_news = adam_update(
+        vec_master,
+        vec_first,
+        vec_second,
+        clip_factor(square) * grad_vec.reshape(1, room)[:, :size],
+        0.3,
+        0.0,
+    )
+    return (
+        (loss_sum, jnp.sqrt(square))
+        + tuple(value.reshape(mat_master.shape) for value in news)
+        + tuple(vec_news)
+        + (vec_news[0].astype(BF),)
+    )
+
+
 def body(
     pixels, visible, restore, mat_master, mat_first, mat_second, vec_master, vec_first, vec_second
 ):
@@ -713,85 +1401,49 @@
     total = mat_master.shape[1] * lax.axis_size("dp")
     masked_total = (PATCHES - VIS) * images * lax.axis_size("dp")
     encoding = lax.axis_index("section") == 0
-    enc_copies = plain_copies(ENC_BASE, ENC_TILES)
-    dec_copies = plain_copies(DEC_BASE, DEC_TILES)
+    enc, dec = plain_layout(ENC_TOTAL), plain_layout(DEC_TOTAL)
     mats = lax.all_gather(mat_master.astype(BF), "dp", axis=1, tiled=True)[0]
     vecs = lax.all_gather(vec_master.astype(BF), "dp", axis=1, tiled=True)[0]
     vecs = vecs.astype(F32).reshape(-1, 128)
-    pix = jnp.pad(pixels, ((0, 0), (0, ROWS_D - PATCHES), (0, 0)))
-    vis = jnp.pad(visible, ((0, 0), (0, ROWS_E - VIS)), constant_values=-1).reshape(-1, 1)
-    places = jnp.pad(restore, ((0, 0), (0, ROWS_D - PATCHES)), constant_values=-1).reshape(-1, 1)
     weights = lax.cond(
         encoding,
         lambda m: natural(m, ENC_MATS),
         lambda m: jnp.pad(natural(m, DEC_MATS), ((0, ENC_TOTAL - DEC_TOTAL), (0, 0), (0, 0))),
         mats,
     )
-    blank_saved = [jnp.zeros(*item) for item in enc_shapes(images).values()]
-    blank_latent = jnp.zeros((images * ROWS_E, DE), BF)
-    latent, saved = lax.cond(
+    dec_in = Layout((ENC_TOTAL, 16, 128), [(lambda ref: ref.at[pl.ds(0, DEC_TOTAL)], 0, DEC_TOTAL)], [])
+    dmats, grad_vecs, loss = train(
+        images, masked_total, enc, dec_in, enc, dec, pixels, visible, restore, vecs, weights
+    )
+    grad_mats = lax.cond(
         encoding,
-        lambda: (lambda out: (out[0], list(out[1:])))(
-            encoder_forward(images, enc_copies, vis, pix, vecs, weights)
-        ),
-        lambda: (blank_latent, blank_saved),
-    )
-    arrived = shifted(latent, "section", 1)
-    dlatent, loss, dmat_dec, dvec_dec = lax.cond(
-        encoding,
-        lambda: [
-            blank_latent,
-            jnp.zeros((8, 128), F32),
-            jnp.zeros((DEC_TOTAL, 16, 128), BF),
-            jnp.zeros(vecs.shape, F32),
-        ],
-        lambda: list(
-            decoder_step(images, dec_copies, masked_total, arrived, places, pix, vecs, weights)
-        ),
-    )
-    returned = shifted(dlatent, "section", -1)
-
-    def encoder_side():
-        dmats, dvec = encoder_backward(images, enc_copies, vis, vecs, returned, saved, weights)
-        return flat_from_natural(dmats.astype(F32), ENC_MATS, total), dvec
-
-    grad_mats, grad_vecs = lax.cond(
-        encoding,
-        encoder_side,
-        lambda: (flat_from_natural(dmat_dec.astype(F32), DEC_MATS, total), dvec_dec),
+        lambda m: flat_from_natural(m.astype(F32), ENC_MATS, total),
+        lambda m: flat_from_natural(m[0:DEC_TOTAL].astype(F32), DEC_MATS, total),
+        dmats,
     )
     summed_mats = lax.psum_scatter(grad_mats[None], "dp", scatter_dimension=1, tiled=True)
     summed_vecs = lax.psum_scatter(
         grad_vecs.reshape(1, -1), "dp", scatter_dimension=1, tiled=True
     )
     square = jnp.sum(summed_mats * summed_mats) + jnp.sum(summed_vecs * summed_vecs)
-    square_all, loss_sum = lax.psum((square, loss[0, 0]), ("section", "dp"))
-    grad_norm = jnp.sqrt(square_all)
-    factor = jnp.minimum(1.0, 0.001 / (grad_norm + 1e-06))
-    mat_new, mat_first_new, mat_second_new = adam_update(
-        mat_master, mat_first, mat_second, factor * summed_mats, 0.05, 0.05
-    )
-    vec_new, vec_first_new, vec_second_new = adam_update(
-        vec_master, vec_first, vec_second, factor * summed_vecs, 0.3, 0.0
-    )
+    square, loss_sum = lax.psum((square, loss[0, 0]), ("section", "dp"))
+    factor = clip_factor(square)
+    mat_news = adam_update(mat_master, mat_first, mat_second, factor * summed_mats, 0.05, 0.05)
+    vec_news = adam_update(vec_master, vec_first, vec_second, factor * summed_vecs, 0.3, 0.0)
     return (
-        loss_sum,
-        grad_norm,
-        mat_new,
-        mat_first_new,
-        mat_second_new,
-        mat_new.astype(BF),
-        vec_new,
-        vec_first_new,
-        vec_second_new,
-        vec_new.astype(BF),
+        (loss_sum, jnp.sqrt(square))
+        + tuple(mat_news)
+        + (mat_news[0].astype(BF),)
+        + tuple(vec_news)
+        + (vec_news[0].astype(BF),)
     )
 
 
 def solution(mesh):
     split = P("section", "dp")
+    fits = mesh.shape["section"] == 2 and mesh.shape["dp"] == 16
     return jax.shard_map(
-        body,
+        body_block if fits else body,
         mesh=mesh,
         in_specs=(P("dp", None, None), P("dp", None), P("dp", None)) + (split,) * 6,
         out_specs=(P(), P()) + (split,) * 8,

time: 2360 us -> 491 us (0.21)
  waiting for transfers between devices: 1670 us -> 140 us
  other arithmetic: 354 us -> 2.12 us
  Pallas kernels: 75.3 us -> 312 us
  local copies, waits for them, and re-layouts: 181 us -> 29.1 us
  blocking collectives: 40.5 us -> 0 us
    unnamed x7 -> x0, waiting for transfers between devices: 1370 us -> none
    all_gather x1 -> x0, other arithmetic: 325 us -> none  [body(): mats = lax.all_gather(mat_master.astype(BF), 'dp', axis=1, tiled=True)[0]]
    pallas_call x2 -> x8, Pallas kernels: 75.3 us -> 312 us  [the longest x1 107 us: scatter_slots(): pl.pallas_call(scatter_kernel, out_shape=jax.ShapeDtypeStruct((SLOT, 16,...]
    all_gather x1 -> x0, waiting for transfers between devices: 156 us -> none  [body(): mats = lax.all_gather(mat_master.astype(BF), 'dp', axis=1, tiled=True)[0]]
    reshape x10 -> x3, local copies, waits for them, and re-layouts: 46.6 us -> 1.79 us  [the longest x1 1.4 us: body_block(): jnp.pad(vec_master[0], (0, room - size)).reshape(-1, 128)]
    psum x1 -> x0, blocking collectives: 40.5 us -> none  [body(): square_all, loss_sum = lax.psum((square, loss[0, 0]), ('section', 'dp'))]
    slice x12 -> x2, local copies, waits for them, and re-layouts: 37.6 us -> 2.36 us  [the longest x1 1.27 us: body_block(): square, loss_sum = (total[0, 0], total[1, 0])]
    unnamed x24 -> x17, local copies, waits for them, and re-layouts: 43.3 us -> 13 us
  transfers between devices with their start and end apart: 6 -> 2, of which waited for: 6 -> 2; matrix products, arithmetic and copies ran while one was open for 1% -> 0% of each run, Pallas kernels for 0% -> 0%
where the time goes in v2:
time: 491 us; the launch traced here: 490 us
  Pallas kernels  312 us (64%)
  waiting for transfers between devices  140 us (29%)
  local copies, waits for them, and re-layouts  29.1 us (6%)
    ppermute x2, waiting for transfers between devices, shifted(): lax.ppermute(value, axis, [(source, source + steps) for source in range(i...  140 us
    pallas_call x1, Pallas kernels, scatter_slots(): pl.pallas_call(scatter_kernel, out_shape=jax.ShapeDtypeStruct((SLOT, 16,...  107 us
    pallas_call x1, Pallas kernels, gather_slots(): pl.pallas_call(gather_kernel, out_shape=jax.ShapeDtypeStruct((16, SLOT, 1...  104 us
    pallas_call x1, Pallas kernels, encoder_backward(): pl.pallas_call(functools.partial(encoder_backward_kernel, images, layout,...  42.4 us
    pallas_call x1, Pallas kernels, encoder_forward(): pl.pallas_call(functools.partial(encoder_forward_kernel, images, layout),...  33.5 us
    unnamed x17, local copies, waits for them, and re-layouts  13 us
  transfers between devices with their start and end apart: 2, of which 2 were waited for; matrix products, arithmetic and copies ran while one was open for 0% of the time, Pallas kernels for 0%

profile of v2, /device:TPU:0, one launch (start us, length us, event | category | flops | bytes accessed | tf_op | source)
XLA Modules:
  0.0 490.1 jit_solution(13938647046444497855)
XLA Ops:
  0.7 0.7 pad.22
  1.3 0.1 reshape.68
  1.4 1.4 pad_bitcast_fusion.1.vec
  2.8 2.4 copy.23
  5.3 1.2 dynamic-slice_bitcast_fusion.table
  6.5 3.7 pack.1.own
  10.2 104.5 %gather_slots.1 = bf16[16,269,16,128]{3,2,1,0:T(8,128)(2,1)} custom-call(bf16[269,16,128]{2,1,0:T(8,128)(2,1)} %pack.1.own), custom_call_target="tpu_custom_call" | custom-call | tf_op jit(solution)/shard_map/gather_slots/pallas_call | solution.py:887
  114.7 0.0 copy-start
  114.7 1.1 slice.15
  115.8 0.1 copy.32
  116.0 0.3 reshape.85
  116.3 0.0 copy-done
  116.3 1.1 pad.23
  117.4 0.0 copy-start.5
  117.4 34.3 %conditional.3 = ((bf16[256,768]{1,0:T(8,128)(2,1)}, bf16[256,768]{1,0:T(8,128)(2,1)}, f32[256,768]{1,0:T(8,128)}, bf16[256,768]{1,0:T(8,128)(2,1)}, bf16[256,23...) conditional(s32[]{:T(128)} %convert_element_type.21, () %tuple.28, ...), branch_computations={%region_0.1_spmd, %region_1.2_spmd} | conditional | bytes 10223742 | solution.py:1319
  117.4 0.8 copy.24.vis
  118.2 33.5 %encoder_forward.1 = (bf16[256,768]{1,0:T(8,128)(2,1)}, bf16[256,768]{1,0:T(8,128)(2,1)}, f32[256,768]{1,0:T(8,128)}, bf16[256,768]{1,0:T(8,128)(2,1)}, bf16[256...) custom-call(s32[256,1]{1,0:T(8,128)} %copy.24.vis, ...), custom_call_target="tpu_custom_call" | custom-call | tf_op jit(solution)/shard_map/cond/branch_1_fun/encoder_forward/pallas_call | solution.py:502
  151.7 2.0 collective-permute-start
  153.7 8.8 %collective-permute-done = bf16[256,768]{1,0:T(8,128)(2,1)} collective-permute-done((bf16[256,768]{1,0:T(8,128)(2,1)}, bf16[256,768]{1,0:T(8,128)(2,1)}, u32[]{:S(2)}, u32[]{:S(2)}) %collective-permute-start) | collective-permute-done | bytes 393248 | tf_op jit(solution)/shard_map/ppermute | solution.py:1309
  162.5 0.0 copy-done.5
  162.5 7.0 %conditional.4 = (bf16[256,768]{1,0:T(8,128)(2,1)}, f32[8,128]{1,0:T(8,128)S(1)}, bf16[16,264,16,128]{3,2,1,0:T(8,128)(2,1)}, bf16[1272,128]{1,0:T(8,128)(2,1)S(1)}) conditional(s32[]{:T(128)} %convert_element_type.21, (s32[4,196]{1,0:T(4,128)S(1)}, bf16[256,768]{1,0:T(8,128)(2,1)}, bf16[4,208,768]{2,1,0:T(8,128)(2,1)}, f32[1272,128]{1,0:T(8,128)S(1)}, ...), branch_computations={%region_2.3_spmd, %region_3.4_spmd} | conditional | flops 162816 | bytes 18024492 | solution.py:1325
  162.5 0.8 broadcast.18
  163.3 6.2 %broadcast.20 = bf16[16,264,16,128]{3,2,1,0:T(8,128)(2,1)} broadcast(bf16[]{:T(256)} %constant.18.clone), dimensions={} | broadcast | bytes 17301506 | tf_op jit(solution)/shard_map/broadcast.9
  169.5 1.3 collective-permute-start.1
  170.8 131.6 %collective-permute-done.1 = bf16[256,768]{1,0:T(8,128)(2,1)} collective-permute-done((bf16[256,768]{1,0:T(8,128)(2,1)}, bf16[256,768]{1,0:T(8,128)(2,1)}, u32[]{:S(2)}, u32[]{:S(2)}) %collective-permute-start.1) | collective-permute-done | bytes 393248 | tf_op jit(solution)/shard_map/ppermute | solution.py:1309
  302.4 44.4 %conditional.5 = ((bf16[16,264,16,128]{3,2,1,0:T(8,128)(2,1)}, bf16[1272,128]{1,0:T(8,128)(2,1)S(1)})) conditional(s32[]{:T(128)} %convert_element_type.21, (bf16[16,264,16,128]{3,2,1,0:T(8,128)(2,1)}, bf16[1272,128]{1,0:T(8,128)(2,1)S(1)}) %tuple.32, (s32[256,1]{0,1:T(1,128)S(1)}, f32[1272,128]{1,0:T(8,128)S(1)}, bf16[256,768]{1,0:T(8,128)(2,1)}, ...), branch_computations={%region_4.5_spmd, %region_5.6_spmd} | conditional | flops 162816 | bytes 978968 | solution.py:1345
  302.4 0.8 copy.25.vis
  303.2 42.4 %encoder_backward.1 = (bf16[16,264,16,128]{3,2,1,0:T(8,128)(2,1)}, f32[1272,128]{1,0:T(8,128)}) custom-call(s32[256,1]{1,0:T(8,128)} %copy.25.vis, f32[1272,128]{1,0:T(8,128)S(1)} %get-tuple-element.63.vec, bf16[256,768]{1,0:T(8,128)(2,1)} %get-tuple-element.64.dlatent, bf16[256,768]{1,0:T(8,128)(2,1)} %get-tuple-element.65.refs_0_, ...), custom_call_target="tpu_custom_call" | custom-call | tf_op jit(solution)/shard_map/cond/branch_1_fun/encoder_backward/pallas_call | solution.py:565
  345.7 1.1 convert.10
  346.8 0.3 reshape.86
  347.1 0.8 copy.27
  347.9 106.7 %scatter_slots.1.total = f32[269,16,128]{2,1,0:T(8,128)} custom-call(bf16[16,264,16,128]{3,2,1,0:T(8,128)(2,1)} %get-tuple-element.159.mats, bf16[16,5,16,128]{3,2,1,0:T(8,128)(2,1)} %bitcast.35), custom_call_target="tpu_custom_call" | custom-call | tf_op jit(solution)/shard_map/scatter_slots/pallas_call | solution.py:1076
  454.6 4.1 unpack.1
  458.7 9.4 %total.1 = f32[8,128]{1,0:T(8,128)} custom-call(f32[8,128]{1,0:T(8,128)} %get-tuple-element.127.part), custom_call_target="tpu_custom_call" | custom-call | tf_op jit(solution)/shard_map/total/pallas_call | solution.py:1244
  468.1 1.3 fusion.3
  470.1 8.1 %adam.1 = (f32[3744,128]{1,0:T(8,128)}, f32[3744,128]{1,0:T(8,128)}, f32[3744,128]{1,0:T(8,128)}, bf16[3744,128]{1,0:T(8,128)(2,1)}) custom-call(f32[8,128]{1,0:T(8,128)} %total.1, f32[3744,128]{1,0:T(8,128)} %get-tuple-element.128.grad, f32[3744,128]{1,0:T(8,128)} %bitcast.29, f32[3744,128]{1,0:T(8,128)} %bitcast.30, f32[3744,128]{1,0:T(8,128)} %bitcast.31), custom_call_target="tpu_custom_call" | custom-call | tf_op jit(solution)/shard_map/adam/pallas_call | solution.py:1295
  478.1 0.0 copy-start.1
  478.2 0.0 copy-start.2
  478.2 0.0 copy-start.3
  478.2 0.0 copy-start.4
  478.2 9.7 %copy.31 = bf16[1,1,3744,128]{3,1,2,0:T(2,128)(2,1)} copy(bf16[1,1,3744,128]{3,2,1,0:T(8,128)(2,1)} %bitcast.36) | data formatting | bytes 1916928
  487.9 0.0 copy-done.1
  487.9 0.0 copy-done.2
  488.0 0.0 copy-done.3
  488.0 0.0 copy-done.4
  488.0 1.0 fusion.1
  (4 shorter events, 0.1 us)
Async XLA Ops:
  114.7 1.5 copy-start
  117.4 45.1 %copy-start.5 = (s32[4,196]{1,0:T(4,128)S(1)}, s32[4,196]{1,0:T(4,128)}, u32[]{:S(2)}) copy-start(s32[4,196]{1,0:T(4,128)} %param.18) | copy-start | bytes 9412
  151.7 10.8 %collective-permute-start = (bf16[256,768]{1,0:T(8,128)(2,1)}, bf16[256,768]{1,0:T(8,128)(2,1)}, u32[]{:S(2)}, u32[]{:S(2)}) collective-permute-start(bf16[256,768]{1,0:T(8,128)(2,1)} %get-tuple-element.110), channel_id=1, source_target_pairs={{0,16},{1,17},{2,18},{3,19},{4,20},{5,21},{6,22},{7,23},{8,24},{9,... | collective-permute-start | bytes 1179656 | tf_op jit(solution)/shard_map/ppermute | solution.py:1309
  169.5 132.9 %collective-permute-start.1 = (bf16[256,768]{1,0:T(8,128)(2,1)}, bf16[256,768]{1,0:T(8,128)(2,1)}, u32[]{:S(2)}, u32[]{:S(2)}) collective-permute-start(bf16[256,768]{1,0:T(8,128)(2,1)} %get-tuple-element.113), channel_id=1, source_target_pairs={{16,0},{17,1},{18,2},{19,3},{20,4},{21,5},{22,6},{23,7},{24,8},{25... | collective-permute-start | bytes 1179656 | tf_op jit(solution)/shard_map/ppermute | solution.py:1309
  478.1 9.8 %copy-start.1 = (f32[1,10176]{1,0:T(1,128)S(1)}, f32[1,10176]{1,0:T(1,128)}, u32[]{:S(2)}) copy-start(f32[1,10176]{1,0:T(1,128)} %param.22) | copy-start | bytes 122116
  478.2 9.8 %copy-start.2 = (f32[1,10176]{1,0:T(1,128)S(1)}, f32[1,10176]{1,0:T(1,128)}, u32[]{:S(2)}) copy-start(f32[1,10176]{1,0:T(1,128)} %param.23) | copy-start | bytes 122116
  478.2 9.8 %copy-start.3 = (f32[1,10176]{1,0:T(1,128)S(1)}, f32[1,10176]{1,0:T(1,128)}, u32[]{:S(2)}) copy-start(f32[1,10176]{1,0:T(1,128)} %param.24) | copy-start | bytes 122116
  478.2 9.8 %copy-start.4 = (f32[80,128]{1,0:T(8,128)S(1)}, f32[80,128]{1,0:T(8,128)}, u32[]{:S(2)}) copy-start(f32[80,128]{1,0:T(8,128)} %get-tuple-element.133) | copy-start | bytes 122884

commit v3 on v2

--- a/solution.py
+++ b/solution.py
@@ -48,11 +48,18 @@
 
 
 class Mat:
-    def __init__(self, ref, base, shape):
+    def __init__(self, ref, base, shape, loads=None, stores=None):
+        self.base, self.loads, self.stores = base, loads, stores
         self.rows, self.columns = shape
         self.blocks = self.columns // 128
         count = self.rows * self.columns // 2048
         self.ref = ref.at[pl.ds(base, count)].reshape(self.rows // 16, self.blocks, 16, 128)
+
+    def need(self):
+        self.loads.need(self.base, self.rows * self.columns // 2048)
+
+    def done(self):
+        self.stores.done(self.base, self.rows * self.columns // 2048)
 
     def cols(self, block):
         parts = [self.ref[:, 2 * block + half].reshape(self.rows, 128) for half in range(2)]
@@ -126,19 +133,24 @@
     return centred * scale, scale
 
 
-CHUNK = 32
-
-
-def chunk_rows(i):
-    return pl.ds(pl.multiple_of(i * CHUNK, CHUNK), CHUNK)
+CHUNKS = (208, 128, 64, 32)
+
+
+def chunk_loop(ref, step, init=0):
+    count = ref.shape[0]
+    size = next(c for c in CHUNKS if count % c == 0)
+
+    def run(i, carry):
+        return step(pl.ds(pl.multiple_of(i * size, size), size), carry)
+
+    return lax.fori_loop(0, count // size, run, init)
 
 
 def norm_rows(x_ref, out_ref, vec, gain_at, shift_at, width, add_ref=None, bias_at=None):
     gain, shift = row_of(vec, gain_at, width), row_of(vec, shift_at, width)
     bias = None if bias_at is None else row_of(vec, bias_at, width)
 
-    def step(i, carry):
-        rows = chunk_rows(i)
+    def step(rows, carry):
         x = x_ref[rows, :]
         if add_ref is not None:
             x = x + add_ref[rows, :] + bias
@@ -147,16 +159,15 @@
         out_ref[rows, :] = (unit * gain + shift).astype(BF)
         return carry
 
-    loop(x_ref.shape[0] // CHUNK, step)
+    chunk_loop(x_ref, step)
 
 
 def norm_back_rows(x_ref, dy_ref, dx_ref, dxb_ref, vec, dvec, gain_at, shift_at, width, bias_at, add):
     gain = row_of(vec, gain_at, width)
     zero = jnp.zeros((8, width), F32)
 
-    def step(i, carry):
+    def step(rows, carry):
         dgain, dshift, dbias = carry
-        rows = chunk_rows(i)
         unit, scale = norm_parts(x_ref[rows, :])
         dy = dy_ref[rows, :].astype(F32)
         dunit = dy * gain
@@ -171,7 +182,7 @@
         dxb_ref[rows, :] = dx.astype(BF)
         return dgain + fold(dy * unit), dshift + fold(dy), dbias + fold(dx)
 
-    dgain, dshift, dbias = loop(x_ref.shape[0] // CHUNK, step, (zero, zero, zero))
+    dgain, dshift, dbias = chunk_loop(x_ref, step, (zero, zero, zero))
     put_row(dvec, gain_at, total_row(dgain))
     put_row(dvec, shift_at, total_row(dshift))
     if bias_at is not None:
@@ -216,7 +227,7 @@
         att[rows, lanes(b, 128)] = out.astype(BF)
         return carry
 
-    loop(groups * blocks, step)
+    lax.fori_loop(0, groups * blocks, step, 0, unroll=4 if groups * blocks % 4 == 0 else 2)
 
 
 def attention_back(qkv, probs, datt, dqkv, dvec, qv_at, group, groups, width, size):
@@ -252,7 +263,7 @@
         dvec[pl.ds(qv_at + blocks + b, 1), :] += total_row(dv)
         return carry
 
-    loop(groups * blocks, step)
+    lax.fori_loop(0, groups * blocks, step, 0, unroll=2)
 
 
 def block_forward(s, mats, vec, at, width, hidden, size, bias, group, groups):
@@ -268,6 +279,7 @@
         s.qkv[:, lanes(j)] = (value * jnp.where(part == 0, scale, 1.0)).astype(BF)
         return carry
 
+    w_qkv.need()
     loop(3 * pairs, qkv_step)
     attention(s.qkv, s.probs, s.att, bias, group, groups, width, size)
 
@@ -275,6 +287,7 @@
         s.x1[:, lanes(j)] = dot(s.att[...], w_proj.cols(j))
         return carry
 
+    w_proj.need()
     loop(pairs, proj_step)
     norm_rows(s.x0, s.n2, vec, at["g2"], at["s2"], width, s.x1, at["bo"])
 
@@ -294,6 +307,8 @@
 
         return carry
 
+    w_up.need()
+    w_down.need()
     loop(hidden // 256, mlp_step)
 
 
@@ -323,7 +338,11 @@
 
         return carry
 
+    w_down.need()
+    w_up.need()
     loop(hidden // 256, mlp_step)
+    d_down.done()
+    d_up.done()
     norm_back_rows(s.x1, s.dn, s.dx, s.dxb, vec, dvec, at["g2"], at["s2"], width, at["bo"], True)
 
     def proj_step(j, carry):
@@ -332,7 +351,9 @@
         d_proj.put_band(j, t_dot(s.att[:, lanes(j)], dxb))
         return carry
 
+    w_proj.need()
     loop(pairs, proj_step)
+    d_proj.done()
     attention_back(s.qkv, s.probs, s.datt, s.dqkv, dvec, at["qv"], group, groups, width, size)
     s.flip[...] = s.n1[...].T
 
@@ -341,11 +362,13 @@
         return carry
 
     loop(3 * pairs, weight_step)
+    d_qkv.done()
 
     def input_step(j, carry):
         s.dn[:, lanes(j)] = dot_t(s.dqkv[...], w_qkv.band(j))
         return carry
 
+    w_qkv.need()
     loop(pairs, input_step)
     norm_back_rows(s.x0, s.dn, s.dx, s.dxb, vec, dvec, at["g1"], at["s1"], width, None, True)
 
@@ -369,16 +392,16 @@
     return Layout((total, 16, 128), [(lambda ref: ref, 0, total)], [])
 
 
-def slot_layout(plan, shape):
+def slot_layout(plan, shape, lead):
     moves, shared, done = [], [], 0
     for device, (first, count, _) in enumerate(plan):
         skip = max(0, done - first)
         if skip and count:
-            shared.append((lambda ref, d=device, n=skip: ref.at[d, pl.ds(0, n)], first, skip))
+            shared.append((lambda ref, d=device, n=skip: ref.at[d, pl.ds(lead, n)], first, skip))
         if count:
             moves.append(
                 (
-                    lambda ref, d=device, a=skip, n=count - skip: ref.at[d, pl.ds(a, n)],
+                    lambda ref, d=device, a=skip, n=count - skip: ref.at[d, pl.ds(lead + a, n)],
                     first + skip,
                     count - skip,
                 )
@@ -399,30 +422,55 @@
 SHARED = 24
 
 
-def load_mats(source, kept, side, sem, layout):
-    started = []
-    for index, (pick, start, count) in enumerate(layout.moves):
-        copy = pltpu.make_async_copy(pick(source), kept.at[pl.ds(start, count)], sem.at[index])
-        copy.start()
-        started.append(copy)
-    for index, (pick, start, count) in enumerate(layout.shared):
-        copy = pltpu.make_async_copy(
-            pick(source),
-            side.at[index, pl.ds(0, count)],
-            sem.at[len(layout.moves) + index],
-        )
-        copy.start()
-        started.append(copy)
-    return started
-
-
-def finish_mats(started, kept, side, layout):
-    for copy in started:
-        copy.wait()
-    for index, (_, start, count) in enumerate(layout.shared):
-        there = pl.ds(start, count)
-        both = kept[there].astype(F32) + side[index, 0:count].astype(F32)
-        kept[there] = both.astype(BF)
+class Loads:
+    def __init__(self, source, kept, side, sem, layout, backward=False):
+        self.kept, self.side, self.flying = kept, side, []
+        moves = list(enumerate(layout.moves))
+        for index, (pick, start, count) in moves[::-1] if backward else moves:
+            copy = pltpu.make_async_copy(pick(source), kept.at[pl.ds(start, count)], sem.at[index])
+            copy.start()
+            self.flying.append((start, count, None, copy))
+        for index, (pick, start, count) in enumerate(layout.shared):
+            copy = pltpu.make_async_copy(
+                pick(source),
+                side.at[index, pl.ds(0, count)],
+                sem.at[len(layout.moves) + index],
+            )
+            copy.start()
+            self.flying.append((start, count, index, copy))
+
+    def need(self, base, tiles):
+        here = [f for f in self.flying if f[0] < base + tiles and f[0] + f[1] > base]
+        self.flying = [f for f in self.flying if f not in here]
+        for item in here:
+            item[3].wait()
+        for start, count, index, _ in here:
+            if index is not None:
+                there = pl.ds(start, count)
+                both = self.kept[there].astype(F32) + self.side[index, 0:count].astype(F32)
+                self.kept[there] = both.astype(BF)
+
+
+class Stores:
+    def __init__(self, kept, out, sem, layout):
+        self.kept, self.out, self.sem = kept, out, sem
+        self.left, self.ready, self.flying = list(enumerate(layout.moves)), set(), []
+
+    def done(self, base, tiles):
+        self.ready.update(range(base, base + tiles))
+        for item in list(self.left):
+            index, (pick, start, count) = item
+            if self.ready.issuperset(range(start, start + count)):
+                copy = pltpu.make_async_copy(
+                    self.kept.at[pl.ds(start, count)], pick(self.out), self.sem.at[index]
+                )
+                copy.start()
+                self.flying.append(copy)
+                self.left.remove(item)
+
+    def finish(self):
+        for copy in self.flying:
+            copy.wait()
 
 
 def load_scratch(layout):
@@ -471,9 +519,9 @@
     latent = refs[0]
     s = Bag(ENC_KEEP, refs[1 : 1 + len(ENC_KEEP)])
     kept, posit, side, sem = refs[1 + len(ENC_KEEP) :]
-    started = load_mats(weights, kept, side, sem, layout)
+    loads = Loads(weights, kept, side, sem, layout)
     rows = images * ROWS_E
-    mats = [Mat(kept, b, shape) for b, shape in zip(ENC_BASE, ENC_MATS)]
+    mats = [Mat(kept, b, shape, loads) for b, shape in zip(ENC_BASE, ENC_MATS)]
     posit[...] = jnp.zeros_like(posit)
     for j in range(DE // 128):
         posit[0:PATCHES, j * 128 : (j + 1) * 128] = position_column(vec, EV[1], DE // 128, j)
@@ -482,7 +530,7 @@
         hot = visible_rows(vis[where, :], ROWS_D)
         s.pick[where, :] = dot(hot, pix[i]).astype(BF)
         s.x0[where, :] = dot(hot, posit[...].astype(BF)) + row_of(vec, EV[0], DE)
-    finish_mats(started, kept, side, layout)
+    mats[0].need()
 
     def embed_step(j, carry):
         s.x0[:, lanes(j)] += dot(s.pick[...], mats[0].cols(j))
@@ -515,30 +563,21 @@
     )(vis, pix, vec, weights)
 
 
-def store_mats(kept, out, sem, layout):
-    started = []
-    for index, (pick, start, count) in enumerate(layout.moves):
-        copy = pltpu.make_async_copy(kept.at[pl.ds(start, count)], pick(out), sem.at[index])
-        copy.start()
-        started.append(copy)
-    return started
-
-
 def encoder_backward_kernel(images, layout, out_layout, vis, vec, dlatent, *refs):
     s = Bag(ENC_KEEP, refs[: len(ENC_KEEP)])
     weights, dmats, dvec = refs[len(ENC_KEEP) : len(ENC_KEEP) + 3]
     kept, dkept, s.dx, s.dxb, s.dn, s.datt, s.dqkv, s.flip, out_sem, side, sem = refs[
         len(ENC_KEEP) + 3 :
     ]
-    started = load_mats(weights, kept, side, sem, layout)
+    loads = Loads(weights, kept, side, sem, layout, True)
+    stores = Stores(dkept, dmats, out_sem, out_layout)
     rows = images * ROWS_E
-    mats = [Mat(kept, b, shape) for b, shape in zip(ENC_BASE, ENC_MATS)]
-    grads = [Mat(dkept, b, shape) for b, shape in zip(ENC_BASE, ENC_MATS)]
+    mats = [Mat(kept, b, shape, loads) for b, shape in zip(ENC_BASE, ENC_MATS)]
+    grads = [Mat(dkept, b, shape, None, stores) for b, shape in zip(ENC_BASE, ENC_MATS)]
     dvec[EV[11] + DE // 128 :, :] = jnp.zeros_like(dvec[EV[11] + DE // 128 :, :])
     norm_back_rows(
         s.x2, dlatent, s.dx, s.dxb, vec, dvec, EV[10], EV[11], DE, EV[9], False
     )
-    finish_mats(started, kept, side, layout)
     block_backward(
         s, mats[1:5], grads[1:5], vec, dvec, ENC_AT, DE, FE, DE // HE, rows, 1
     )
@@ -549,13 +588,13 @@
         return carry
 
     loop(DE // 256, embed_step)
-    stores = store_mats(dkept, dmats, out_sem, out_layout)
+    grads[0].done()
+    mats[0].need()
     hot = visible_rows(vis[...], ROWS_D)
     for j in range(DE // 128):
         value = t_dot(hot, s.dxb[:, j * 128 : (j + 1) * 128])
         dvec[pl.ds(EV[1] + j, PATCHES, stride=DE // 128), :] = value[0:PATCHES]
-    for copy in stores:
-        copy.wait()
+    stores.finish()
 
 
 def encoder_backward(images, layout, out_layout, vis, vec, dlatent, saved, weights):
@@ -596,14 +635,15 @@
     kept, dkept, posit, dguess, out_sem, side, sem = refs[18:]
     s.datt = s.n2
     rows = images * ROWS_D
-    mats = [Mat(kept, b, shape) for b, shape in zip(DEC_BASE, DEC_MATS)]
-    grads = [Mat(dkept, b, shape) for b, shape in zip(DEC_BASE, DEC_MATS)]
-    started = load_mats(weights, kept, side, sem, layout)
+    loads = Loads(weights, kept, side, sem, layout)
+    stores = Stores(dkept, dmats, out_sem, out_layout)
+    mats = [Mat(kept, b, shape, loads) for b, shape in zip(DEC_BASE, DEC_MATS)]
+    grads = [Mat(dkept, b, shape, None, stores) for b, shape in zip(DEC_BASE, DEC_MATS)]
     posit[...] = jnp.zeros_like(posit)
     for j in range(DD // 128):
         posit[0:PATCHES, j * 128 : (j + 1) * 128] = position_column(vec, DV[2], DD // 128, j)
     dvec[DV[13] + PIX // 128 :, :] = jnp.zeros_like(dvec[DV[13] + PIX // 128 :, :])
-    finish_mats(started, kept, side, layout)
+    mats[0].need()
     for i in range(images):
         part = pl.ds(i * ROWS_E, ROWS_E)
         where = pl.ds(i * ROWS_D, ROWS_D)
@@ -639,6 +679,7 @@
         put_row_at(dvec, DV[13], j, total_row(column))
         return total + count
 
+    mats[5].need()
     total = loop(PIX // 256, head_step, jnp.zeros((8, 256), F32))
     loss[...] = jnp.broadcast_to(jnp.sum(total) * (1.0 / PIX), (8, 128))
     s.flip[...] = s.dxb[...].T
@@ -648,6 +689,7 @@
         return carry
 
     loop(PIX // 256, head_weight_step)
+    grads[5].done()
 
     def head_input_step(j, carry):
         s.dn[:, lanes(j)] = dot_t(dguess[...], mats[5].band(j))
@@ -681,8 +723,8 @@
     for j in range(DE // 256):
         grads[0].put_band(j, t_dot(latent[:, j * 256 : (j + 1) * 256], back))
         dlatent[:, j * 256 : (j + 1) * 256] = dot_t(back, mats[0].band(j)).astype(BF)
-    for copy in store_mats(dkept, dmats, out_sem, out_layout):
-        copy.wait()
+    grads[0].done()
+    stores.finish()
 
 
 def decoder_step(images, layout, out_layout, masked_total, latent, places, pix, vec, weights):
@@ -753,6 +795,7 @@
 SLOT = SLOT_M + SLOT_V
 PART = ((0, 224), (224, SLOT - 224))
 MARGIN = 384
+LINES = 3744
 
 
 def shard_plan(shapes, total, devices):
@@ -934,7 +977,54 @@
         return self.ref[pl.ds(index.start - self.start, index.size)]
 
 
-def scatter_kernel(mats, vecs, out, held, core_in, side_a, side_b, z_a, z_b, load, send, r_core, r_side, r_z):
+def owned_limits(plans):
+    limits = []
+    for plan, shapes in zip(plans, (ENC_MATS, DEC_MATS)):
+        low = 0
+        for _, count, pieces in plan:
+            if not pieces:
+                limits.append((0, 0, 0, 0, 0))
+                continue
+            blocks, line, _, _ = pieces[0]
+            skip = -line // blocks if line < 0 else 0
+            last, line, rows, _ = pieces[-1]
+            over = max(0, line + rows * 16 * last - LINES) // last
+            limits.append((count, blocks, skip, last, over))
+    return limits
+
+
+def finish_tiles(out, sources, start, count, owned, square):
+    tiles, first, skip, last, over = owned
+    row = lax.broadcasted_iota(jnp.int32, (1, 16, 1), 1)
+
+    def some(base, size, square):
+        value = sources[0][pl.ds(base, size)].astype(F32)
+        for source in sources[1:]:
+            value = value + source[pl.ds(base, size)].astype(F32)
+        out[pl.ds(base, size)] = value
+        tile = base - SLOT_V + lax.broadcasted_iota(jnp.int32, (size, 1, 1), 0)
+        mine = (tile < tiles) & ((tile >= first) | (row >= skip))
+        mine = mine & ((tile < tiles - last) | (row < 16 - over))
+        mine = mine | (tile < 0)
+        value = jnp.where(mine, value * value, 0.0)
+        return square + value.reshape(size * 2, 8, 128).sum(0)
+
+    def body(i, carry):
+        return some(start + i * 8, 8, carry)
+
+    square = lax.fori_loop(0, count // 8, body, square)
+    if count % 8:
+        square = some(start + count // 8 * 8, count % 8, square)
+    return square
+
+
+def scatter_kernel(limits, mats, vecs, loss, out, total, held, core_in, side_a, side_b, z_a, z_b, parts, load, send, r_core, r_side, r_z, r_parts):
+    me = lax.axis_index("section") * 16 + lax.axis_index("dp")
+
+    def other(k):
+        device = lax.rem(me + k, 32)
+        return device, (device // 16, lax.rem(device, 16))
+
     def run(s, z, y, c):
         around = devices_around(z, y, c, s)
         loads = {}
@@ -947,17 +1037,20 @@
                     index = slot(zz, yy, cc)
                     pair = (
                         pltpu.make_async_copy(
-                            mats.at[index], held.at[index, pl.ds(0, SLOT_M)], load.at[n]
+                            mats.at[index], held.at[index, pl.ds(SLOT_V, SLOT_M)], load.at[n]
                         ),
                         pltpu.make_async_copy(
-                            vecs.at[index], held.at[index, pl.ds(SLOT_M, SLOT_V)], load.at[16 + n]
+                            vecs.at[index], held.at[index, pl.ds(0, SLOT_V)], load.at[16 + n]
                         ),
                     )
                     for copy in pair:
                         copy.start()
                     loads[n] = pair
                     n += 1
-        greet(around)
+        barrier = pltpu.get_barrier_semaphore()
+        for k in range(1, 32):
+            pl.semaphore_signal(barrier, inc=1, device_id=other(k)[1], device_id_type=MESH)
+        pl.semaphore_wait(barrier, 31)
         sent = []
 
         def remote(source, target, sem, name):
@@ -1057,27 +1150,66 @@
         for zz in order[:-1]:
             along(0, zz, False)
         arrive(side_b, r_side.at[DEPTH])
-        add_tiles(
+        owned = [sum(jnp.where(me == k, row[n], 0) for k, row in enumerate(limits)) for n in range(5)]
+        square = finish_tiles(
             out,
             side_sources(z, y) + gathered(1, y) + [Shifted(side_b, PART[1][0])],
             *PART[1],
+            owned,
+            jnp.zeros((8, 128), F32),
         )
         arrive(side_a.at[z], r_side.at[z])
-        add_tiles(out, side_sources(z, y) + [side_a.at[z]] + gathered(0, y), *PART[0])
+        square = finish_tiles(
+            out,
+            side_sources(z, y) + [side_a.at[z]] + gathered(0, y),
+            *PART[0],
+            owned,
+            square,
+        )
+        row = lax.broadcasted_iota(jnp.int32, (8, 128), 0)
+        parts[me] = jnp.where(row == 0, jnp.sum(square), loss[...])
         for copy in sent:
             copy.wait_send()
 
     for_each_depth(run)
-
-
-def scatter_slots(mats, vecs):
+    copies = []
+    for k in range(1, 32):
+        copy = pltpu.make_async_remote_copy(
+            parts.at[me],
+            parts.at[me],
+            send.at[k],
+            r_parts.at[me],
+            device_id=other(k)[1],
+            device_id_type=MESH,
+        )
+        copy.start()
+        copies.append(copy)
+    for k in range(1, 32):
+        device, where = other(k)
+        pltpu.make_async_remote_copy(
+            parts.at[device],
+            parts.at[device],
+            send.at[k],
+            r_parts.at[device],
+            device_id=where,
+            device_id_type=MESH,
+        ).wait_recv()
+    total[...] = jnp.sum(parts[...], 0)
+    for copy in copies:
+        copy.wait_send()
+
+
+def scatter_slots(limits, mats, vecs, loss):
     hbm = pl.BlockSpec(memory_space=pl.ANY)
     tail = PART[1][1]
     return pl.pallas_call(
-        scatter_kernel,
-        out_shape=jax.ShapeDtypeStruct((SLOT, 16, 128), F32),
-        in_specs=[hbm, hbm],
-        out_specs=pl.BlockSpec(memory_space=pltpu.VMEM),
+        functools.partial(scatter_kernel, limits),
+        out_shape=[
+            jax.ShapeDtypeStruct((SLOT, 16, 128), F32),
+            jax.ShapeDtypeStruct((8, 128), F32),
+        ],
+        in_specs=[hbm, hbm, pl.BlockSpec(memory_space=pltpu.VMEM)],
+        out_specs=[pl.BlockSpec(memory_space=pltpu.VMEM)] * 2,
         scratch_shapes=[
             pltpu.VMEM((16, SLOT, 16, 128), BF),
             pltpu.VMEM((8, SLOT, 16, 128), BF),
@@ -1085,17 +1217,19 @@
             pltpu.VMEM((tail, 16, 128), BF),
             pltpu.VMEM((2, DEPTH, PART[0][1], 16, 128), BF),
             pltpu.VMEM((2, DEPTH, 2, tail, 16, 128), BF),
+            pltpu.VMEM((32, 8, 128), F32),
             pltpu.SemaphoreType.DMA((32,)),
-            pltpu.SemaphoreType.DMA((24,)),
+            pltpu.SemaphoreType.DMA((32,)),
             pltpu.SemaphoreType.DMA((8,)),
             pltpu.SemaphoreType.DMA((DEPTH + 1,)),
             pltpu.SemaphoreType.DMA((2, DEPTH, 3)),
+            pltpu.SemaphoreType.DMA((32,)),
         ],
         name="scatter_slots",
         compiler_params=pltpu.CompilerParams(
             collective_id=1, has_side_effects=True, vmem_limit_bytes=VMEM_LIMIT
         ),
-    )(mats, vecs)
+    )(mats, vecs, loss)
 
 
 def piece_table(lines):
@@ -1118,7 +1252,7 @@
                 def step(i, carry):
                     for j in range(width):
                         line = MARGIN + table[piece, 1] + i * (16 * width) + j
-                        run(line, width, table[piece, 3] + i * width + j)
+                        run(line, width, SLOT_V + table[piece, 3] + i * width + j)
                     return carry
 
                 lax.fori_loop(0, table[piece, 2], step, 0)
@@ -1130,7 +1264,7 @@
     copy.start()
     lines[0:MARGIN, :] = jnp.zeros((MARGIN, 128), F32)
     lines[MARGIN + count :, :] = jnp.zeros((MARGIN, 128), F32)
-    out[SLOT_M:] = vec[...].astype(BF).reshape(SLOT_V, 16, 128)
+    out[0:SLOT_V] = vec[...].astype(BF).reshape(SLOT_V, 16, 128)
     copy.wait()
 
     def run(line, width, tile):
@@ -1159,103 +1293,6 @@
     )(table, mat, vec)
 
 
-def unpack_kernel(widths, table, total, loss, grad, vec, part, lines):
-    count = grad.shape[0]
-    lines[...] = jnp.zeros_like(lines)
-
-    def run(line, width, tile):
-        lines[pl.ds(line, 16, stride=width), :] = total[tile]
-
-    each_tile(table, widths, run)
-    vec[...] = total[SLOT_M:].reshape(SLOT_V * 16, 128)
-
-    def square(i, carry):
-        rows = pl.ds(pl.multiple_of(i * 96, 96), 96)
-        value = lines[pl.ds(pl.multiple_of(MARGIN + i * 96, 96), 96), :]
-        grad[rows, :] = value
-        return carry + fold(value * value)
-
-    carry = fold(vec[...] * vec[...])
-    carry = lax.fori_loop(0, count // 96, square, carry)
-    row = lax.broadcasted_iota(jnp.int32, (8, 128), 0)
-    part[...] = jnp.where(row == 0, jnp.sum(carry), loss[...])
-
-
-def unpack(table, widths, count, total, loss):
-    vm = pl.BlockSpec(memory_space=pltpu.VMEM)
-    return pl.pallas_call(
-        functools.partial(unpack_kernel, widths),
-        out_shape=[
-            jax.ShapeDtypeStruct((count, 128), F32),
-            jax.ShapeDtypeStruct((SLOT_V * 16, 128), F32),
-            jax.ShapeDtypeStruct((8, 128), F32),
-        ],
-        in_specs=[pl.BlockSpec(memory_space=pltpu.SMEM), vm, vm],
-        out_specs=[vm, vm, vm],
-        scratch_shapes=[pltpu.VMEM((count + 2 * MARGIN, 128), F32)],
-        name="unpack",
-        compiler_params=pltpu.CompilerParams(vmem_limit_bytes=VMEM_LIMIT),
-    )(table, total, loss)
-
-
-def total_kernel(part, out, parts, send, recv):
-    s, d = lax.axis_index("section"), lax.axis_index("dp")
-    count = parts.shape[0]
-    me = s * 16 + d
-    barrier = pltpu.get_barrier_semaphore()
-
-    def target(k):
-        other = lax.rem(me + k, count)
-        return other, (other // 16, lax.rem(other, 16))
-
-    for k in range(1, count):
-        pl.semaphore_signal(barrier, inc=1, device_id=target(k)[1], device_id_type=MESH)
-    pl.semaphore_wait(barrier, count - 1)
-    sent = []
-    for k in range(1, count):
-        copy = pltpu.make_async_remote_copy(
-            part,
-            parts.at[me],
-            send.at[k],
-            recv.at[me],
-            device_id=target(k)[1],
-            device_id_type=MESH,
-        )
-        copy.start()
-        sent.append(copy)
-    parts[me] = part[...]
-    for k in range(1, count):
-        other = target(k)[0]
-        pltpu.make_async_remote_copy(
-            part,
-            parts.at[other],
-            send.at[k],
-            recv.at[other],
-            device_id=target(k)[1],
-            device_id_type=MESH,
-        ).wait_recv()
-    out[...] = jnp.sum(parts[...], 0)
-    for copy in sent:
-        copy.wait_send()
-
-
-def total_over_all(part):
-    vm = pl.BlockSpec(memory_space=pltpu.VMEM)
-    return pl.pallas_call(
-        total_kernel,
-        out_shape=jax.ShapeDtypeStruct((8, 128), F32),
-        in_specs=[vm],
-        out_specs=vm,
-        scratch_shapes=[
-            pltpu.VMEM((32, 8, 128), F32),
-            pltpu.SemaphoreType.DMA((32,)),
-            pltpu.SemaphoreType.DMA((32,)),
-        ],
-        name="total",
-        compiler_params=pltpu.CompilerParams(collective_id=2, has_side_effects=True),
-    )(part)
-
-
 def clip_factor(square):
     return jnp.minimum(1.0, 0.001 / (jnp.sqrt(square) + 1e-06))
 
@@ -1269,38 +1306,84 @@
     return (master, first, second)
 
 
-def adam_kernel(total, grad, master, first, second, new, new_first, new_second, copy):
+STEPS = 6
+
+
+def update_kernel(widths, table, tiles, total, *refs):
+    states, news, news_vec, (lines, held, fresh, sem_in, sem_out) = (
+        refs[0:3],
+        refs[3:6],
+        refs[6],
+        refs[7:],
+    )
+    count = held.shape[1]
+    size = count // STEPS
+
+    def part(i):
+        return pl.ds(i * size, size)
+
+    loads = [
+        [
+            pltpu.make_async_copy(state.at[part(i)], held.at[n, part(i)], sem_in.at[n, i])
+            for n, state in enumerate(states)
+        ]
+        for i in range(STEPS)
+    ]
+    for step in loads:
+        for copy in step:
+            copy.start()
+    lines[...] = jnp.zeros_like(lines)
+
+    def run(line, width, tile):
+        lines[pl.ds(line, 16, stride=width), :] = tiles[tile]
+
+    each_tile(table, widths, run)
+    news_vec[...] = tiles[0:SLOT_V].reshape(SLOT_V * 16, 128)
     factor = clip_factor(total[0:1, :])
-    step = 104
-
-    def run(i, carry):
-        rows = pl.ds(pl.multiple_of(i * step, 8), step)
-        a, b, c = adam_update(
-            master[rows, :], first[rows, :], second[rows, :], factor * grad[rows, :], 0.05, 0.05
-        )
-        new[rows, :] = a
-        new_first[rows, :] = b
-        new_second[rows, :] = c
-        return carry
-
-    lax.fori_loop(0, grad.shape[0] // step, run, 0)
-    copy[...] = new[...].astype(BF)
-
-
-def adam(total, grad, master, first, second):
-    count = grad.shape[0]
-    size = 624
-    block = pl.BlockSpec((size, 128), lambda i: (i, 0))
+    stores = []
+    for i in range(STEPS):
+        for copy in loads[i]:
+            copy.wait()
+
+        def body(k, carry, i=i):
+            base = i * size + k * 104
+            rows = pl.ds(pl.multiple_of(base, 8), 104)
+            grad = factor * lines[pl.ds(pl.multiple_of(MARGIN + base, 8), 104), :]
+            for n, value in enumerate(
+                adam_update(held[0, rows, :], held[1, rows, :], held[2, rows, :], grad, 0.05, 0.05)
+            ):
+                fresh[n, rows, :] = value
+            return carry
+
+        lax.fori_loop(0, size // 104, body, 0)
+        for n, new in enumerate(news):
+            copy = pltpu.make_async_copy(fresh.at[n, part(i)], new.at[part(i)], sem_out.at[n, i])
+            copy.start()
+            stores.append(copy)
+    for copy in stores:
+        copy.wait()
+
+
+def update(table, widths, tiles, total, states):
+    count = states[0].shape[0]
+    vm = pl.BlockSpec(memory_space=pltpu.VMEM)
+    hbm = pl.BlockSpec(memory_space=pl.ANY)
     shape = jax.ShapeDtypeStruct((count, 128), F32)
     return pl.pallas_call(
-        adam_kernel,
-        grid=(count // size,),
-        out_shape=[shape] * 3 + [jax.ShapeDtypeStruct((count, 128), BF)],
-        in_specs=[pl.BlockSpec((8, 128), lambda i: (0, 0))] + [block] * 4,
-        out_specs=[block] * 4,
-        name="adam",
+        functools.partial(update_kernel, widths),
+        out_shape=[shape] * 3 + [jax.ShapeDtypeStruct((SLOT_V * 16, 128), F32)],
+        in_specs=[pl.BlockSpec(memory_space=pltpu.SMEM), vm, vm] + [hbm] * 3,
+        out_specs=[hbm] * 3 + [vm],
+        scratch_shapes=[
+            pltpu.VMEM((count + 2 * MARGIN, 128), F32),
+            pltpu.VMEM((3, count, 128), F32),
+            pltpu.VMEM((3, count, 128), F32),
+            pltpu.SemaphoreType.DMA((3, STEPS)),
+            pltpu.SemaphoreType.DMA((3, STEPS)),
+        ],
+        name="update",
         compiler_params=pltpu.CompilerParams(vmem_limit_bytes=VMEM_LIMIT),
-    )(total, grad, master, first, second)
+    )(table, tiles, total, *states)
 
 
 def shifted(value, axis, steps):
@@ -1366,18 +1449,19 @@
         table, widths, lines[0], jnp.pad(vec_master[0], (0, room - size)).reshape(-1, 128)
     )
     slots = gather_slots(own)
-    vecs = slots[:, SLOT_M:].reshape(16, room)[:, :size].reshape(-1, 128).astype(F32)
-    inward = [slot_layout(plan, slots.shape) for plan in plans]
+    vecs = slots[:, :SLOT_V].reshape(16, room)[:, :size].reshape(-1, 128).astype(F32)
+    inward = [slot_layout(plan, slots.shape, SLOT_V) for plan in plans]
     outward = [whole_slots(plan, (16, SLOT_M, 16, 128)) for plan in plans]
     dmats, dvec, loss = train(
         images, masked_total, *inward, *outward, pixels, visible, restore, vecs, slots
     )
     dvec = jnp.pad(dvec.reshape(16, size), ((0, 0), (0, room - size))).astype(BF)
-    total = scatter_slots(dmats, dvec.reshape(16, SLOT_V, 16, 128))
-    grad, grad_vec, part = unpack(table, widths, count, total, loss)
-    total = total_over_all(part)
+    tiles, total = scatter_slots(
+        owned_limits(plans), dmats, dvec.reshape(16, SLOT_V, 16, 128), loss
+    )
+    *news, grad_vec = update(table, widths, tiles, total, lines)
+    news = [value.reshape(mat_master.shape) for value in news]
     square, loss_sum = total[0, 0], total[1, 0]
-    news = adam(total, grad, *lines)
     vec_news = adam_update(
         vec_master,
         vec_first,
@@ -1388,7 +1472,8 @@
     )
     return (
         (loss_sum, jnp.sqrt(square))
-        + tuple(value.reshape(mat_master.shape) for value in news)
+        + tuple(news)
+        + (news[0].astype(BF),)
         + tuple(vec_news)
         + (vec_news[0].astype(BF),)
     )

time: 491 us -> 418 us (0.85)
  waiting for transfers between devices: 140 us -> 98 us
  Pallas kernels: 312 us -> 287 us
  local copies, waits for them, and re-layouts: 29.1 us -> 20 us
    ppermute x2, waiting for transfers between devices: 140 us -> 98 us  [shifted(): lax.ppermute(value, axis, [(source, source + steps) for source in range(i...]
    unnamed x17 -> x18, local copies, waits for them, and re-layouts: 13 us -> 3.35 us
    pallas_call x1, Pallas kernels: 33.5 us -> 24.2 us  [encoder_forward(): pl.pallas_call(functools.partial(encoder_forward_kernel, images, layout),...]
    pallas_call x4 -> x2, Pallas kernels: 128 us -> 120 us  [the longest x1 113 us: scatter_slots(): pl.pallas_call(functools.partial(scatter_kernel, limits), out_shape=[jax....]
    pallas_call x1, Pallas kernels: 42.4 us -> 34.6 us  [encoder_backward(): pl.pallas_call(functools.partial(encoder_backward_kernel, images, layout,...]
where the time goes in v3:
time: 418 us; the launch traced here: 417 us
  Pallas kernels  287 us (69%)
  waiting for transfers between devices  98 us (23%)
  local copies, waits for them, and re-layouts  20 us (5%)
  other arithmetic  6.44 us (2%)
    pallas_call x1, Pallas kernels, scatter_slots(): pl.pallas_call(functools.partial(scatter_kernel, limits), out_shape=[jax....  113 us
    pallas_call x1, Pallas kernels, gather_slots(): pl.pallas_call(gather_kernel, out_shape=jax.ShapeDtypeStruct((16, SLOT, 1...  104 us
    ppermute x2, waiting for transfers between devices, shifted(): lax.ppermute(value, axis, [(source, source + steps) for source in range(i...  98 us
    pallas_call x1, Pallas kernels, encoder_backward(): pl.pallas_call(functools.partial(encoder_backward_kernel, images, layout,...  34.6 us
    pallas_call x1, Pallas kernels, encoder_forward(): pl.pallas_call(functools.partial(encoder_forward_kernel, images, layout),...  24.2 us
    another operation x6, local copies, waits for them, and re-layouts  9.17 us
  transfers between devices with their start and end apart: 2, of which 2 were waited for; matrix products, arithmetic and copies ran while one was open for 0% of the time, Pallas kernels for 0%

profile of v3, /device:TPU:0, one launch (start us, length us, event | category | flops | bytes accessed | tf_op | source)
XLA Modules:
  0.0 417.3 jit_solution(13009169892608934243)
XLA Ops:
  0.7 0.7 pad.22
  1.3 0.1 reshape.77
  1.4 1.4 pad_bitcast_fusion.1.vec
  2.8 2.4 copy.23
  5.3 1.2 dynamic-slice_bitcast_fusion.table
  6.5 3.7 pack.1.own
  10.2 104.5 %gather_slots.1 = bf16[16,269,16,128]{3,2,1,0:T(8,128)(2,1)} custom-call(bf16[269,16,128]{2,1,0:T(8,128)(2,1)} %pack.1.own), custom_call_target="tpu_custom_call" | custom-call | tf_op jit(solution)/shard_map/gather_slots/pallas_call | solution.py:930
  114.7 0.0 copy-start
  114.7 1.1 slice.15
  115.8 0.1 copy.29
  116.0 0.3 reshape.93
  116.3 0.0 copy-done
  116.3 1.1 pad.23
  117.4 0.0 copy-start.6
  117.4 25.0 %conditional.3 = ((bf16[256,768]{1,0:T(8,128)(2,1)}, bf16[256,768]{1,0:T(8,128)(2,1)}, f32[256,768]{1,0:T(8,128)}, bf16[256,768]{1,0:T(8,128)(2,1)}, bf16[256,23...) conditional(s32[]{:T(128)} %convert_element_type.32, () %tuple.28, ...), branch_computations={%region_0.1_spmd, %region_1.2_spmd} | conditional | bytes 10223742 | solution.py:1402
  117.4 0.8 copy.24.vis
  118.2 24.2 %encoder_forward.1 = (bf16[256,768]{1,0:T(8,128)(2,1)}, bf16[256,768]{1,0:T(8,128)(2,1)}, f32[256,768]{1,0:T(8,128)}, bf16[256,768]{1,0:T(8,128)(2,1)}, bf16[256...) custom-call(s32[256,1]{1,0:T(8,128)} %copy.24.vis, ...), custom_call_target="tpu_custom_call" | custom-call | tf_op jit(solution)/shard_map/cond/branch_1_fun/encoder_forward/pallas_call | solution.py:550
  142.4 2.1 collective-permute-start
  144.5 8.8 %collective-permute-done = bf16[256,768]{1,0:T(8,128)(2,1)} collective-permute-done((bf16[256,768]{1,0:T(8,128)(2,1)}, bf16[256,768]{1,0:T(8,128)(2,1)}, u32[]{:S(2)}, u32[]{:S(2)}) %collective-permute-start) | collective-permute-done | bytes 393248 | tf_op jit(solution)/shard_map/ppermute | solution.py:1392
  153.3 0.0 copy-done.6
  153.3 7.6 %conditional.4 = (bf16[256,768]{1,0:T(8,128)(2,1)}, f32[8,128]{1,0:T(8,128)}, bf16[16,264,16,128]{3,2,1,0:T(8,128)(2,1)}, bf16[1272,128]{1,0:T(8,128)(2,1)S(1)}) conditional(s32[]{:T(128)} %convert_element_type.32, (s32[4,196]{1,0:T(4,128)S(1)}, bf16[256,768]{1,0:T(8,128)(2,1)}, bf16[4,208,768]{2,1,0:T(8,128)(2,1)}, f32[1272,128]{1,0:T(8,128)S(1)}, ...), branch_computations={%region_2.3_spmd, %region_3.4_spmd} | conditional | flops 162816 | bytes 18024492 | solution.py:1408
  153.3 0.6 broadcast.19
  153.9 0.8 broadcast.18
  154.7 6.2 %broadcast.20 = bf16[16,264,16,128]{3,2,1,0:T(8,128)(2,1)} broadcast(bf16[]{:T(256)} %constant.18.clone), dimensions={} | broadcast | bytes 17301506 | tf_op jit(solution)/shard_map/broadcast.9
  160.9 1.3 collective-permute-start.1
  162.1 89.2 %collective-permute-done.1 = bf16[256,768]{1,0:T(8,128)(2,1)} collective-permute-done((bf16[256,768]{1,0:T(8,128)(2,1)}, bf16[256,768]{1,0:T(8,128)(2,1)}, u32[]{:S(2)}, u32[]{:S(2)}) %collective-permute-start.1) | collective-permute-done | bytes 393248 | tf_op jit(solution)/shard_map/ppermute | solution.py:1392
  251.3 36.5 %conditional.5 = ((bf16[16,264,16,128]{3,2,1,0:T(8,128)(2,1)}, bf16[1272,128]{1,0:T(8,128)(2,1)S(1)})) conditional(s32[]{:T(128)} %convert_element_type.32, (bf16[16,264,16,128]{3,2,1,0:T(8,128)(2,1)}, bf16[1272,128]{1,0:T(8,128)(2,1)S(1)}) %tuple.32, (s32[256,1]{0,1:T(1,128)S(1)}, f32[1272,128]{1,0:T(8,128)S(1)}, bf16[256,768]{1,0:T(8,128)(2,1)}, ...), branch_computations={%region_4.5_spmd, %region_5.6_spmd} | conditional | flops 162816 | bytes 978968 | solution.py:1428
  251.3 0.8 copy.25.vis
  252.1 34.6 %encoder_backward.1 = (bf16[16,264,16,128]{3,2,1,0:T(8,128)(2,1)}, f32[1272,128]{1,0:T(8,128)}) custom-call(s32[256,1]{1,0:T(8,128)} %copy.25.vis, f32[1272,128]{1,0:T(8,128)S(1)} %get-tuple-element.63.vec, bf16[256,768]{1,0:T(8,128)(2,1)} %get-tuple-element.64.dlatent, bf16[256,768]{1,0:T(8,128)(2,1)} %get-tuple-element.65.refs_0_, ...), custom_call_target="tpu_custom_call" | custom-call | tf_op jit(solution)/shard_map/cond/branch_1_fun/encoder_backward/pallas_call | solution.py:604
  286.7 1.1 convert.10
  287.8 0.0 copy-start.5
  287.9 0.3 reshape.94
  288.2 0.8 copy.27
  289.0 0.0 copy-done.5
  289.0 112.9 %scatter_slots.1 = (f32[269,16,128]{2,1,0:T(8,128)}, f32[8,128]{1,0:T(8,128)}) custom-call(bf16[16,264,16,128]{3,2,1,0:T(8,128)(2,1)} %get-tuple-element.157.mats, bf16[16,5,16,128]{3,2,1,0:T(8,128)(2,1)} %bitcast.31, f32[8,128]{1,0:T(8,128)S(1)} %copy-done.5), custom_call_target="tpu_custom_call" | custom-call | tf_op jit(solution)/shard_map/scatter_slots/pallas_call | solution.py:1205
  401.9 1.3 fusion.3
  403.8 6.9 %update.1 = (f32[3744,128]{1,0:T(8,128)}, f32[3744,128]{1,0:T(8,128)}, f32[3744,128]{1,0:T(8,128)}, f32[80,128]{1,0:T(8,128)}) custom-call(s32[2,4]{1,0:T(2,128)} %dynamic-slice_bitcast_fusion.table, f32[269,16,128]{2,1,0:T(8,128)} %get-tuple-element.127.tiles, f32[8,128]{1,0:T(8,128)} %get-tuple-element.126.total, f32[3744,128]{1,0:T(8,128)} %bitcast.24, ...), custom_call_target="tpu_custom_call" | custom-call | tf_op jit(solution)/shard_map/update/pallas_call | solution.py:1372
  410.7 0.0 copy-start.1
  410.7 0.0 copy-start.2
  410.8 0.0 copy-start.3
  410.8 0.0 copy-start.4
  410.8 4.3 %convert_element_type.35 = bf16[1,479232]{1,0:T(2,128)(2,1)} convert(f32[1,479232]{1,0:T(1,128)} %bitcast.27) | non-fusion elementwise | flops 479232 | bytes 2875392 | tf_op jit(solution)/shard_map/convert_element_type | solution.py:1476
  415.2 0.0 copy-done.1
  415.2 0.0 copy-done.2
  415.2 0.0 copy-done.3
  415.2 0.0 copy-done.4
  415.2 1.0 fusion.1
  (3 shorter events, 0.1 us)
Async XLA Ops:
  114.7 1.5 copy-start
  117.4 35.9 %copy-start.6 = (s32[4,196]{1,0:T(4,128)S(1)}, s32[4,196]{1,0:T(4,128)}, u32[]{:S(2)}) copy-start(s32[4,196]{1,0:T(4,128)} %param.18) | copy-start | bytes 9412
  142.4 10.8 %collective-permute-start = (bf16[256,768]{1,0:T(8,128)(2,1)}, bf16[256,768]{1,0:T(8,128)(2,1)}, u32[]{:S(2)}, u32[]{:S(2)}) collective-permute-start(bf16[256,768]{1,0:T(8,128)(2,1)} %get-tuple-element.109), channel_id=1, source_target_pairs={{0,16},{1,17},{2,18},{3,19},{4,20},{5,21},{6,22},{7,23},{8,24},{9,... | collective-permute-start | bytes 1179656 | tf_op jit(solution)/shard_map/ppermute | solution.py:1392
  160.9 90.5 %collective-permute-start.1 = (bf16[256,768]{1,0:T(8,128)(2,1)}, bf16[256,768]{1,0:T(8,128)(2,1)}, u32[]{:S(2)}, u32[]{:S(2)}) collective-permute-start(bf16[256,768]{1,0:T(8,128)(2,1)} %get-tuple-element.112), channel_id=1, source_target_pairs={{16,0},{17,1},{18,2},{19,3},{20,4},{21,5},{22,6},{23,7},{24,8},{25... | collective-permute-start | bytes 1179656 | tf_op jit(solution)/shard_map/ppermute | solution.py:1392
  287.8 1.1 copy-start.5
  410.7 4.4 %copy-start.1 = (f32[1,10176]{1,0:T(1,128)S(1)}, f32[1,10176]{1,0:T(1,128)}, u32[]{:S(2)}) copy-start(f32[1,10176]{1,0:T(1,128)} %param.22) | copy-start | bytes 122116
  410.7 4.4 %copy-start.2 = (f32[1,10176]{1,0:T(1,128)S(1)}, f32[1,10176]{1,0:T(1,128)}, u32[]{:S(2)}) copy-start(f32[1,10176]{1,0:T(1,128)} %param.23) | copy-start | bytes 122116
  410.8 4.4 %copy-start.3 = (f32[1,10176]{1,0:T(1,128)S(1)}, f32[1,10176]{1,0:T(1,128)}, u32[]{:S(2)}) copy-start(f32[1,10176]{1,0:T(1,128)} %param.24) | copy-start | bytes 122116
  410.8 4.4 %copy-start.4 = (f32[80,128]{1,0:T(8,128)S(1)}, f32[80,128]{1,0:T(8,128)}, u32[]{:S(2)}) copy-start(f32[80,128]{1,0:T(8,128)} %get-tuple-element.131) | copy-start | bytes 122884

commit v4 on v3

--- a/solution.py
+++ b/solution.py
@@ -793,7 +793,22 @@
 DEPTH, WIDTH = 4, 2
 SLOT_M, SLOT_V = 264, 5
 SLOT = SLOT_M + SLOT_V
-PART = ((0, 224), (224, SLOT - 224))
+SIZES = (249, 261, 269, 239)
+FIRST_Z = 4
+PARTS = FIRST_Z + 1
+
+
+def cut_of(depth, part):
+    size = SIZES[depth]
+    tail = size // 6
+    if part == FIRST_Z:
+        return size - tail, tail
+    low, high = ((size - tail) * n // FIRST_Z for n in (part, part + 1))
+    return low, high - low
+
+
+MOST = max(SIZES[z] - SIZES[z] // 6 for z in range(DEPTH))
+TAIL = max(SIZES[z] // 6 for z in range(DEPTH))
 MARGIN = 384
 LINES = 3744
 
@@ -854,70 +869,72 @@
     def run(s, z, y, c):
         around = devices_around(z, y, c, s)
         greet(around)
-        slot = lambda zz, yy, cc: zz * 4 + yy * 2 + cc
         sent = []
 
-        def at(ref, index, part):
-            start, count = PART[part]
-            return ref.at[index, pl.ds(start, count)]
-
-        def push(index, part, targets, mine=False):
-            start, count = PART[part]
+        def slot(zz, yy, cc):
+            return zz * 4 + yy * 2 + cc
+
+        def at(zz, yy, cc, part):
+            return out.at[slot(zz, yy, cc), pl.ds(*cut_of(zz, part))]
+
+        def push(zz, yy, part, targets, mine=False):
+            target = at(zz, yy, c, part)
             for name in targets:
                 if name not in around:
                     continue
                 copy = pltpu.make_async_remote_copy(
-                    own.at[pl.ds(start, count)] if mine else at(out, index, part),
-                    at(out, index, part),
+                    own.at[pl.ds(*cut_of(z, part))] if mine else target,
+                    target,
                     send.at[len(sent)],
-                    recv.at[index, part],
+                    recv.at[slot(zz, yy, c), part],
                     device_id=around[name],
                     device_id_type=MESH,
                 )
                 copy.start()
                 sent.append(copy)
 
-        def arrive(index, part):
+        def arrive(zz, yy, cc, part):
+            target = at(zz, yy, cc, part)
             pltpu.make_async_remote_copy(
-                at(out, index, part),
-                at(out, index, part),
+                target,
+                target,
                 send.at[0],
-                recv.at[index, part],
+                recv.at[slot(zz, yy, cc), part],
                 device_id=around["core"],
                 device_id_type=MESH,
             ).wait_recv()
 
-        me = slot(z, y, c)
-        push(me, 1, ["side"], True)
-        push(me, 0, ["up", "down", "side"], True)
-        push(me, 1, ["up", "down"], True)
-        push(me, 0, ["core"], True)
-        push(me, 1, ["core"], True)
-        keep = pltpu.make_async_copy(own, out.at[me], local)
+        tail = FIRST_Z
+        push(z, y, tail, ["side"], True)
+        for part in range(FIRST_Z):
+            push(z, y, part, ["up", "down", "side"], True)
+        push(z, y, tail, ["up", "down"], True)
+        for part in range(PARTS):
+            push(z, y, part, ["core"], True)
+        keep = pltpu.make_async_copy(own, out.at[slot(z, y, c)], local)
         keep.start()
-        arrive(slot(z, 1 - y, c), 1)
-        push(slot(z, 1 - y, c), 1, ["up", "down", "core"])
-        for k in range(1, DEPTH):
-            for zz in (z - k, z + k):
-                if 0 <= zz < DEPTH:
-                    onward = "up" if zz < z else "down"
-                    arrive(slot(zz, y, c), 0)
-                    push(slot(zz, y, c), 0, [onward, "side", "core"])
-                    for yy in (y, 1 - y):
-                        arrive(slot(zz, yy, c), 1)
-                        push(slot(zz, yy, c), 1, [onward, "core"])
-            for zz in sorted({z - k + 1, z + k - 1}):
-                if 0 <= zz < DEPTH:
-                    arrive(slot(zz, 1 - y, c), 0)
-                    push(slot(zz, 1 - y, c), 0, ["core"])
-        for zz in (z - DEPTH + 1, z + DEPTH - 1):
-            if 0 <= zz < DEPTH:
-                arrive(slot(zz, 1 - y, c), 0)
-                push(slot(zz, 1 - y, c), 0, ["core"])
+        arrive(z, 1 - y, c, tail)
+        push(z, 1 - y, tail, ["up", "down", "core"])
+        waiting = [z]
+        for k in range(1, DEPTH + 1):
+            near = [zz for zz in (z - k, z + k) if 0 <= zz < DEPTH]
+            for part in range(FIRST_Z):
+                for zz in near:
+                    arrive(zz, y, c, part)
+                    push(zz, y, part, ["up" if zz < z else "down", "side", "core"])
+            for zz in near:
+                for yy in (y, 1 - y):
+                    arrive(zz, yy, c, tail)
+                    push(zz, yy, tail, ["up" if zz < z else "down", "core"])
+            for part in range(FIRST_Z):
+                for zz in waiting:
+                    arrive(zz, 1 - y, c, part)
+                    push(zz, 1 - y, part, ["core"])
+            waiting = near
         for zz in range(DEPTH):
             for yy in range(WIDTH):
-                for part in range(2):
-                    arrive(slot(zz, yy, 1 - c), part)
+                for part in range(PARTS):
+                    arrive(zz, yy, 1 - c, part)
         keep.wait()
         for copy in sent:
             copy.wait_send()
@@ -933,8 +950,8 @@
         in_specs=[hbm],
         out_specs=hbm,
         scratch_shapes=[
-            pltpu.SemaphoreType.DMA((48,)),
-            pltpu.SemaphoreType.DMA((16, 2)),
+            pltpu.SemaphoreType.DMA((128,)),
+            pltpu.SemaphoreType.DMA((16, PARTS)),
             pltpu.SemaphoreType.DMA,
         ],
         name="gather_slots",
@@ -1068,9 +1085,8 @@
             copy.start()
             sent.append(copy)
 
-        def cut(index, part):
-            start, count = PART[part]
-            return held.at[index, pl.ds(start, count)]
+        def cut(zz, yy, part):
+            return held.at[slot(zz, yy, c), pl.ds(*cut_of(zz, part))]
 
         def arrive(target, sem):
             pltpu.make_async_remote_copy(
@@ -1083,8 +1099,8 @@
                 for copy in loads[n]:
                     copy.wait()
                 push(
-                    held.at[slot(zz, yy, 1 - c)],
-                    core_in.at[zz * 2 + yy],
+                    held.at[slot(zz, yy, 1 - c), pl.ds(0, SIZES[zz])],
+                    core_in.at[zz * 2 + yy, pl.ds(0, SIZES[zz])],
                     r_core.at[zz * 2 + yy],
                     "core",
                 )
@@ -1098,74 +1114,72 @@
             yy = 1 - y if flip else y
             for copy in loads[8 + order.index(zz) * 2 + (0 if flip else 1)]:
                 copy.wait()
-            arrive(core_in.at[zz * 2 + yy], r_core.at[zz * 2 + yy])
+            arrive(core_in.at[zz * 2 + yy, pl.ds(0, SIZES[zz])], r_core.at[zz * 2 + yy])
+
+        tail = FIRST_Z
 
         def z_in(part, way, zz, yy):
-            if part == 0:
-                return z_a.at[way, zz], r_z.at[way, zz, 2]
-            return z_b.at[way, zz, yy], r_z.at[way, zz, yy]
-
-        def side_sources(zz, yy):
+            start, count = cut_of(zz, part)
+            if part < tail:
+                return z_a.at[way, zz, pl.ds(start, count)], r_z.at[way, zz, part]
+            return z_b.at[way, zz, yy, pl.ds(0, count)], r_z.at[way, zz, tail + yy]
+
+        def side_in(zz, part):
+            start, count = cut_of(zz, part)
+            if part < tail:
+                return side_a.at[zz, pl.ds(start, count)], r_side.at[zz, part]
+            return side_b.at[pl.ds(0, count)], r_side.at[zz, tail]
+
+        def came(zz, part, pair):
+            arrive(*pair)
+            return Shifted(pair[0], cut_of(zz, part)[0])
+
+        def core_sources(zz, yy):
             return [held.at[slot(zz, yy, c)], core_in.at[zz * 2 + yy]]
-
-        for zz in order:
-            prepare(zz, True)
-            index = slot(zz, 1 - y, c)
-            add_tiles(held.at[index], side_sources(zz, 1 - y), *PART[0])
-            push(cut(index, 0), side_a.at[zz], r_side.at[zz], "side")
 
         def along(part, zz, flip):
             yy = 1 - y if flip else y
             prepare(zz, flip)
-            index = slot(zz, yy, c)
             way, name, first = (0, "up", 0) if zz > z else (1, "down", DEPTH - 1)
-            sources = side_sources(zz, yy)
-            if part == 0:
-                arrive(side_a.at[zz], r_side.at[zz])
-                sources.append(side_a.at[zz])
+            sources = core_sources(zz, yy)
+            if part < tail:
+                sources.append(came(zz, part, side_in(zz, part)))
             if z != first:
-                ref, sem = z_in(part, way, zz, yy)
-                arrive(ref, sem)
-                sources.append(ref if part == 0 else Shifted(ref, PART[1][0]))
-            add_tiles(held.at[index], sources, *PART[part])
-            ref, sem = z_in(part, way, zz, yy)
-            push(cut(index, part), ref, sem, name)
+                sources.append(came(zz, part, z_in(part, way, zz, yy)))
+            add_tiles(held.at[slot(zz, yy, c)], sources, *cut_of(zz, part))
+            push(cut(zz, yy, part), *z_in(part, way, zz, yy), name)
 
         def gathered(part, yy):
-            found = []
-            for way, here in ((0, z > 0), (1, z < DEPTH - 1)):
-                if here:
-                    ref, sem = z_in(part, way, z, yy)
-                    arrive(ref, sem)
-                    found.append(ref if part == 0 else Shifted(ref, PART[1][0]))
-            return found
-
+            return [
+                came(z, part, z_in(part, way, z, yy))
+                for way, here in ((0, z > 0), (1, z < DEPTH - 1))
+                if here
+            ]
+
+        for zz in order:
+            prepare(zz, True)
+            for part in range(tail):
+                add_tiles(held.at[slot(zz, 1 - y, c)], core_sources(zz, 1 - y), *cut_of(zz, part))
+                push(cut(zz, 1 - y, part), *side_in(zz, part), "side")
+            if zz != z:
+                along(tail, zz, True)
+                along(tail, zz, False)
+        prepare(z, False)
+        add_tiles(
+            held.at[slot(z, 1 - y, c)],
+            core_sources(z, 1 - y) + gathered(tail, 1 - y),
+            *cut_of(z, tail),
+        )
+        push(cut(z, 1 - y, tail), *side_in(z, tail), "side")
         for zz in order[:-1]:
-            along(1, zz, True)
-            along(1, zz, False)
-        prepare(z, False)
-        index = slot(z, 1 - y, c)
-        add_tiles(held.at[index], side_sources(z, 1 - y) + gathered(1, 1 - y), *PART[1])
-        push(cut(index, 1), side_b, r_side.at[DEPTH], "side")
-        for zz in order[:-1]:
-            along(0, zz, False)
-        arrive(side_b, r_side.at[DEPTH])
+            for part in range(tail):
+                along(part, zz, False)
         owned = [sum(jnp.where(me == k, row[n], 0) for k, row in enumerate(limits)) for n in range(5)]
-        square = finish_tiles(
-            out,
-            side_sources(z, y) + gathered(1, y) + [Shifted(side_b, PART[1][0])],
-            *PART[1],
-            owned,
-            jnp.zeros((8, 128), F32),
-        )
-        arrive(side_a.at[z], r_side.at[z])
-        square = finish_tiles(
-            out,
-            side_sources(z, y) + [side_a.at[z]] + gathered(0, y),
-            *PART[0],
-            owned,
-            square,
-        )
+        square = jnp.zeros((8, 128), F32)
+        for part in (tail,) + tuple(range(tail)):
+            sources = core_sources(z, y) + gathered(part, y)
+            sources.append(came(z, part, side_in(z, part)))
+            square = finish_tiles(out, sources, *cut_of(z, part), owned, square)
         row = lax.broadcasted_iota(jnp.int32, (8, 128), 0)
         parts[me] = jnp.where(row == 0, jnp.sum(square), loss[...])
         for copy in sent:
@@ -1201,7 +1215,6 @@
 
 def scatter_slots(limits, mats, vecs, loss):
     hbm = pl.BlockSpec(memory_space=pl.ANY)
-    tail = PART[1][1]
     return pl.pallas_call(
         functools.partial(scatter_kernel, limits),
         out_shape=[
@@ -1213,16 +1226,16 @@
         scratch_shapes=[
             pltpu.VMEM((16, SLOT, 16, 128), BF),
             pltpu.VMEM((8, SLOT, 16, 128), BF),
-            pltpu.VMEM((DEPTH, PART[0][1], 16, 128), BF),
-            pltpu.VMEM((tail, 16, 128), BF),
-            pltpu.VMEM((2, DEPTH, PART[0][1], 16, 128), BF),
-            pltpu.VMEM((2, DEPTH, 2, tail, 16, 128), BF),
+            pltpu.VMEM((DEPTH, MOST, 16, 128), BF),
+            pltpu.VMEM((TAIL, 16, 128), BF),
+            pltpu.VMEM((2, DEPTH, MOST, 16, 128), BF),
+            pltpu.VMEM((2, DEPTH, 2, TAIL, 16, 128), BF),
             pltpu.VMEM((32, 8, 128), F32),
             pltpu.SemaphoreType.DMA((32,)),
-            pltpu.SemaphoreType.DMA((32,)),
+            pltpu.SemaphoreType.DMA((64,)),
             pltpu.SemaphoreType.DMA((8,)),
-            pltpu.SemaphoreType.DMA((DEPTH + 1,)),
-            pltpu.SemaphoreType.DMA((2, DEPTH, 3)),
+            pltpu.SemaphoreType.DMA((DEPTH, PARTS)),
+            pltpu.SemaphoreType.DMA((2, DEPTH, PARTS + 1)),
             pltpu.SemaphoreType.DMA((32,)),
         ],
         name="scatter_slots",

time: 418 us -> 395 us (0.945); the launches traced: 417 us -> 388 us
  Pallas kernels: 287 us -> 257 us
  loops' own time: 0.02 us -> 8.28 us
  waiting for transfers between devices: 98 us -> 89.8 us
    pallas_call x1, Pallas kernels: 113 us -> 97.4 us  [scatter_slots(): pl.pallas_call(functools.partial(scatter_kernel, limits), out_shape=[jax....]
    pallas_call x1, Pallas kernels: 104 us -> 89.8 us  [gather_slots(): pl.pallas_call(gather_kernel, out_shape=jax.ShapeDtypeStruct((16, SLOT, 1...]
    another operation x1, loops' own time: 0.01 us -> 8.27 us  [train(): lax.cond(encoding, lambda: [blank_latent, jnp.zeros((8, 128), F32), jnp.z...]
    ppermute x2, waiting for transfers between devices: 98 us -> 89.8 us  [shifted(): lax.ppermute(value, axis, [(source, source + steps) for source in range(i...]
where the time goes in v4:
time: 395 us; the launch traced here: 388 us
  Pallas kernels  257 us (65%)
  waiting for transfers between devices  89.8 us (23%)
  local copies, waits for them, and re-layouts  20 us (5%)
  loops' own time  8.28 us (2%)
  other arithmetic  6.44 us (2%)
    pallas_call x1, Pallas kernels, scatter_slots(): pl.pallas_call(functools.partial(scatter_kernel, limits), out_shape=[jax....  97.4 us
    ppermute x2, waiting for transfers between devices, shifted(): lax.ppermute(value, axis, [(source, source + steps) for source in range(i...  89.8 us
    pallas_call x1, Pallas kernels, gather_slots(): pl.pallas_call(gather_kernel, out_shape=jax.ShapeDtypeStruct((16, SLOT, 1...  89.8 us
    pallas_call x1, Pallas kernels, encoder_backward(): pl.pallas_call(functools.partial(encoder_backward_kernel, images, layout,...  34.6 us
    pallas_call x1, Pallas kernels, encoder_forward(): pl.pallas_call(functools.partial(encoder_forward_kernel, images, layout),...  24.2 us
    another operation x6, local copies, waits for them, and re-layouts  9.17 us
    another operation x1, loops' own time, train(): lax.cond(encoding, lambda: [blank_latent, jnp.zeros((8, 128), F32), jnp.z...  8.27 us
  transfers between devices with their start and end apart: 2, of which 2 were waited for; matrix products, arithmetic and copies ran while one was open for 0% of the time, Pallas kernels for 0%

profile of v4, /device:TPU:0, one launch (start us, length us, event | category | flops | bytes accessed | tf_op | source)
XLA Modules:
  0.0 387.6 jit_solution(16595040885022030804)
XLA Ops:
  0.7 0.7 pad.22
  1.3 0.1 reshape.77
  1.4 1.4 pad_bitcast_fusion.1.vec
  2.8 2.4 copy.23
  5.3 1.2 dynamic-slice_bitcast_fusion.table
  6.5 3.7 pack.1.own
  10.2 89.8 %gather_slots.1 = bf16[16,269,16,128]{3,2,1,0:T(8,128)(2,1)} custom-call(bf16[269,16,128]{2,1,0:T(8,128)(2,1)} %pack.1.own), custom_call_target="tpu_custom_call" | custom-call | tf_op jit(solution)/shard_map/gather_slots/pallas_call | solution.py:947
  100.0 0.0 copy-start
  100.0 1.1 slice.15
  101.1 0.1 copy.29
  101.3 0.3 reshape.93
  101.5 0.0 copy-done
  101.5 1.1 pad.23
  102.7 0.0 copy-start.6
  102.7 25.0 %conditional.3 = ((bf16[256,768]{1,0:T(8,128)(2,1)}, bf16[256,768]{1,0:T(8,128)(2,1)}, f32[256,768]{1,0:T(8,128)}, bf16[256,768]{1,0:T(8,128)(2,1)}, bf16[256,23...) conditional(s32[]{:T(128)} %convert_element_type.32, () %tuple.28, ...), branch_computations={%region_0.1_spmd, %region_1.2_spmd} | conditional | bytes 10223742 | solution.py:1415
  102.7 0.8 copy.24.vis
  103.5 24.2 %encoder_forward.1 = (bf16[256,768]{1,0:T(8,128)(2,1)}, bf16[256,768]{1,0:T(8,128)(2,1)}, f32[256,768]{1,0:T(8,128)}, bf16[256,768]{1,0:T(8,128)(2,1)}, bf16[256...) custom-call(s32[256,1]{1,0:T(8,128)} %copy.24.vis, ...), custom_call_target="tpu_custom_call" | custom-call | tf_op jit(solution)/shard_map/cond/branch_1_fun/encoder_forward/pallas_call | solution.py:550
  127.7 2.1 collective-permute-start
  129.8 8.8 %collective-permute-done = bf16[256,768]{1,0:T(8,128)(2,1)} collective-permute-done((bf16[256,768]{1,0:T(8,128)(2,1)}, bf16[256,768]{1,0:T(8,128)(2,1)}, u32[]{:S(2)}, u32[]{:S(2)}) %collective-permute-start) | collective-permute-done | bytes 393248 | tf_op jit(solution)/shard_map/ppermute | solution.py:1405
  138.6 0.0 copy-done.6
  138.6 15.8 %conditional.4 = (bf16[256,768]{1,0:T(8,128)(2,1)}, f32[8,128]{1,0:T(8,128)}, bf16[16,264,16,128]{3,2,1,0:T(8,128)(2,1)}, bf16[1272,128]{1,0:T(8,128)(2,1)S(1)}) conditional(s32[]{:T(128)} %convert_element_type.32, (s32[4,196]{1,0:T(4,128)S(1)}, bf16[256,768]{1,0:T(8,128)(2,1)}, bf16[4,208,768]{2,1,0:T(8,128)(2,1)}, f32[1272,128]{1,0:T(8,128)S(1)}, ...), branch_computations={%region_2.3_spmd, %region_3.4_spmd} | conditional | flops 162816 | bytes 18024492 | solution.py:1421
  146.9 0.6 broadcast.19
  147.5 0.8 broadcast.18
  148.3 6.2 %broadcast.20 = bf16[16,264,16,128]{3,2,1,0:T(8,128)(2,1)} broadcast(bf16[]{:T(256)} %constant.18.clone), dimensions={} | broadcast | bytes 17301506 | tf_op jit(solution)/shard_map/broadcast.9
  154.4 1.3 collective-permute-start.1
  155.7 81.0 %collective-permute-done.1 = bf16[256,768]{1,0:T(8,128)(2,1)} collective-permute-done((bf16[256,768]{1,0:T(8,128)(2,1)}, bf16[256,768]{1,0:T(8,128)(2,1)}, u32[]{:S(2)}, u32[]{:S(2)}) %collective-permute-start.1) | collective-permute-done | bytes 393248 | tf_op jit(solution)/shard_map/ppermute | solution.py:1405
  236.7 36.5 %conditional.5 = ((bf16[16,264,16,128]{3,2,1,0:T(8,128)(2,1)}, bf16[1272,128]{1,0:T(8,128)(2,1)S(1)})) conditional(s32[]{:T(128)} %convert_element_type.32, (bf16[16,264,16,128]{3,2,1,0:T(8,128)(2,1)}, bf16[1272,128]{1,0:T(8,128)(2,1)S(1)}) %tuple.32, (s32[256,1]{0,1:T(1,128)S(1)}, f32[1272,128]{1,0:T(8,128)S(1)}, bf16[256,768]{1,0:T(8,128)(2,1)}, ...), branch_computations={%region_4.5_spmd, %region_5.6_spmd} | conditional | flops 162816 | bytes 978968 | solution.py:1441
  236.7 0.8 copy.25.vis
  237.5 34.6 %encoder_backward.1 = (bf16[16,264,16,128]{3,2,1,0:T(8,128)(2,1)}, f32[1272,128]{1,0:T(8,128)}) custom-call(s32[256,1]{1,0:T(8,128)} %copy.25.vis, f32[1272,128]{1,0:T(8,128)S(1)} %get-tuple-element.63.vec, bf16[256,768]{1,0:T(8,128)(2,1)} %get-tuple-element.64.dlatent, bf16[256,768]{1,0:T(8,128)(2,1)} %get-tuple-element.65.refs_0_, ...), custom_call_target="tpu_custom_call" | custom-call | tf_op jit(solution)/shard_map/cond/branch_1_fun/encoder_backward/pallas_call | solution.py:604
  272.1 1.1 convert.10
  273.2 0.0 copy-start.5
  273.2 0.3 reshape.94
  273.6 0.8 copy.27
  274.3 0.0 copy-done.5
  274.3 97.4 %scatter_slots.1 = (f32[269,16,128]{2,1,0:T(8,128)}, f32[8,128]{1,0:T(8,128)}) custom-call(bf16[16,264,16,128]{3,2,1,0:T(8,128)(2,1)} %get-tuple-element.157.mats, bf16[16,5,16,128]{3,2,1,0:T(8,128)(2,1)} %bitcast.31, f32[8,128]{1,0:T(8,128)S(1)} %copy-done.5), custom_call_target="tpu_custom_call" | custom-call | tf_op jit(solution)/shard_map/scatter_slots/pallas_call | solution.py:1218
  371.7 1.3 fusion.3
  373.7 6.9 %update.1 = (f32[3744,128]{1,0:T(8,128)}, f32[3744,128]{1,0:T(8,128)}, f32[3744,128]{1,0:T(8,128)}, f32[80,128]{1,0:T(8,128)}) custom-call(s32[2,4]{1,0:T(2,128)} %dynamic-slice_bitcast_fusion.table, f32[269,16,128]{2,1,0:T(8,128)} %get-tuple-element.127.tiles, f32[8,128]{1,0:T(8,128)} %get-tuple-element.126.total, f32[3744,128]{1,0:T(8,128)} %bitcast.24, ...), custom_call_target="tpu_custom_call" | custom-call | tf_op jit(solution)/shard_map/update/pallas_call | solution.py:1385
  380.6 0.0 copy-start.1
  380.6 0.0 copy-start.2
  380.6 0.0 copy-start.3
  380.6 0.0 copy-start.4
  380.7 4.3 %convert_element_type.35 = bf16[1,479232]{1,0:T(2,128)(2,1)} convert(f32[1,479232]{1,0:T(1,128)} %bitcast.27) | non-fusion elementwise | flops 479232 | bytes 2875392 | tf_op jit(solution)/shard_map/convert_element_type | solution.py:1489
  385.0 0.0 copy-done.1
  385.0 0.0 copy-done.2
  385.0 0.0 copy-done.3
  385.1 0.0 copy-done.4
  385.1 1.0 fusion.1
  (3 shorter events, 0.1 us)
Async XLA Ops:
  100.0 1.5 copy-start
  102.7 35.9 %copy-start.6 = (s32[4,196]{1,0:T(4,128)S(1)}, s32[4,196]{1,0:T(4,128)}, u32[]{:S(2)}) copy-start(s32[4,196]{1,0:T(4,128)} %param.18) | copy-start | bytes 9412
  127.7 10.9 %collective-permute-start = (bf16[256,768]{1,0:T(8,128)(2,1)}, bf16[256,768]{1,0:T(8,128)(2,1)}, u32[]{:S(2)}, u32[]{:S(2)}) collective-permute-start(bf16[256,768]{1,0:T(8,128)(2,1)} %get-tuple-element.109), channel_id=1, source_target_pairs={{0,16},{1,17},{2,18},{3,19},{4,20},{5,21},{6,22},{7,23},{8,24},{9,... | collective-permute-start | bytes 1179656 | tf_op jit(solution)/shard_map/ppermute | solution.py:1405
  154.4 82.2 %collective-permute-start.1 = (bf16[256,768]{1,0:T(8,128)(2,1)}, bf16[256,768]{1,0:T(8,128)(2,1)}, u32[]{:S(2)}, u32[]{:S(2)}) collective-permute-start(bf16[256,768]{1,0:T(8,128)(2,1)} %get-tuple-element.112), channel_id=1, source_target_pairs={{16,0},{17,1},{18,2},{19,3},{20,4},{21,5},{22,6},{23,7},{24,8},{25... | collective-permute-start | bytes 1179656 | tf_op jit(solution)/shard_map/ppermute | solution.py:1405
  273.2 1.1 copy-start.5
  380.6 4.4 %copy-start.1 = (f32[1,10176]{1,0:T(1,128)S(1)}, f32[1,10176]{1,0:T(1,128)}, u32[]{:S(2)}) copy-start(f32[1,10176]{1,0:T(1,128)} %param.22) | copy-start | bytes 122116
  380.6 4.4 %copy-start.2 = (f32[1,10176]{1,0:T(1,128)S(1)}, f32[1,10176]{1,0:T(1,128)}, u32[]{:S(2)}) copy-start(f32[1,10176]{1,0:T(1,128)} %param.23) | copy-start | bytes 122116
  380.6 4.4 %copy-start.3 = (f32[1,10176]{1,0:T(1,128)S(1)}, f32[1,10176]{1,0:T(1,128)}, u32[]{:S(2)}) copy-start(f32[1,10176]{1,0:T(1,128)} %param.24) | copy-start | bytes 122116
  380.6 4.4 %copy-start.4 = (f32[80,128]{1,0:T(8,128)S(1)}, f32[80,128]{1,0:T(8,128)}, u32[]{:S(2)}) copy-start(f32[80,128]{1,0:T(8,128)} %get-tuple-element.131) | copy-start | bytes 122884
